TPU v7x, 512 devices: a whole 4x8x8 slice. The times are simulated.
512 devices in a mesh: brick: 128 (over z, y, core), region: 4 (over x).
Axes of the slice: x: 4, y: 8, z: 8, core: 2. Of those that a mesh axis runs over, the one named last changes fastest.
Arguments:
- micrograph: bfloat16 [4, 128, 512], P('region', 'brick'), may hold values from -6 to 6
- tissue: int32 [4, 128], P('region', 'brick'), may hold values from 0 to 1, as said below
- neighbours: int32 [4, 128, 26], P('region', 'brick'), may hold values from -1 to 127, as said below
- first_weight: bfloat16 [64, 27], replicated, may hold values from -1.25 to 1.25
- first_bias: float32 [64], replicated, may hold values from -3 to 3
- second_weight: bfloat16 [64, 1728], replicated, may hold values from -0.15625 to 0.15625
- second_bias: float32 [64], replicated, may hold values from -3 to 3
- head_weight: bfloat16 [4, 64], replicated, may hold values from -0.75 to 0.75
- head_bias: float32 [4], replicated, may hold values from -3 to 3
- cotangent: bfloat16 [4, 128, 4, 512], P('region', 'brick'), may hold values from -6 to 6
Outputs:
- prediction: bfloat16 [4, 128, 4, 512], P('region', 'brick')
- first_weight_grad: float32 [64, 27], replicated
- first_bias_grad: float32 [64], replicated
- second_weight_grad: float32 [64, 1728], replicated
- second_bias_grad: float32 [64], replicated
- head_weight_grad: float32 [4, 64], replicated
- head_bias_grad: float32 [4], replicated
Inputs may be any that keep to these rules, and one draw needn't show every extreme that they name: 1 marks a slot that holds a tissue brick, 0 an empty slot whose outputs are zero. `neighbours`: an entry is -1 or the index, in the same region, of a tissue brick that touches the brick in that direction; empty slots list -1 only; the lists are symmetric (if brick n lists m in direction (a, b, c), m lists n in direction (-a, -b, -c)); every entry in a direction with b ≠ 0 is -1 (a region is one brick thick along y); a brick m listed by n in direction (a, 0, c) has m = n + 2 a + c, so its device is at most 3 away, and in every draw some brick lists one whose device is exactly 3 away.
All inputs are finite; a program needn't handle non-finite values.
Results may differ from a plain program's by a relative error of at most 0.015.
Values may be sent and summed in bfloat16 or wider, within the bound.
No kernel may reach another device: no remote copies, remote signals or barrier semaphores. Data moves between devices by JAX's collectives and lax.ppermute only.
A program may use at most 64 MiB of HBM per device.

v0:
```python
from functools import partial

import jax
import jax.numpy as jnp
from jax import lax
from jax.sharding import PartitionSpec as P

EDGE = 8
TAPS = 27
REACH = 3


DIRECTIONS = [
    (shift_x, shift_y, shift_z)
    for shift_x in (-1, 0, 1)
    for shift_y in (-1, 0, 1)
    for shift_z in (-1, 0, 1)
    if (shift_x, shift_y, shift_z) != (0, 0, 0)
]
TAP_OFFSETS = [
    (shift_x, shift_y, shift_z)
    for shift_x in (-1, 0, 1)
    for shift_y in (-1, 0, 1)
    for shift_z in (-1, 0, 1)
]


def passed_along(block, axis, distance):
    devices = range(lax.axis_size(axis))
    route = [(i - distance, i) for i in devices if i - distance in devices]
    return lax.ppermute(block, axis, route)


def face_table(volume, margin):
    side_len = volume.shape[-1]
    sections = [
        volume[:, :, :margin],
        volume[:, :, side_len - margin :],
        volume[:, :, :, :margin],
        volume[:, :, :, side_len - margin :],
        volume[:, :, :, :, :margin],
        volume[:, :, :, :, side_len - margin :],
    ]
    return jnp.concatenate(
        [section.reshape(section.shape[0], section.shape[1], -1) for section in sections], axis=2
    )


def assemble(volume, table, row_index, present, margin):
    number, channels, side_len = (volume.shape[0], volume.shape[1], volume.shape[2])
    face_size = margin * side_len * side_len
    pieces = {(0, 0, 0): volume}
    for dir_index, direction in enumerate(DIRECTIONS):
        normal = [axis_id for axis_id in range(3) if direction[axis_id] != 0][0]
        face_index = 2 * normal + (0 if direction[normal] > 0 else 1)
        selected = jnp.take(
            table[:, :, face_index * face_size : (face_index + 1) * face_size],
            row_index[:, dir_index],
            axis=0,
        )
        extent = [side_len, side_len, side_len]
        extent[normal] = margin
        selected = selected.reshape((number, channels) + tuple(extent))
        sources = []
        for axis_id in range(3):
            if axis_id == normal or direction[axis_id] > 0:
                sources.append(slice(0, margin))
            elif direction[axis_id] < 0:
                sources.append(slice(side_len - margin, side_len))
            else:
                sources.append(slice(0, side_len))
        portion = selected[:, :, sources[0], sources[1], sources[2]]
        presence = present[:, dir_index].astype(portion.dtype).reshape(number, 1, 1, 1, 1)
        pieces[direction] = portion * presence
    planes = []
    for shift_x in (-1, 0, 1):
        lines = []
        for shift_y in (-1, 0, 1):
            lines.append(
                jnp.concatenate(
                    [pieces[shift_x, shift_y, shift_z] for shift_z in (-1, 0, 1)], axis=4
                )
            )
        planes.append(jnp.concatenate(lines, axis=3))
    return jnp.concatenate(planes, axis=2)


def window_group(padded, margin, out_len, sign, group_id):
    number, inputs = (padded.shape[0], padded.shape[1])
    views = []
    for offset in TAP_OFFSETS[9 * group_id : 9 * group_id + 9]:
        start_x, start_y, start_z = [margin + sign * value for value in offset]
        views.append(
            padded[
                :,
                :,
                start_x : start_x + out_len,
                start_y : start_y + out_len,
                start_z : start_z + out_len,
            ].reshape(number, inputs, -1)
        )
    return jnp.concatenate(views, axis=1)


def convolve(padded, blocks, margin, out_len, sign):
    inputs = padded.shape[1]
    outputs_ch = blocks.shape[1]
    running = None
    for group_id in range(3):
        stacked = window_group(padded, margin, out_len, sign, group_id)
        grouped = (
            blocks[9 * group_id : 9 * group_id + 9]
            .transpose(1, 0, 2)
            .reshape(outputs_ch, 9 * inputs)
        )
        contrib = jnp.einsum("oj,njp->nop", grouped, stacked, preferred_element_type=jnp.float32)
        running = contrib if running is None else running + contrib
    return running


def tap_grads(left, padded, margin, out_len, exact):
    columns = []
    for group_id in range(3):
        stacked = window_group(padded, margin, out_len, 1, group_id)
        if exact:
            columns.append(
                jnp.einsum(
                    "nop,njp->oj",
                    left,
                    stacked.astype(jnp.float32),
                    precision=lax.Precision.HIGHEST,
                )
            )
        else:
            columns.append(
                jnp.einsum("nop,njp->oj", left, stacked, preferred_element_type=jnp.float32)
            )
    return jnp.concatenate(columns, axis=1)


def gelu_slope(values):
    _, backward = jax.vjp(partial(jax.nn.gelu, approximate=True), values)
    return backward(jnp.ones_like(values))[0]


def em_window(faces):
    parts_list = []
    for offset in range(-REACH, REACH + 1):
        if offset == 0:
            parts_list.append(faces)
        else:
            parts_list.append(passed_along(faces, "brick", -offset))
    return jnp.concatenate(parts_list, axis=0)


def first_window(faces):
    parts_list = []
    for offset in range(-REACH, REACH + 1):
        if offset == 0:
            parts_list.append(faces)
        else:
            parts_list.append(passed_along(faces, "brick", -offset))
    return jnp.concatenate(parts_list, axis=0)


def grad_window(faces):
    parts_list = []
    for offset in range(-REACH, REACH + 1):
        if offset == 0:
            parts_list.append(faces)
        else:
            parts_list.append(passed_along(faces, "brick", -offset))
    return jnp.concatenate(parts_list, axis=0)


def shards(
    micrograph,
    tissue,
    neighbours,
    first_weight,
    first_bias,
    second_weight,
    second_bias,
    head_weight,
    head_bias,
    cotangent,
):
    number = micrograph.shape[1]
    channels = first_weight.shape[0]
    position = lax.axis_index("brick")
    neighbour_ids = neighbours[0]
    present = neighbour_ids >= 0
    holder = jnp.where(present, neighbour_ids // number, position)
    row_index = jnp.where(present, (holder - position + REACH) * number + neighbour_ids % number, 0)
    active = tissue[0].astype(jnp.float32).reshape(number, 1, 1)
    blocks_first = first_weight.T[:, :, None]
    blocks_second = second_weight.reshape(channels, TAPS, channels).transpose(1, 0, 2)
    blocks_back = blocks_second.transpose(0, 2, 1)
    volume = micrograph[0].reshape(number, 1, EDGE, EDGE, EDGE)
    em_pad = assemble(volume, em_window(face_table(volume, 1)), row_index, present, 1)
    z_first = convolve(em_pad, blocks_first, 1, EDGE, 1) + first_bias[None, :, None]
    h_first = (jax.nn.gelu(z_first, approximate=True) * active).astype(jnp.bfloat16)
    cube_first = h_first.reshape(number, channels, EDGE, EDGE, EDGE)
    first_table = first_window(face_table(cube_first, 1))
    first_pad = assemble(cube_first, first_table, row_index, present, 1)
    z_second = convolve(first_pad, blocks_second, 1, EDGE, 1) + second_bias[None, :, None]
    h_second = (jax.nn.gelu(z_second, approximate=True) * active).astype(jnp.bfloat16)
    linear = (
        jnp.einsum("kc,ncp->nkp", head_weight, h_second, preferred_element_type=jnp.float32)
        + head_bias[None, :, None]
    )
    prediction = (linear * active).astype(jnp.bfloat16)
    total_bricks = lax.axis_size("brick") * number * lax.axis_size("region")
    dpred = (cotangent[0].astype(jnp.float32) * active / total_bricks).astype(jnp.bfloat16)
    grad_wh = jnp.einsum("nkp,ncp->kc", dpred, h_second, preferred_element_type=jnp.float32)
    grad_bh = jnp.sum(dpred.astype(jnp.float32), axis=(0, 2))
    dh_second = jnp.einsum("kc,nkp->ncp", head_weight, dpred, preferred_element_type=jnp.float32)
    dz_second = (dh_second * gelu_slope(z_second) * active).astype(jnp.bfloat16)
    grad_w2 = tap_grads(dz_second, first_pad, 1, EDGE, False)
    grad_b2 = jnp.sum(dz_second.astype(jnp.float32), axis=(0, 2))
    cube_grad = dz_second.reshape(number, channels, EDGE, EDGE, EDGE)
    grad_table = grad_window(face_table(cube_grad, 1))
    grad_pad = assemble(cube_grad, grad_table, row_index, present, 1)
    dh_first = convolve(grad_pad, blocks_back, 1, EDGE, -1)
    dz_first = dh_first * gelu_slope(z_first) * active
    grad_w1 = tap_grads(dz_first, em_pad, 1, EDGE, True)
    grad_b1 = jnp.sum(dz_first, axis=(0, 2))
    grad_w1, grad_b1, grad_w2, grad_b2, grad_wh, grad_bh = lax.psum(
        (grad_w1, grad_b1, grad_w2, grad_b2, grad_wh, grad_bh), ("brick", "region")
    )
    return (prediction[None], grad_w1, grad_b1, grad_w2, grad_b2, grad_wh, grad_bh)


def solution(mesh):
    return jax.shard_map(
        shards,
        mesh=mesh,
        in_specs=(
            P("region", "brick", None),
            P("region", "brick"),
            P("region", "brick", None),
            P(),
            P(),
            P(),
            P(),
            P(),
            P(),
            P("region", "brick", None, None),
        ),
        out_specs=(P("region", "brick", None, None), P(), P(), P(), P(), P(), P()),
        check_vma=False,
    )
```

profile of v0, /device:TPU:1, one launch (start us, length us, event | category | flops | bytes accessed | tf_op | source)
XLA Modules:
  0.0 461.3 jit_solution(3678511156505006840)
XLA Ops:
  7.2 0.7 reduce.1
  8.9 1.3 collective-permute-start.5
  10.2 1.3 collective-permute-start.4
  11.5 8.8 %collective-permute-start.3 = (bf16[1,1,384]{2,1,0:T(2,128)(2,1)S(1)}, bf16[1,1,384]{2,1,0:T(2,128)(2,1)S(1)}, u32[]{:S(2)}, u32[]{:S(2)}) collective-permute-start(bf16[1,1,384]{2,1,0:T(2,128)(2,1)S(1)} %concatenate.282), channel_id=1, source_target_pairs={{4,0},{8,4},{12,8},{16,12},{20,16},{24,20},{28,24},{32,28},{36,32}... | collective-permute-start | bytes 2312 | tf_op jit(solution)/shard_map/ppermute | solution.py:31
  20.3 4.2 collective-permute-start.2
  24.4 3.8 collective-permute-start
  43.2 0.7 fusion.233
  80.5 0.7 fusion.234
  81.2 0.7 fusion.232
  100.2 3.3 collective-permute-start.1
  103.5 0.7 collective-permute-done.1
  104.5 0.7 slice.1088
  122.8 0.7 copy-done.31
  123.5 0.9 multiply_convert_fusion.1
  124.7 4.8 %collective-permute-start.6 = (bf16[1,64,384]{1,2,0:T(8,128)(2,1)S(1)}, bf16[1,64,384]{1,2,0:T(8,128)(2,1)S(1)}, u32[]{:S(2)}, u32[]{:S(2)}) collective-permute-start(bf16[1,64,384]{1,2,0:T(8,128)(2,1)S(1)} %constant_dynamic-update-slice_fusion.7), channel_id=1, source_target_pairs={{0,12},{4,16},{8,20},{12,24},{16,28},{20,32},{24,36},{28,40},{32,4... | collective-permute-start | bytes 147464 | tf_op jit(solution)/shard_map/ppermute | solution.py:31
  130.4 1.3 collective-permute-start.11
  131.7 1.3 collective-permute-start.10
  133.0 1.9 collective-permute-start.9
  135.0 3.6 collective-permute-start.8
  138.6 4.3 collective-permute-start.7
  143.0 1.6 collective-permute-done.7
  145.6 0.7 copy.57
  146.9 0.7 copy.60
  147.6 0.7 copy.59
  148.3 0.7 copy.58
  150.3 1.0 fusion.218
  151.3 0.8 copy-done.15
  152.2 0.8 copy-done.14
  153.0 0.8 copy-done.13
  154.7 0.9 convolution_add_fusion.3
  155.8 1.3 concatenate.327
  159.6 1.3 collective-permute-start.17
  160.9 1.3 collective-permute-start.16
  162.2 1.9 collective-permute-start.15
  164.1 4.4 collective-permute-start.14
  168.6 5.0 %collective-permute-start.12 = (bf16[1,64,384]{1,2,0:T(8,128)(2,1)S(1)}, bf16[1,64,384]{1,2,0:T(8,128)(2,1)S(1)}, u32[]{:S(2)}, u32[]{:S(2)}) collective-permute-start(bf16[1,64,384]{1,2,0:T(8,128)(2,1)S(1)} %constant_dynamic-update-slice_fusion.34), channel_id=1, source_target_pairs={{0,12},{4,16},{8,20},{12,24},{16,28},{20,32},{24,36},{28,40},{32,4... | collective-permute-start | bytes 147464 | tf_op jit(solution)/shard_map/ppermute | solution.py:31
  173.5 0.9 concatenate.352
  175.1 0.7 fusion.15
  175.8 4.6 collective-permute-start.13
  180.5 1.6 collective-permute-done.13
  183.9 0.7 copy.81
  184.6 0.7 copy.80
  186.5 0.9 fusion.216
  187.5 0.8 copy-done.17
  188.3 0.8 copy-done.16
  194.4 118.7 %all-reduce = (f32[64,27]{0,1:T(8,128)}, f32[64]{0:T(128)}, f32[64]{0:T(128)}, f32[4,64]{1,0:T(4,128)}, f32[4]{0:T(128)}) all-reduce(f32[64,27]{0,1:T(8,128)S(1)} %pad_maximum_fusion.7, f32[64]{0:T(128)S(1)} %get-tuple-element.276, f32[64]{0:T(128)S(1)} %get-tuple-element.278, ...), channel_id=1, replica_groups=mesh['brick'=128,'region'=4] {'brick','region'}, use_global_device_ids=true, to_apply=%region_0.3 | all-reduce | flops 2116 | bytes 16928 | tf_op jit(solution)/shard_map/psum | solution.py:228
  313.1 139.5 %all-reduce.3.cloned.1.call-done = f32[64,1728]{1,0:T(8,128)} async-done(((f32[64,1728]{1,0:T(8,128)}), f32[64,1728]{1,0:T(8,128)}) %all-reduce.3.cloned.1.call-update) | async-done | bytes 442384 | tf_op jit(solution)/shard_map/psum | solution.py:228
  452.6 1.8 copy.157
  (361 shorter events, 31.3 us)
Async XLA Ops:
  7.2 151.0 %copy-start = (bf16[4,64]{1,0:T(4,128)(2,1)S(1)}, bf16[4,64]{1,0:T(4,128)(2,1)}, u32[]{:S(2)}) copy-start(bf16[4,64]{1,0:T(4,128)(2,1)} %param.21) | copy-start | bytes 1540
  7.2 445.4 %all-reduce.3.cloned.1.call-start = ((), (), s32[]{:S(2)}) async-start(), calls=%async_computation | async-start | bytes 917504 | tf_op jit(solution)/shard_map/psum | solution.py:228
  8.9 95.4 %collective-permute-start.5 = (bf16[1,1,384]{2,1,0:T(2,128)(2,1)S(1)}, bf16[1,1,384]{2,1,0:T(2,128)(2,1)S(1)}, u32[]{:S(2)}, u32[]{:S(2)}) collective-permute-start(bf16[1,1,384]{2,1,0:T(2,128)(2,1)S(1)} %concatenate.282), channel_id=1, source_target_pairs={{12,0},{16,4},{20,8},{24,12},{28,16},{32,20},{36,24},{40,28},{44,3... | collective-permute-start | bytes 2312 | tf_op jit(solution)/shard_map/ppermute | solution.py:31
  10.2 94.1 %collective-permute-start.4 = (bf16[1,1,384]{2,1,0:T(2,128)(2,1)S(1)}, bf16[1,1,384]{2,1,0:T(2,128)(2,1)S(1)}, u32[]{:S(2)}, u32[]{:S(2)}) collective-permute-start(bf16[1,1,384]{2,1,0:T(2,128)(2,1)S(1)} %concatenate.282), channel_id=1, source_target_pairs={{8,0},{12,4},{16,8},{20,12},{24,16},{28,20},{32,24},{36,28},{40,32... | collective-permute-start | bytes 2312 | tf_op jit(solution)/shard_map/ppermute | solution.py:31
  11.5 92.8 %collective-permute-start.3 = (bf16[1,1,384]{2,1,0:T(2,128)(2,1)S(1)}, bf16[1,1,384]{2,1,0:T(2,128)(2,1)S(1)}, u32[]{:S(2)}, u32[]{:S(2)}) collective-permute-start(bf16[1,1,384]{2,1,0:T(2,128)(2,1)S(1)} %concatenate.282), channel_id=1, source_target_pairs={{4,0},{8,4},{12,8},{16,12},{20,16},{24,20},{28,24},{32,28},{36,32}... | collective-permute-start | bytes 2312 | tf_op jit(solution)/shard_map/ppermute | solution.py:31
  20.3 83.9 %collective-permute-start.2 = (bf16[1,1,384]{2,1,0:T(2,128)(2,1)S(1)}, bf16[1,1,384]{2,1,0:T(2,128)(2,1)S(1)}, u32[]{:S(2)}, u32[]{:S(2)}) collective-permute-start(bf16[1,1,384]{2,1,0:T(2,128)(2,1)S(1)} %concatenate.282), channel_id=1, source_target_pairs={{0,4},{4,8},{8,12},{12,16},{16,20},{20,24},{24,28},{28,32},{32,36}... | collective-permute-start | bytes 2312 | tf_op jit(solution)/shard_map/ppermute | solution.py:31
  24.4 75.8 %collective-permute-start = (bf16[1,1,384]{2,1,0:T(2,128)(2,1)S(1)}, bf16[1,1,384]{2,1,0:T(2,128)(2,1)S(1)}, u32[]{:S(2)}, u32[]{:S(2)}) collective-permute-start(bf16[1,1,384]{2,1,0:T(2,128)(2,1)S(1)} %concatenate.282), channel_id=1, source_target_pairs={{0,12},{4,16},{8,20},{12,24},{16,28},{20,32},{24,36},{28,40},{32,4... | collective-permute-start | bytes 2312 | tf_op jit(solution)/shard_map/ppermute | solution.py:31
  36.7 62.4 %copy-start.18 = (bf16[64,1728]{1,0:T(8,128)(2,1)S(1)}, bf16[64,1728]{1,0:T(8,128)(2,1)}, u32[]{:S(2)}) copy-start(bf16[64,1728]{1,0:T(8,128)(2,1)} %param.19) | copy-start | bytes 663556
  100.2 4.0 collective-permute-start.1
  120.7 0.7 copy-start.27
  120.8 0.8 copy-start.19
  121.4 0.7 copy-start.28
  122.8 1.6 copy-start.24
  122.8 0.7 copy-start.31
  124.6 4.8 %copy-start.26 = (bf16[1,1,4,512]{3,2,1,0:T(4,128)(2,1)S(1)}, bf16[1,1,4,512]{3,2,1,0:T(4,128)(2,1)}, u32[]{:S(2)}) copy-start(bf16[1,1,4,512]{3,2,1,0:T(4,128)(2,1)} %param.23) | copy-start | bytes 12292
  124.7 14.0 %collective-permute-start.6 = (bf16[1,64,384]{1,2,0:T(8,128)(2,1)S(1)}, bf16[1,64,384]{1,2,0:T(8,128)(2,1)S(1)}, u32[]{:S(2)}, u32[]{:S(2)}) collective-permute-start(bf16[1,64,384]{1,2,0:T(8,128)(2,1)S(1)} %constant_dynamic-update-slice_fusion.7), channel_id=1, source_target_pairs={{0,12},{4,16},{8,20},{12,24},{16,28},{20,32},{24,36},{28,40},{32,4... | collective-permute-start | bytes 147464 | tf_op jit(solution)/shard_map/ppermute | solution.py:31
  130.4 14.4 %collective-permute-start.11 = (bf16[1,64,384]{1,2,0:T(8,128)(2,1)S(1)}, bf16[1,64,384]{1,2,0:T(8,128)(2,1)S(1)}, u32[]{:S(2)}, u32[]{:S(2)}) collective-permute-start(bf16[1,64,384]{1,2,0:T(8,128)(2,1)S(1)} %constant_dynamic-update-slice_fusion.7), channel_id=1, source_target_pairs={{12,0},{16,4},{20,8},{24,12},{28,16},{32,20},{36,24},{40,28},{44,3... | collective-permute-start | bytes 147464 | tf_op jit(solution)/shard_map/ppermute | solution.py:31
  131.7 13.0 %collective-permute-start.10 = (bf16[1,64,384]{1,2,0:T(8,128)(2,1)S(1)}, bf16[1,64,384]{1,2,0:T(8,128)(2,1)S(1)}, u32[]{:S(2)}, u32[]{:S(2)}) collective-permute-start(bf16[1,64,384]{1,2,0:T(8,128)(2,1)S(1)} %constant_dynamic-update-slice_fusion.7), channel_id=1, source_target_pairs={{8,0},{12,4},{16,8},{20,12},{24,16},{28,20},{32,24},{36,28},{40,32... | collective-permute-start | bytes 147464 | tf_op jit(solution)/shard_map/ppermute | solution.py:31
  133.0 11.7 %collective-permute-start.9 = (bf16[1,64,384]{1,2,0:T(8,128)(2,1)S(1)}, bf16[1,64,384]{1,2,0:T(8,128)(2,1)S(1)}, u32[]{:S(2)}, u32[]{:S(2)}) collective-permute-start(bf16[1,64,384]{1,2,0:T(8,128)(2,1)S(1)} %constant_dynamic-update-slice_fusion.7), channel_id=1, source_target_pairs={{4,0},{8,4},{12,8},{16,12},{20,16},{24,20},{28,24},{32,28},{36,32}... | collective-permute-start | bytes 147464 | tf_op jit(solution)/shard_map/ppermute | solution.py:31
  135.0 9.7 %collective-permute-start.8 = (bf16[1,64,384]{1,2,0:T(8,128)(2,1)S(1)}, bf16[1,64,384]{1,2,0:T(8,128)(2,1)S(1)}, u32[]{:S(2)}, u32[]{:S(2)}) collective-permute-start(bf16[1,64,384]{1,2,0:T(8,128)(2,1)S(1)} %constant_dynamic-update-slice_fusion.7), channel_id=1, source_target_pairs={{0,4},{4,8},{8,12},{12,16},{16,20},{20,24},{24,28},{28,32},{32,36}... | collective-permute-start | bytes 147464 | tf_op jit(solution)/shard_map/ppermute | solution.py:31
  138.6 6.0 %collective-permute-start.7 = (bf16[1,64,384]{1,2,0:T(8,128)(2,1)S(1)}, bf16[1,64,384]{1,2,0:T(8,128)(2,1)S(1)}, u32[]{:S(2)}, u32[]{:S(2)}) collective-permute-start(bf16[1,64,384]{1,2,0:T(8,128)(2,1)S(1)} %constant_dynamic-update-slice_fusion.7), channel_id=1, source_target_pairs={{0,8},{4,12},{8,16},{12,20},{16,24},{20,28},{24,32},{28,36},{32,40... | collective-permute-start | bytes 147464 | tf_op jit(solution)/shard_map/ppermute | solution.py:31
  150.3 1.0 copy-start.12
  151.3 0.8 copy-start.15
  152.1 0.8 copy-start.14
  153.0 0.8 copy-start.13
  154.6 1.0 copy-start.6
  154.7 1.0 copy-start.7
  154.7 1.0 copy-start.8
  154.7 1.1 copy-start.9
  154.7 1.1 copy-start.10
  155.8 1.4 copy-start.11
  159.6 22.7 %collective-permute-start.17 = (bf16[1,64,384]{1,2,0:T(8,128)(2,1)S(1)}, bf16[1,64,384]{1,2,0:T(8,128)(2,1)S(1)}, u32[]{:S(2)}, u32[]{:S(2)}) collective-permute-start(bf16[1,64,384]{1,2,0:T(8,128)(2,1)S(1)} %constant_dynamic-update-slice_fusion.34), channel_id=1, source_target_pairs={{12,0},{16,4},{20,8},{24,12},{28,16},{32,20},{36,24},{40,28},{44,3... | collective-permute-start | bytes 147464 | tf_op jit(solution)/shard_map/ppermute | solution.py:31
  160.9 21.4 %collective-permute-start.16 = (bf16[1,64,384]{1,2,0:T(8,128)(2,1)S(1)}, bf16[1,64,384]{1,2,0:T(8,128)(2,1)S(1)}, u32[]{:S(2)}, u32[]{:S(2)}) collective-permute-start(bf16[1,64,384]{1,2,0:T(8,128)(2,1)S(1)} %constant_dynamic-update-slice_fusion.34), channel_id=1, source_target_pairs={{8,0},{12,4},{16,8},{20,12},{24,16},{28,20},{32,24},{36,28},{40,32... | collective-permute-start | bytes 147464 | tf_op jit(solution)/shard_map/ppermute | solution.py:31
  162.2 20.0 %collective-permute-start.15 = (bf16[1,64,384]{1,2,0:T(8,128)(2,1)S(1)}, bf16[1,64,384]{1,2,0:T(8,128)(2,1)S(1)}, u32[]{:S(2)}, u32[]{:S(2)}) collective-permute-start(bf16[1,64,384]{1,2,0:T(8,128)(2,1)S(1)} %constant_dynamic-update-slice_fusion.34), channel_id=1, source_target_pairs={{4,0},{8,4},{12,8},{16,12},{20,16},{24,20},{28,24},{32,28},{36,32}... | collective-permute-start | bytes 147464 | tf_op jit(solution)/shard_map/ppermute | solution.py:31
  164.1 18.0 %collective-permute-start.14 = (bf16[1,64,384]{1,2,0:T(8,128)(2,1)S(1)}, bf16[1,64,384]{1,2,0:T(8,128)(2,1)S(1)}, u32[]{:S(2)}, u32[]{:S(2)}) collective-permute-start(bf16[1,64,384]{1,2,0:T(8,128)(2,1)S(1)} %constant_dynamic-update-slice_fusion.34), channel_id=1, source_target_pairs={{0,4},{4,8},{8,12},{12,16},{16,20},{20,24},{24,28},{28,32},{32,36}... | collective-permute-start | bytes 147464 | tf_op jit(solution)/shard_map/ppermute | solution.py:31
  168.6 7.3 %collective-permute-start.12 = (bf16[1,64,384]{1,2,0:T(8,128)(2,1)S(1)}, bf16[1,64,384]{1,2,0:T(8,128)(2,1)S(1)}, u32[]{:S(2)}, u32[]{:S(2)}) collective-permute-start(bf16[1,64,384]{1,2,0:T(8,128)(2,1)S(1)} %constant_dynamic-update-slice_fusion.34), channel_id=1, source_target_pairs={{0,12},{4,16},{8,20},{12,24},{16,28},{20,32},{24,36},{28,40},{32,4... | collective-permute-start | bytes 147464 | tf_op jit(solution)/shard_map/ppermute | solution.py:31
  175.8 6.2 %collective-permute-start.13 = (bf16[1,64,384]{1,2,0:T(8,128)(2,1)S(1)}, bf16[1,64,384]{1,2,0:T(8,128)(2,1)S(1)}, u32[]{:S(2)}, u32[]{:S(2)}) collective-permute-start(bf16[1,64,384]{1,2,0:T(8,128)(2,1)S(1)} %constant_dynamic-update-slice_fusion.34), channel_id=1, source_target_pairs={{0,8},{4,12},{8,16},{12,20},{16,24},{20,28},{24,32},{28,36},{32,40... | collective-permute-start | bytes 147464 | tf_op jit(solution)/shard_map/ppermute | solution.py:31
  187.5 0.8 copy-start.17
  188.3 0.8 copy-start.16
  190.0 0.9 copy-start.1
  190.0 1.0 copy-start.2
  190.0 1.0 copy-start.3
  190.0 1.1 copy-start.4
  190.0 1.1 copy-start.5
  191.2 0.9 copy-start.23
  192.1 0.7 copy-start.25
  192.8 0.7 copy-start.22
  193.5 0.7 copy-start.20
  (4 other events, 2.6 us)
Sparse Core Ops, SparseCore 0:
  174.6 278.0 all-reduce.2
where the time goes:
time: 464 us; the launch traced here: 461 us
  waiting for transfers between devices  143 us (31%)
  blocking collectives  119 us (26%)
  between operations  88.5 us (19%)
  starting transfers between devices  58.4 us (13%)
  local copies, waits for them, and re-layouts  41.3 us (9%)
  matrix products  6.25 us (1%)
  other arithmetic  4.71 us (1%)
    psum x1, waiting for transfers between devices, shards(): lax.psum((grad_w1, grad_b1, grad_w2, grad_b2, grad_wh, grad_bh), ('brick'...  140 us
    psum x1, blocking collectives, shards(): lax.psum((grad_w1, grad_b1, grad_w2, grad_b2, grad_wh, grad_bh), ('brick'...  119 us
    ppermute x18, starting transfers between devices, passed_along(): return lax.ppermute(block, axis, route)  58.3 us
    unnamed x121, local copies, waits for them, and re-layouts  13.4 us
  transfers between devices with their start and end apart: 19, of which 4 were waited for; matrix products, arithmetic and copies ran while one was open for 3% of the time, Pallas kernels for 0%

commit v1 on v0

v1 whole, which is shorter than its diff:
```python
import jax
import jax.numpy as jnp
import numpy as np
from jax import lax
from jax.experimental import pallas as pl
from jax.experimental.pallas import tpu as pltpu
from jax.sharding import Mesh, PartitionSpec as P

EDGE = 8
C = 64
OUT_CH = 4
ROW = 12
GROUP = 576
ACROSS = 1728
BLOCKS = 16
ROOT = 0.7978845608028654
CUBIC = 0.044715


def region_of(place):
    return -1 if place < 2 else (1 if place > 9 else 0)


def tables():
    even = np.zeros((384, 128), np.float32)
    odd = np.zeros((384, 128), np.float32)
    for step in (-1, 0, 1):
        for y in range(EDGE):
            for z in range(EDGE):
                place = z + 2 + 8 * step
                if 0 <= place < ROW:
                    lane = y * ROW + place
                    even[(step + 1) * 128 + y * 8 + z, lane] = 1
                    odd[(step + 1) * 128 + 64 + y * 8 + z, lane] = 1
    spread = np.zeros((128, 512), np.float32)
    for y in range(EDGE):
        for place in range(1, ROW - 1):
            lane = y * ROW + place
            dc = region_of(place)
            for shift in (-1, 0, 1):
                ec = region_of(place + shift) - dc
                for ea in (-1, 0, 1):
                    spread[16 * (dc + 1) + 3 * (ea + 1) + ec + 1, (shift + 1) * 128 + lane] = 1
            for da in (-1, 0, 1):
                spread[3 * (da + 1) + dc + 1, 384 + lane] = 1
    keep = np.zeros((3, 48, 128), np.float32)
    for shift in (-1, 0, 1):
        for cell in range(10):
            da = region_of(cell + 1)
            ea = region_of(cell + 1 + shift) - da
            for dc in (-1, 0, 1):
                first = 16 * (dc + 1) + 3 * (ea + 1)
                keep[dc + 1, 10 * (shift + 1) + cell, first : first + 3] = 1
    for cell in range(10):
        da = region_of(cell + 1)
        keep[0, 30 + cell, 3 * (da + 1) : 3 * (da + 1) + 3] = 1
    return even, odd, spread, keep


def gelu_parts(v):
    square = v * v
    t = jnp.tanh(ROOT * v * (1.0 + CUBIC * square))
    half = 0.5 * (1.0 + t)
    value = v * half
    slope = half + 0.5 * v * (1.0 - t * t) * (ROOT * (1.0 + 3.0 * CUBIC * square))
    return value, slope


def turn(block, amount):
    amount = (-amount) % 128
    return block if amount == 0 else pltpu.roll(block, amount, 1)


def dot(a, b):
    return jnp.dot(a, b, preferred_element_type=jnp.float32)


def dot_t(a, b):
    return lax.dot_general(a, b, (((1,), (1,)), ((), ())), preferred_element_type=jnp.float32)


SHIFTS = [(b, c) for b in (-1, 0, 1) for c in (-1, 0, 1)]


def brick_kernel(
    place_ref,
    near_ref,
    cot_ref,
    w1_ref,
    b1_ref,
    w2_ref,
    b2_ref,
    hw_ref,
    hb_ref,
    even_ref,
    odd_ref,
    spread_ref,
    keep_ref,
    pred_ref,
    part_ref,
    rows_ref,
    flag_ref,
    s1_ref,
    h1_ref,
    slope_ref,
    v_ref,
    wb_ref,
    g_ref,
):
    position = place_ref[0]
    bf16 = jnp.bfloat16
    f32 = jnp.float32
    last = near_ref.shape[0] - 1
    tiles = {}
    for w in range(-3, 4):
        tiles[w] = near_ref[jnp.clip(position + w, 0, last)].astype(f32)
    rows_ref[...] = jnp.zeros_like(rows_ref)
    for rc in (-1, 0, 1):
        lanes = slice(128 * (rc + 1), 128 * (rc + 2))
        rows_ref[0:1, lanes] = tiles[-2 + rc][3:4]
        rows_ref[1:5, lanes] = tiles[rc][0:4]
        rows_ref[5:6, lanes] = tiles[2 + rc][0:1]
    lines = rows_ref[...].astype(bf16)
    cells_even = dot(lines, even_ref[...])
    cells_odd = dot(lines, odd_ref[...])
    flags = {w: tiles[w][4:5] for w in range(-3, 4)}
    for shift in (-1, 0, 1):
        for cell in range(10):
            da = region_of(cell + 1)
            row = 10 * (shift + 1) + cell
            flag_ref[row : row + 1] = sum(
                flags[2 * da + dc] * keep_ref[dc + 1, row : row + 1] for dc in (-1, 0, 1)
            )
    for cell in range(10):
        flag_ref[30 + cell : 31 + cell] = flags[0] * keep_ref[0, 30 + cell : 31 + cell]
    flag_ref[40:48] = jnp.zeros((8, 128), f32)
    masks = dot(flag_ref[...].astype(bf16), spread_ref[...])
    valid = masks[30:40, 384:512]
    s1_ref[...] = jnp.zeros_like(s1_ref)
    for b, c in SHIFTS:
        amount = 12 * b + c
        moved = [turn(cells_even, amount), turn(cells_odd, amount)]
        for a in (-1, 0, 1):
            tap = 9 * (a + 1) + 3 * (b + 1) + c + 1
            for cell in range(10):
                source = cell + 1 + a
                row = 10 * (a + 1) + cell
                s1_ref[cell, tap : tap + 1] = (
                    moved[source % 2][source // 2 : source // 2 + 1]
                    * masks[row : row + 1, 128 * (c + 1) : 128 * (c + 2)]
                )
    w1 = w1_ref[...]
    b1 = b1_ref[...]
    for cell in range(10):
        taps = s1_ref[cell].astype(bf16)
        value, slope = gelu_parts(dot(w1, taps) + b1)
        ok = valid[cell : cell + 1]
        slope_ref[cell] = slope * ok
        h1 = (value * ok).astype(bf16).astype(f32)
        for index, (b, c) in enumerate(SHIFTS):
            v_ref[cell, 64 * index : 64 * index + 64] = turn(h1, 12 * b + c).astype(bf16)
    active = valid[2:3, 2:3]
    w2 = w2_ref[...]
    b2 = b2_ref[...]
    hw = hw_ref[...]
    hb = hb_ref[...]
    own = even_ref[128:192]
    cot = (cot_ref[...].astype(f32) * (active / 512.0)).astype(bf16)
    d_pred, dz2, h2_all = [], [], []
    for x in range(8):
        stack = v_ref[x : x + 3].reshape(ACROSS, 128)
        value, slope = gelu_parts(dot(w2, stack) + b2)
        h2 = (value * active).astype(bf16)
        pred = ((dot(hw, h2) + hb) * active).astype(bf16)
        pred_ref[:, 64 * x : 64 * x + 64] = dot_t(pred, own).astype(bf16)
        dp = dot(cot[:, 64 * x : 64 * x + 64], own)
        d_pred.append(dp)
        dp = dp.astype(bf16)
        dh2 = lax.dot_general(hw, dp, (((0,), (0,)), ((), ())), preferred_element_type=f32)
        d2 = (dh2 * slope * active).astype(bf16)
        dz2.append(d2)
        h2_all.append(h2)
    grad_b2 = sum(d.astype(f32) for d in dz2)
    grad_b2 = jnp.sum(grad_b2, axis=1, keepdims=True)
    grad_w2 = None
    for x in range(0, 8, 2):
        left = jnp.concatenate(dz2[x : x + 2], axis=1)
        right = jnp.concatenate(
            [v_ref[x : x + 3].reshape(ACROSS, 128), v_ref[x + 1 : x + 4].reshape(ACROSS, 128)], axis=1
        )
        piece = dot_t(left, right)
        grad_w2 = piece if grad_w2 is None else grad_w2 + piece
    for block in range(13):
        part_ref[block] = grad_w2[:, 128 * block : 128 * block + 128].astype(bf16)
    d_flat = jnp.concatenate(d_pred, axis=1)
    h2_flat = jnp.concatenate(h2_all, axis=1)
    grad_wh = dot_t(h2_flat, d_flat.astype(bf16))
    grad_bh = jnp.sum(d_flat, axis=1, keepdims=True)
    w2f = w2.astype(f32)
    for pair in range(14):
        wide = w2f[:, 128 * pair : min(128 * pair + 128, ACROSS)].T
        for half in range(wide.shape[0] // 64):
            tap = 2 * pair + half
            at = 64 * ((2 - tap // 9) * 9 + tap % 9)
            wb_ref[:, at : at + 64] = wide[64 * half : 64 * half + 64].astype(bf16)
    for x in range(8):
        d2 = dz2[x].astype(f32)
        for index, (b, c) in enumerate(SHIFTS):
            g_ref[x, 64 * index : 64 * index + 64] = turn(d2, -(12 * b + c)).astype(bf16)
    grad_w1 = None
    for cell in range(10):
        low, high = max(cell - 2, 0), min(cell + 1, 8)
        skip = low - (cell - 2)
        stack = g_ref[low:high].reshape((high - low) * GROUP, 128)
        back = wb_ref[:, skip * GROUP : (skip + high - low) * GROUP]
        dz1 = dot(back, stack) * slope_ref[cell]
        head = dz1.astype(bf16)
        tail = (dz1 - head.astype(f32)).astype(bf16)
        taps = s1_ref[cell]
        ones = lax.broadcasted_iota(jnp.int32, (32, 128), 0) == 27
        taps = jnp.where(ones, 1.0, taps).astype(bf16)
        piece = dot_t(head, taps) + dot_t(tail, taps)
        grad_w1 = piece if grad_w1 is None else grad_w1 + piece
    column = jnp.concatenate([grad_bh, jnp.zeros((60, 1), f32)], axis=0)
    small = jnp.concatenate(
        [grad_w1[:, 0:28], grad_b2, grad_wh, column, jnp.zeros((64, 30), f32)], axis=1
    )
    part_ref[13] = jnp.concatenate([grad_w2[:, 1664:1728], small], axis=1).astype(bf16)
    part_ref[14] = jnp.concatenate([small.T, jnp.zeros((64, 64), f32)], axis=1).astype(bf16)
    part_ref[15] = jnp.zeros((64, 128), bf16)


def unpack_kernel(all_ref, w1_ref, b1_ref, w2_ref, b2_ref, hw_ref, hb_ref):
    f32 = jnp.float32
    for block in range(13):
        w2_ref[:, 128 * block : 128 * block + 128] = all_ref[block].astype(f32)
    mixed = all_ref[13].astype(f32)
    w2_ref[:, 1664:1728] = mixed[:, 0:64]
    w1_ref[...] = mixed[:, 64:91]
    rows = all_ref[14].astype(f32)
    b1_ref[...] = rows[27:28, 0:64]
    b2_ref[...] = rows[28:29, 0:64]
    hw_ref[...] = rows[29:33, 0:64]
    hb_ref[...] = rows[33:34, 0:4]


VMEM = pl.BlockSpec(memory_space=pltpu.VMEM)
SMEM = pl.BlockSpec(memory_space=pltpu.SMEM)
BIG = 48 * 1024 * 1024


def all_brick_work(near, position, cot, w1, b1, w2, b2, hw, hb):
    bf16, f32 = jnp.bfloat16, jnp.float32
    even, odd, spread, keep = tables()
    return pl.pallas_call(
        brick_kernel,
        out_shape=(
            jax.ShapeDtypeStruct((OUT_CH, 512), bf16),
            jax.ShapeDtypeStruct((BLOCKS, C, 128), bf16),
        ),
        in_specs=[SMEM] + [VMEM] * 12,
        out_specs=(VMEM, VMEM),
        scratch_shapes=[
            pltpu.VMEM((8, 384), f32),
            pltpu.VMEM((48, 128), f32),
            pltpu.VMEM((10, 32, 128), f32),
            pltpu.VMEM((8, 128), f32),
            pltpu.VMEM((10, C, 128), f32),
            pltpu.VMEM((10, GROUP, 128), bf16),
            pltpu.VMEM((C, ACROSS), bf16),
            pltpu.VMEM((8, GROUP, 128), bf16),
        ],
        compiler_params=pltpu.CompilerParams(vmem_limit_bytes=BIG),
        name="brick",
    )(
        position,
        near,
        cot,
        w1,
        b1,
        w2,
        b2,
        hw,
        hb,
        even.astype(bf16),
        odd.astype(bf16),
        spread.astype(bf16),
        keep,
    )


def unpack(gathered):
    f32 = jnp.float32
    return pl.pallas_call(
        unpack_kernel,
        out_shape=(
            jax.ShapeDtypeStruct((C, 27), f32),
            jax.ShapeDtypeStruct((1, C), f32),
            jax.ShapeDtypeStruct((C, ACROSS), f32),
            jax.ShapeDtypeStruct((1, C), f32),
            jax.ShapeDtypeStruct((OUT_CH, C), f32),
            jax.ShapeDtypeStruct((1, OUT_CH), f32),
        ),
        in_specs=[VMEM],
        out_specs=(VMEM,) * 6,
        name="unpack",
    )(gathered)


def spread_out(block, axes, number):
    copies = jnp.broadcast_to(block[None], (number,) + block.shape)
    return lax.all_to_all(copies, axes, 0, 0, tiled=True)


PLANE = [3 * (a + 1) + c + 1 for a in (-1, 0, 1) for c in (-1, 0, 1)]


def shards(micrograph, tissue, neighbours, w1, b1, w2, b2, hw, hb, cot):
    bf16, f32 = jnp.bfloat16, jnp.float32
    position = lax.axis_index(("z", "y", "core")).astype(jnp.int32).reshape(1)
    listed = neighbours[0, 0]
    flags = jnp.concatenate(
        [
            jnp.where(listed[3:6] >= 0, 1, 0),
            jnp.where(listed[12:13] >= 0, 1, 0),
            tissue[0],
            jnp.where(listed[13:14] >= 0, 1, 0),
            jnp.where(listed[20:23] >= 0, 1, 0),
            jnp.zeros((7,), jnp.int32),
        ]
    )
    flags = jnp.concatenate([flags, flags, flags, jnp.zeros((80,), jnp.int32)]).astype(bf16)
    mine = jnp.concatenate([micrograph[0, 0], flags]).reshape(5, 128)
    near = spread_out(mine, ("z", "y", "core"), 128)
    w1p = jnp.pad(w1, ((0, 0), (0, 5)))
    prediction, parts = all_brick_work(
        near, position, cot[0, 0], w1p, b1[:, None], w2, b2[:, None], hw, hb[:, None]
    )
    mixed = lax.all_to_all(parts.reshape(64, 16, 128), ("z", "y"), 0, 0, tiled=True)
    share = jnp.sum(mixed.astype(f32), axis=0)
    shares = spread_out(share, ("core", "x"), 8)
    share = jnp.sum(shares, axis=0).astype(bf16)
    gathered = spread_out(share, ("z", "y"), 64).reshape(BLOCKS, C, 128)
    g_w1, g_b1, g_w2, g_b2, g_hw, g_hb = unpack(gathered)
    return (
        prediction[None, None],
        g_w1,
        g_b1.reshape(C),
        g_w2,
        g_b2.reshape(C),
        g_hw,
        g_hb.reshape(OUT_CH),
    )


def solution(mesh):
    fine = Mesh(mesh.devices.reshape(8, 8, 2, 4), ("z", "y", "core", "x"))
    brick = ("z", "y", "core")
    return jax.shard_map(
        shards,
        mesh=fine,
        in_specs=(
            P("x", brick, None),
            P("x", brick),
            P("x", brick, None),
            P(),
            P(),
            P(),
            P(),
            P(),
            P(),
            P("x", brick, None, None),
        ),
        out_specs=(P("x", brick, None, None), P(), P(), P(), P(), P(), P()),
        check_vma=False,
    )
```

time: 464 us -> 97.4 us (0.21)
  waiting for transfers between devices: 143 us -> 14.8 us
  between operations: 88.5 us -> 2.78 us
  blocking collectives: 119 us -> 46.7 us
  starting transfers between devices: 58.4 us -> 18.6 us
  local copies, waits for them, and re-layouts: 41.3 us -> 4.69 us
  Pallas kernels: 0 us -> 8.12 us
  matrix products: 6.25 us -> 0 us
    psum x1 -> x0, waiting for transfers between devices: 140 us -> none  [shards(): lax.psum((grad_w1, grad_b1, grad_w2, grad_b2, grad_wh, grad_bh), ('brick'...]
    psum x1 -> x0, blocking collectives: 119 us -> none  [shards(): lax.psum((grad_w1, grad_b1, grad_w2, grad_b2, grad_wh, grad_bh), ('brick'...]
    ppermute x18 -> x0, starting transfers between devices: 58.3 us -> none  [passed_along(): return lax.ppermute(block, axis, route)]
    all_to_all x0 -> x3, blocking collectives: none -> 46.7 us  [the longest x2 30 us: spread_out(): return lax.all_to_all(copies, axes, 0, 0, tiled=True)]
    all_to_all x0 -> x1, starting transfers between devices: none -> 18.6 us  [spread_out(): return lax.all_to_all(copies, axes, 0, 0, tiled=True)]
    all_to_all x0 -> x1, waiting for transfers between devices: none -> 14.8 us  [spread_out(): return lax.all_to_all(copies, axes, 0, 0, tiled=True)]
    unnamed x121 -> x28, local copies, waits for them, and re-layouts: 13.4 us -> 2.91 us
    reshape x69 -> x0, local copies, waits for them, and re-layouts: 10.5 us -> none  [the longest x42 7.79 us: window_group(): views.append(padded[:, :, start_x:start_x + out_len, start_y:start_y + ou...]
  transfers between devices with their start and end apart: 19 -> 1, of which waited for: 4 -> 1; matrix products, arithmetic and copies ran while one was open for 3% -> 0% of each run, Pallas kernels for 0% -> 0%
where the time goes in v1:
time: 97.4 us; the launch traced here: 96.6 us
  blocking collectives  46.7 us (48%)
  starting transfers between devices  18.6 us (19%)
  waiting for transfers between devices  14.8 us (15%)
  Pallas kernels  8.12 us (8%)
  local copies, waits for them, and re-layouts  4.69 us (5%)
  between operations  2.78 us (3%)
    all_to_all x2, blocking collectives, spread_out(): return lax.all_to_all(copies, axes, 0, 0, tiled=True)  30 us
    all_to_all x1, starting transfers between devices, spread_out(): return lax.all_to_all(copies, axes, 0, 0, tiled=True)  18.6 us
    all_to_all x1, blocking collectives, shards(): lax.all_to_all(parts.reshape(64, 16, 128), ('z', 'y'), 0, 0, tiled=True)  16.7 us
    all_to_all x1, waiting for transfers between devices, spread_out(): return lax.all_to_all(copies, axes, 0, 0, tiled=True)  14.8 us
    pallas_call x1, Pallas kernels, all_brick_work(): pl.pallas_call(brick_kernel, out_shape=(jax.ShapeDtypeStruct((OUT_CH, 512...  6.36 us
    unnamed x28, local copies, waits for them, and re-layouts  2.91 us
  transfers between devices with their start and end apart: 1, of which 1 were waited for; matrix products, arithmetic and copies ran while one was open for 0% of the time, Pallas kernels for 0%

profile of v1, /device:TPU:1, one launch (start us, length us, event | category | flops | bytes accessed | tf_op | source)
XLA Modules:
  0.0 96.6 jit_solution(8940841151293901148)
XLA Ops:
  0.6 0.0 copy-start.8
  0.6 0.8 fusion.3
  1.5 0.0 copy-done.8
  1.5 0.6 fusion.4
  4.0 0.0 copy-start.9
  4.0 0.7 copy-done.9
  4.7 0.1 concatenate.8
  4.9 0.7 broadcast_in_dim.51
  5.6 0.0 copy-start.12
  5.6 0.0 copy-start.7
  5.6 0.0 copy-start.10
  5.6 0.0 copy-start.11
  5.6 0.0 copy-start
  5.6 0.0 copy-start.2
  5.6 0.0 copy-start.3
  5.6 0.0 copy-start.4
  5.7 18.6 %all-to-all-start = ((bf16[128,5,128]{2,1,0:T(8,128)(2,1)}), bf16[128,5,128]{2,1,0:T(8,128)(2,1)S(1)}, u32[]{:S(2)}, u32[]{:S(2)}) async-start(bf16[128,5,128]{2,1,0:T(8,128)(2,1)} %broadcast_in_dim.51), calls=%async_computation | async-start | bytes 524288 | tf_op jit(solution)/shard_map/all_to_all | solution.py:312
  24.2 0.0 copy-start.1
  24.3 0.0 copy-done.12
  24.3 0.1 copy.29.hb_ref
  24.4 0.0 copy-done.7
  24.4 0.1 copy.26
  24.5 0.0 copy-done.10
  24.5 0.1 copy.27.b1_ref
  24.6 0.0 copy-done.11
  24.6 0.1 copy.28.b2_ref
  24.7 0.0 copy-start.5
  24.7 14.8 %all-to-all-done.near_ref = bf16[128,5,128]{2,1,0:T(8,128)(2,1)S(1)} async-done(((bf16[128,5,128]{2,1,0:T(8,128)(2,1)}), bf16[128,5,128]{2,1,0:T(8,128)(2,1)S(1)}, u32[]{:S(2)}, u32[]{:S(2)}) %all-to-all-start) | async-done | bytes 163872 | tf_op jit(solution)/shard_map/all_to_all | solution.py:312
  39.5 0.0 copy-start.6
  39.5 0.0 copy-done
  39.5 0.0 copy-done.2
  39.5 0.0 copy-done.3
  39.5 0.0 copy-done.4
  39.5 0.0 copy-done.1
  39.5 0.0 copy-done.5
  39.5 0.6 copy-done.6
  40.2 6.4 %brick.1 = (bf16[4,512]{1,0:T(4,128)(2,1)}, bf16[16,64,128]{2,1,0:T(8,128)(2,1)S(1)}) custom-call(s32[1]{0:T(128)} %bitcast.place_ref, bf16[128,5,128]{2,1,0:T(8,128)(2,1)S(1)} %all-to-all-done.near_ref, bf16[4,512]{1,0:T(4,128)(2,1)S(1)} %bitcast.20, bf16[64,32]{1,0:T(8,128)(2,1)S(1)} %pad.4.w1_ref, f32[64,1]{1,0:T(8,128)S(1)} %copy.27.b1_ref, ...), custom_call_target="tpu_custom_call" | custom-call | tf_op jit(solution)/shard_map/brick/pallas_call | solution.py:255
  46.5 16.7 %all_to_all.20 = bf16[64,16,128]{2,1,0:T(8,128)(2,1)S(1)} all-to-all(bf16[64,16,128]{2,1,0:T(8,128)(2,1)S(1)} %bitcast.19), channel_id=1, replica_groups=mesh['z'=8,'y'=8,'core'=2,'x'=4] {'z','y'}, dimensions={0} | all-to-all | bytes 524288 | tf_op jit(solution)/shard_map/all_to_all | solution.py:339
  63.3 0.1 convert_reduce_fusion
  63.4 12.1 %all_to_all.21 = f32[8,16,128]{2,1,0:T(8,128)S(1)} all-to-all(f32[8,16,128]{2,1,0:T(8,128)S(1)} %broadcast_in_dim.56), channel_id=1, replica_groups=mesh['z'=8,'y'=8,'core'=2,'x'=4] {'core','x'}, dimensions={0} | all-to-all | bytes 131072 | tf_op jit(solution)/shard_map/all_to_all | solution.py:312
  75.5 17.9 %all_to_all.22 = bf16[64,16,128]{2,1,0:T(8,128)(2,1)} all-to-all(bf16[64,16,128]{2,1,0:T(8,128)(2,1)S(1)} %broadcast_in_dim.57), channel_id=1, replica_groups=mesh['z'=8,'y'=8,'core'=2,'x'=4] {'z','y'}, dimensions={0} | all-to-all | bytes 524288 | tf_op jit(solution)/shard_map/all_to_all | solution.py:312
  93.4 1.8 %unpack.1 = (f32[64,27]{1,0:T(8,128)}, f32[1,64]{1,0:T(1,128)}, f32[64,1728]{1,0:T(8,128)}, f32[1,64]{1,0:T(1,128)}, f32[4,64]{1,0:T(4,128)}, /*index=5*/f32[1,4]{1,0:T(1,128)}) custom-call(bf16[16,64,128]{2,1,0:T(8,128)(2,1)} %bitcast.21), custom_call_target="tpu_custom_call" | custom-call | tf_op jit(solution)/shard_map/unpack/pallas_call | solution.py:294
  95.2 1.4 %copy.30 = f32[64,27]{0,1:T(8,128)} copy(f32[64,27]{1,0:T(8,128)} %get-tuple-element.31) | data formatting | bytes 13824
  (7 shorter events, 0.1 us)
Async XLA Ops:
  0.6 0.8 copy-start.8
  4.0 0.7 copy-start.9
  5.6 18.7 %copy-start.12 = (f32[4]{0:T(128)S(1)}, f32[4]{0:T(128)}, u32[]{:S(2)}) copy-start(f32[4]{0:T(128)} %param.22) | copy-start | bytes 52
  5.6 18.8 %copy-start.7 = (bf16[64,27]{0,1:T(8,128)(2,1)S(1)}, bf16[64,27]{0,1:T(8,128)(2,1)}, u32[]{:S(2)}) copy-start(bf16[64,27]{0,1:T(8,128)(2,1)} %param.17) | copy-start | bytes 10372
  5.6 18.9 %copy-start.10 = (f32[64]{0:T(128)S(1)}, f32[64]{0:T(128)}, u32[]{:S(2)}) copy-start(f32[64]{0:T(128)} %param.18) | copy-start | bytes 772
  5.6 19.0 %copy-start.11 = (f32[64]{0:T(128)S(1)}, f32[64]{0:T(128)}, u32[]{:S(2)}) copy-start(f32[64]{0:T(128)} %param.20) | copy-start | bytes 772
  5.6 33.9 %copy-start = (bf16[64,1728]{1,0:T(8,128)(2,1)S(1)}, bf16[64,1728]{1,0:T(8,128)(2,1)}, u32[]{:S(2)}) copy-start(bf16[64,1728]{1,0:T(8,128)(2,1)} %w2_ref.1) | copy-start | bytes 663556
  5.6 33.9 %copy-start.2 = (bf16[384,128]{1,0:T(8,128)(2,1)S(1)}, bf16[384,128]{1,0:T(8,128)(2,1)}, u32[]{:S(2)}) copy-start(bf16[384,128]{1,0:T(8,128)(2,1)} %constant.51.clone.odd_ref) | copy-start | bytes 294916
  5.6 33.9 %copy-start.3 = (bf16[384,128]{1,0:T(8,128)(2,1)S(1)}, bf16[384,128]{1,0:T(8,128)(2,1)}, u32[]{:S(2)}) copy-start(bf16[384,128]{1,0:T(8,128)(2,1)} %constant.50.clone.even_ref) | copy-start | bytes 294916
  5.6 33.9 %copy-start.4 = (f32[3,48,128]{2,1,0:T(8,128)S(1)}, f32[3,48,128]{2,1,0:T(8,128)}, u32[]{:S(2)}) copy-start(f32[3,48,128]{2,1,0:T(8,128)} %constant.53.clone.keep_ref) | copy-start | bytes 221188
  5.7 33.8 %all-to-all-start = ((bf16[128,5,128]{2,1,0:T(8,128)(2,1)}), bf16[128,5,128]{2,1,0:T(8,128)(2,1)S(1)}, u32[]{:S(2)}, u32[]{:S(2)}) async-start(bf16[128,5,128]{2,1,0:T(8,128)(2,1)} %broadcast_in_dim.51), calls=%async_computation | async-start | bytes 524288 | tf_op jit(solution)/shard_map/all_to_all | solution.py:312
  24.2 15.3 %copy-start.1 = (bf16[128,512]{1,0:T(8,128)(2,1)S(1)}, bf16[128,512]{1,0:T(8,128)(2,1)}, u32[]{:S(2)}) copy-start(bf16[128,512]{1,0:T(8,128)(2,1)} %constant.52.clone.spread_ref) | copy-start | bytes 393220
  24.7 14.8 %copy-start.5 = (bf16[1,1,4,512]{3,2,1,0:T(4,128)(2,1)S(1)}, bf16[1,1,4,512]{3,2,1,0:T(4,128)(2,1)}, u32[]{:S(2)}) copy-start(bf16[1,1,4,512]{3,2,1,0:T(4,128)(2,1)} %param.23) | copy-start | bytes 12292
  39.5 0.7 copy-start.6

commit v2 on v1

--- a/solution.py
+++ b/solution.py
@@ -13,6 +13,7 @@
 GROUP = 576
 ACROSS = 1728
 BLOCKS = 16
+GROUP_SIZE = 8
 ROOT = 0.7978845608028654
 CUBIC = 0.044715
 
@@ -85,6 +86,7 @@
 def brick_kernel(
     place_ref,
     near_ref,
+    far_ref,
     cot_ref,
     w1_ref,
     b1_ref,
@@ -110,10 +112,11 @@
     position = place_ref[0]
     bf16 = jnp.bfloat16
     f32 = jnp.float32
-    last = near_ref.shape[0] - 1
     tiles = {}
     for w in range(-3, 4):
-        tiles[w] = near_ref[jnp.clip(position + w, 0, last)].astype(f32)
+        at = lax.rem(position + w + GROUP_SIZE, GROUP_SIZE)
+        inside = at == position + w
+        tiles[w] = jnp.where(inside, near_ref[at].astype(f32), far_ref[at].astype(f32))
     rows_ref[...] = jnp.zeros_like(rows_ref)
     for rc in (-1, 0, 1):
         lanes = slice(128 * (rc + 1), 128 * (rc + 2))
@@ -230,14 +233,35 @@
     part_ref[15] = jnp.zeros((64, 128), bf16)
 
 
+LISTED = (3, 4, 5, 12, None, 13, 20, 21, 22)
+
+
+def pack_kernel(list_ref, tissue_ref, cells_ref, out_ref):
+    f32 = jnp.float32
+    lane = lax.broadcasted_iota(jnp.int32, (1, 128), 1)
+    slot = jnp.where(lane < 48, lane % 16, 16)
+    flags = jnp.zeros((1, 128), f32)
+    for index, entry in enumerate(LISTED):
+        if entry is None:
+            present = tissue_ref[0, 0] > 0
+        else:
+            present = list_ref[0, entry] >= 0
+        flags = jnp.where(slot == index, jnp.where(present, 1.0, 0.0), flags)
+    cells = cells_ref[...].astype(f32)
+    rows = [cells[:, 128 * row : 128 * row + 128] for row in range(4)]
+    tile = jnp.concatenate(rows + [flags], axis=0).astype(jnp.bfloat16)
+    for copy in range(GROUP_SIZE):
+        out_ref[copy] = tile
+
+
 def unpack_kernel(all_ref, w1_ref, b1_ref, w2_ref, b2_ref, hw_ref, hb_ref):
     f32 = jnp.float32
     for block in range(13):
         w2_ref[:, 128 * block : 128 * block + 128] = all_ref[block].astype(f32)
     mixed = all_ref[13].astype(f32)
     w2_ref[:, 1664:1728] = mixed[:, 0:64]
-    w1_ref[...] = mixed[:, 64:91]
     rows = all_ref[14].astype(f32)
+    w1_ref[...] = rows[0:27, 0:64]
     b1_ref[...] = rows[27:28, 0:64]
     b2_ref[...] = rows[28:29, 0:64]
     hw_ref[...] = rows[29:33, 0:64]
@@ -249,7 +273,7 @@
 BIG = 48 * 1024 * 1024
 
 
-def all_brick_work(near, position, cot, w1, b1, w2, b2, hw, hb):
+def all_brick_work(near, far, position, cot, w1, b1, w2, b2, hw, hb):
     bf16, f32 = jnp.bfloat16, jnp.float32
     even, odd, spread, keep = tables()
     return pl.pallas_call(
@@ -258,7 +282,7 @@
             jax.ShapeDtypeStruct((OUT_CH, 512), bf16),
             jax.ShapeDtypeStruct((BLOCKS, C, 128), bf16),
         ),
-        in_specs=[SMEM] + [VMEM] * 12,
+        in_specs=[SMEM] + [VMEM] * 13,
         out_specs=(VMEM, VMEM),
         scratch_shapes=[
             pltpu.VMEM((8, 384), f32),
@@ -275,6 +299,7 @@
     )(
         position,
         near,
+        far,
         cot,
         w1,
         b1,
@@ -294,7 +319,7 @@
     return pl.pallas_call(
         unpack_kernel,
         out_shape=(
-            jax.ShapeDtypeStruct((C, 27), f32),
+            jax.ShapeDtypeStruct((27, C), f32),
             jax.ShapeDtypeStruct((1, C), f32),
             jax.ShapeDtypeStruct((C, ACROSS), f32),
             jax.ShapeDtypeStruct((1, C), f32),
@@ -307,44 +332,52 @@
     )(gathered)
 
 
+def pack(neighbours, tissue, micrograph):
+    return pl.pallas_call(
+        pack_kernel,
+        out_shape=jax.ShapeDtypeStruct((GROUP_SIZE, 5, 128), jnp.bfloat16),
+        in_specs=[SMEM, SMEM, VMEM],
+        out_specs=VMEM,
+        name="pack",
+    )(neighbours, tissue, micrograph)
+
+
 def spread_out(block, axes, number):
     copies = jnp.broadcast_to(block[None], (number,) + block.shape)
     return lax.all_to_all(copies, axes, 0, 0, tiled=True)
 
 
-PLANE = [3 * (a + 1) + c + 1 for a in (-1, 0, 1) for c in (-1, 0, 1)]
+BRICK = ("z", "yhi", "ylo", "core")
+FIRST = ("yhi", "ylo", "x")
+SECOND = ("z", "core")
+HALF = GROUP_SIZE // 2
+PAIRS = [
+    pair
+    for lower in range(HALF, 128 - HALF)
+    if lower % GROUP_SIZE >= HALF
+    for pair in ((lower, lower + HALF), (lower + HALF, lower))
+]
 
 
 def shards(micrograph, tissue, neighbours, w1, b1, w2, b2, hw, hb, cot):
     bf16, f32 = jnp.bfloat16, jnp.float32
-    position = lax.axis_index(("z", "y", "core")).astype(jnp.int32).reshape(1)
-    listed = neighbours[0, 0]
-    flags = jnp.concatenate(
-        [
-            jnp.where(listed[3:6] >= 0, 1, 0),
-            jnp.where(listed[12:13] >= 0, 1, 0),
-            tissue[0],
-            jnp.where(listed[13:14] >= 0, 1, 0),
-            jnp.where(listed[20:23] >= 0, 1, 0),
-            jnp.zeros((7,), jnp.int32),
-        ]
-    )
-    flags = jnp.concatenate([flags, flags, flags, jnp.zeros((80,), jnp.int32)]).astype(bf16)
-    mine = jnp.concatenate([micrograph[0, 0], flags]).reshape(5, 128)
-    near = spread_out(mine, ("z", "y", "core"), 128)
+    position = lax.axis_index(("ylo", "core")).astype(jnp.int32).reshape(1)
+    mine = pack(neighbours[0], tissue, micrograph[0])
+    near = lax.all_to_all(mine, ("ylo", "core"), 0, 0, tiled=True)
+    far = lax.ppermute(near, BRICK, PAIRS)
     w1p = jnp.pad(w1, ((0, 0), (0, 5)))
     prediction, parts = all_brick_work(
-        near, position, cot[0, 0], w1p, b1[:, None], w2, b2[:, None], hw, hb[:, None]
+        near, far, position, cot[0, 0], w1p, b1[:, None], w2, b2[:, None], hw, hb[:, None]
     )
-    mixed = lax.all_to_all(parts.reshape(64, 16, 128), ("z", "y"), 0, 0, tiled=True)
-    share = jnp.sum(mixed.astype(f32), axis=0)
-    shares = spread_out(share, ("core", "x"), 8)
-    share = jnp.sum(shares, axis=0).astype(bf16)
-    gathered = spread_out(share, ("z", "y"), 64).reshape(BLOCKS, C, 128)
+    mixed = lax.all_to_all(parts.reshape(32, 32, 128), FIRST, 0, 0, tiled=True)
+    share = jnp.sum(mixed.astype(f32), axis=0).astype(bf16)
+    shares = spread_out(share, SECOND, 16)
+    share = jnp.sum(shares.astype(f32), axis=0).astype(bf16)
+    gathered = spread_out(share, FIRST, 32).reshape(BLOCKS, C, 128)
     g_w1, g_b1, g_w2, g_b2, g_hw, g_hb = unpack(gathered)
     return (
         prediction[None, None],
-        g_w1,
+        g_w1.T,
         g_b1.reshape(C),
         g_w2,
         g_b2.reshape(C),
@@ -354,23 +387,22 @@
 
 
 def solution(mesh):
-    fine = Mesh(mesh.devices.reshape(8, 8, 2, 4), ("z", "y", "core", "x"))
-    brick = ("z", "y", "core")
+    fine = Mesh(mesh.devices.reshape(8, 2, 4, 2, 4), ("z", "yhi", "ylo", "core", "x"))
     return jax.shard_map(
         shards,
         mesh=fine,
         in_specs=(
-            P("x", brick, None),
-            P("x", brick),
-            P("x", brick, None),
-            P(),
-            P(),
-            P(),
-            P(),
-            P(),
-            P(),
-            P("x", brick, None, None),
+            P("x", BRICK, None),
+            P("x", BRICK),
+            P("x", BRICK, None),
+            P(),
+            P(),
+            P(),
+            P(),
+            P(),
+            P(),
+            P("x", BRICK, None, None),
         ),
-        out_specs=(P("x", brick, None, None), P(), P(), P(), P(), P(), P()),
+        out_specs=(P("x", BRICK, None, None), P(), P(), P(), P(), P(), P()),
         check_vma=False,
     )

time: 97.4 us -> 90.6 us (0.930)
  blocking collectives: 46.7 us -> 72.5 us
  starting transfers between devices: 18.6 us -> 0.65 us
  waiting for transfers between devices: 14.8 us -> 0.01 us
  between operations: 2.78 us -> 1.42 us
  Pallas kernels: 8.12 us -> 9.44 us
  local copies, waits for them, and re-layouts: 4.69 us -> 5.87 us
    all_to_all x1 -> x0, starting transfers between devices: 18.6 us -> none  [spread_out(): return lax.all_to_all(copies, axes, 0, 0, tiled=True)]
    all_to_all x1 -> x2, blocking collectives: 16.7 us -> 33 us  [the longest x1 17.9 us: shards(): mixed = lax.all_to_all(parts.reshape(32, 32, 128), FIRST, 0, 0, tiled=True)]
    all_to_all x1 -> x0, waiting for transfers between devices: 14.8 us -> none  [spread_out(): return lax.all_to_all(copies, axes, 0, 0, tiled=True)]
    all_to_all x2, blocking collectives: 30 us -> 39.6 us  [spread_out(): return lax.all_to_all(copies, axes, 0, 0, tiled=True)]
    pallas_call x1 -> x2, Pallas kernels: 1.76 us -> 3.07 us  [the longest x1 1.75 us: unpack(): pl.pallas_call(unpack_kernel, out_shape=(jax.ShapeDtypeStruct((27, C), f3...]
    unnamed x28 -> x17, local copies, waits for them, and re-layouts: 2.91 us -> 4.19 us
  transfers between devices with their start and end apart: 1 -> 1, of which waited for: 1 -> 0; matrix products, arithmetic and copies ran while one was open for 0% -> 3% of each run, Pallas kernels for 0% -> 0%
where the time goes in v2:
time: 90.6 us; the launch traced here: 90 us
  blocking collectives  72.5 us (80%)
  Pallas kernels  9.44 us (10%)
  local copies, waits for them, and re-layouts  5.87 us (6%)
  between operations  1.42 us (2%)
    all_to_all x2, blocking collectives, spread_out(): return lax.all_to_all(copies, axes, 0, 0, tiled=True)  39.6 us
    all_to_all x1, blocking collectives, shards(): mixed = lax.all_to_all(parts.reshape(32, 32, 128), FIRST, 0, 0, tiled=True)  17.9 us
    all_to_all x1, blocking collectives, shards(): near = lax.all_to_all(mine, ('ylo', 'core'), 0, 0, tiled=True)  15 us
    pallas_call x1, Pallas kernels, all_brick_work(): pl.pallas_call(brick_kernel, out_shape=(jax.ShapeDtypeStruct((OUT_CH, 512...  6.38 us
    unnamed x17, local copies, waits for them, and re-layouts  4.19 us
  transfers between devices with their start and end apart: 1, of which 0 were waited for; matrix products, arithmetic and copies ran while one was open for 3% of the time, Pallas kernels for 0%

profile of v2, /device:TPU:1, one launch (start us, length us, event | category | flops | bytes accessed | tf_op | source)
XLA Modules:
  0.0 90.0 jit_solution(11304270469379170346)
XLA Ops:
  0.6 0.0 copy-start.1
  1.3 1.3 %pack.1 = bf16[8,5,128]{2,1,0:T(8,128)(2,1)} custom-call(s32[1,26]{1,0:T(1,128)} %bitcast.20, s32[1,1]{1,0:T(1,128)S(6)} %copy.29.tissue_ref, bf16[1,512]{1,0:T(2,128)(2,1)} %bitcast.17), custom_call_target="tpu_custom_call" | custom-call | tf_op jit(solution)/shard_map/pack/pallas_call | solution.py:336
  2.6 15.0 %all_to_all.20.near_ref = bf16[8,5,128]{2,1,0:T(8,128)(2,1)S(1)} all-to-all(bf16[8,5,128]{2,1,0:T(8,128)(2,1)} %pack.1), channel_id=1, replica_groups=mesh['z'=8,'yhi'=2,'ylo'=4,'core'=2,'x'=4] {'ylo','core'}, dimensions={0} | all-to-all | bytes 20480 | tf_op jit(solution)/shard_map/all_to_all | solution.py:366
  17.7 0.7 collective-permute-start
  18.3 0.0 copy-start.7
  18.4 0.0 copy-start.4
  18.4 0.8 copy.28.hb_ref
  19.1 0.8 copy.25
  19.9 0.7 copy.26.b1_ref
  20.7 0.0 copy-done.7
  20.7 0.1 copy.27.b2_ref
  20.8 0.0 copy-start.5
  20.8 0.0 collective-permute-done.far_ref
  20.8 0.0 copy-start.6
  20.8 0.0 copy-done.1
  20.8 0.0 copy-done.4
  20.8 0.6 copy-done.5
  21.5 0.0 copy-done.6
  21.5 0.0 copy-start
  21.5 0.9 %copy-done = bf16[64,1728]{1,0:T(8,128)(2,1)S(1)} copy-done((bf16[64,1728]{1,0:T(8,128)(2,1)S(1)}, bf16[64,1728]{1,0:T(8,128)(2,1)}, u32[]{:S(2)}) %copy-start) | copy-done | bytes 221208
  22.4 0.0 copy-start.2
  22.4 0.9 copy-done.2
  23.3 0.0 copy-start.3
  23.3 0.9 copy-done.3
  24.2 6.4 %brick.1 = (bf16[4,512]{1,0:T(4,128)(2,1)}, bf16[16,64,128]{2,1,0:T(8,128)(2,1)S(1)}) custom-call(s32[1]{0:T(128)} %bitcast.place_ref, bf16[8,5,128]{2,1,0:T(8,128)(2,1)S(1)} %all_to_all.20.near_ref, bf16[8,5,128]{2,1,0:T(8,128)(2,1)S(1)} %collective-permute-done.far_ref, bf16[4,512]{1,0:T(4,128)(2,1)S(1)} %bitcast.15, bf16[64,32]{1,0:T(8,128)(2,1)S(1)} %pad.4.w1_ref, ...), custom_call_target="tpu_custom_call" | custom-call | tf_op jit(solution)/shard_map/brick/pallas_call | solution.py:279
  30.6 17.9 %all_to_all.21 = bf16[32,32,128]{2,1,0:T(8,128)(2,1)S(1)} all-to-all(bf16[32,32,128]{2,1,0:T(8,128)(2,1)S(1)} %bitcast.14), channel_id=1, replica_groups=mesh['z'=8,'yhi'=2,'ylo'=4,'core'=2,'x'=4] {'yhi','ylo','x'}, dimensions={0} | all-to-all | bytes 524288 | tf_op jit(solution)/shard_map/all_to_all | solution.py:372
  48.5 0.1 reduce_sum.24
  48.6 23.1 %all_to_all.22 = bf16[16,32,128]{2,1,0:T(8,128)(2,1)S(1)} all-to-all(bf16[16,32,128]{2,1,0:T(8,128)(2,1)S(1)} %broadcast_in_dim.28), channel_id=1, replica_groups=mesh['z'=8,'yhi'=2,'ylo'=4,'core'=2,'x'=4] {'z','core'}, dimensions={0} | all-to-all | bytes 262144 | tf_op jit(solution)/shard_map/all_to_all | solution.py:347
  71.7 16.5 %all_to_all.23 = bf16[32,32,128]{2,1,0:T(8,128)(2,1)} all-to-all(bf16[32,32,128]{2,1,0:T(8,128)(2,1)S(1)} %broadcast_in_dim.29), channel_id=1, replica_groups=mesh['z'=8,'yhi'=2,'ylo'=4,'core'=2,'x'=4] {'yhi','ylo','x'}, dimensions={0} | all-to-all | bytes 524288 | tf_op jit(solution)/shard_map/all_to_all | solution.py:347
  88.3 1.8 %unpack.1 = (f32[27,64]{1,0:T(8,128)}, f32[1,64]{1,0:T(1,128)}, f32[64,1728]{1,0:T(8,128)}, f32[1,64]{1,0:T(1,128)}, f32[4,64]{1,0:T(4,128)}, /*index=5*/f32[1,4]{1,0:T(1,128)}) custom-call(bf16[16,64,128]{2,1,0:T(8,128)(2,1)} %bitcast.16), custom_call_target="tpu_custom_call" | custom-call | tf_op jit(solution)/shard_map/unpack/pallas_call | solution.py:319
  (4 shorter events, 0.1 us)
Async XLA Ops:
  0.6 20.2 %copy-start.1 = (bf16[128,512]{1,0:T(8,128)(2,1)S(1)}, bf16[128,512]{1,0:T(8,128)(2,1)}, u32[]{:S(2)}) copy-start(bf16[128,512]{1,0:T(8,128)(2,1)} %constant.28.clone.spread_ref) | copy-start | bytes 393220
  17.7 3.1 %collective-permute-start = (bf16[8,5,128]{2,1,0:T(8,128)(2,1)S(1)}, bf16[8,5,128]{2,1,0:T(8,128)(2,1)S(1)}, u32[]{:S(2)}, u32[]{:S(2)}) collective-permute-start(bf16[8,5,128]{2,1,0:T(8,128)(2,1)S(1)} %all_to_all.20.near_ref), channel_id=1, source_target_pairs={{16,32},{32,16},{20,36},{36,20},{24,40},{40,24},{28,44},{44,28},{4... | collective-permute-start | bytes 30728 | tf_op jit(solution)/shard_map/ppermute | solution.py:367
  18.3 2.3 %copy-start.7 = (f32[64]{0:T(128)S(1)}, f32[64]{0:T(128)}, u32[]{:S(2)}) copy-start(f32[64]{0:T(128)} %param.20) | copy-start | bytes 772
  18.4 2.5 %copy-start.4 = (f32[3,48,128]{2,1,0:T(8,128)S(1)}, f32[3,48,128]{2,1,0:T(8,128)}, u32[]{:S(2)}) copy-start(f32[3,48,128]{2,1,0:T(8,128)} %constant.29.clone.keep_ref) | copy-start | bytes 221188
  20.8 0.7 copy-start.5
  20.8 0.7 copy-start.6
  21.5 0.9 %copy-start = (bf16[64,1728]{1,0:T(8,128)(2,1)S(1)}, bf16[64,1728]{1,0:T(8,128)(2,1)}, u32[]{:S(2)}) copy-start(bf16[64,1728]{1,0:T(8,128)(2,1)} %w2_ref.1) | copy-start | bytes 663556
  22.4 0.9 copy-start.2
  23.3 0.9 copy-start.3

commit v3 on v2

--- a/solution.py
+++ b/solution.py
@@ -83,10 +83,8 @@
 SHIFTS = [(b, c) for b in (-1, 0, 1) for c in (-1, 0, 1)]
 
 
-def brick_kernel(
-    place_ref,
-    near_ref,
-    far_ref,
+def prep_kernel(
+    tissue_ref,
     cot_ref,
     w1_ref,
     b1_ref,
@@ -98,15 +96,84 @@
     odd_ref,
     spread_ref,
     keep_ref,
+    even_out,
+    odd_out,
+    spread_out_ref,
+    keep_out,
+    w1_out,
+    w2_out,
+    wb_out,
+    hw_out,
+    b1_out,
+    b2_out,
+    hb_out,
+    dp_out,
+    dh2_out,
+    gbh_out,
+):
+    bf16 = jnp.bfloat16
+    f32 = jnp.float32
+    even_out[...] = even_ref[...]
+    odd_out[...] = odd_ref[...]
+    spread_out_ref[...] = spread_ref[...]
+    keep_out[...] = keep_ref[...]
+    w2_out[...] = w2_ref[...]
+    hw = hw_ref[...]
+    hw_out[...] = hw
+    rows = jnp.concatenate([b1_ref[...], b2_ref[...], jnp.zeros((6, C), f32)], axis=0)
+    columns = rows.T
+    b1_out[...] = jnp.broadcast_to(columns[:, 0:1], (C, 128))
+    b2_out[...] = jnp.broadcast_to(columns[:, 1:2], (C, 128))
+    heads = jnp.concatenate([hb_ref[...], jnp.zeros((1, 124), f32)], axis=1)
+    heads = jnp.concatenate([heads, jnp.zeros((7, 128), f32)], axis=0).T
+    hb_out[...] = jnp.broadcast_to(heads[0:OUT_CH, 0:1], (OUT_CH, 128))
+    w1 = jnp.concatenate([w1_ref[...].astype(f32), jnp.zeros((5, C), f32)], axis=0).T
+    w1_out[...] = w1.astype(bf16)
+    w2f = w2_ref[...].astype(f32)
+    for pair in range(14):
+        wide = w2f[:, 128 * pair : min(128 * pair + 128, ACROSS)].T
+        for half in range(wide.shape[0] // 64):
+            tap = 2 * pair + half
+            at = 64 * ((2 - tap // 9) * 9 + tap % 9)
+            wb_out[:, at : at + 64] = wide[64 * half : 64 * half + 64].astype(bf16)
+    own = even_ref[128:192]
+    scale = jnp.where(tissue_ref[0, 0] > 0, 1.0 / 512.0, 0.0)
+    cot = (cot_ref[...].astype(f32) * scale).astype(bf16)
+    total = jnp.zeros((OUT_CH, 128), f32)
+    for x in range(8):
+        dp = dot(cot[:, 64 * x : 64 * x + 64], own)
+        total = total + dp
+        dp = dp.astype(bf16)
+        dp_out[:, 128 * x : 128 * x + 128] = dp
+        dh2_out[x] = lax.dot_general(hw, dp, (((0,), (0,)), ((), ())), preferred_element_type=f32)
+    gbh_out[...] = jnp.broadcast_to(jnp.sum(total, axis=1, keepdims=True), (OUT_CH, 128))
+
+
+def brick_kernel(
+    place_ref,
+    near_ref,
+    far_ref,
+    even_ref,
+    odd_ref,
+    spread_ref,
+    keep_ref,
+    w1_ref,
+    w2_ref,
+    wb_ref,
+    hw_ref,
+    b1_ref,
+    b2_ref,
+    hb_ref,
+    dp_ref,
+    dh2_ref,
+    gbh_ref,
     pred_ref,
     part_ref,
     rows_ref,
     flag_ref,
     s1_ref,
-    h1_ref,
     slope_ref,
     v_ref,
-    wb_ref,
     g_ref,
 ):
     position = place_ref[0]
@@ -139,7 +206,10 @@
     flag_ref[40:48] = jnp.zeros((8, 128), f32)
     masks = dot(flag_ref[...].astype(bf16), spread_ref[...])
     valid = masks[30:40, 384:512]
-    s1_ref[...] = jnp.zeros_like(s1_ref)
+    for cell in range(10):
+        s1_ref[cell, 24:32] = jnp.where(
+            lax.broadcasted_iota(jnp.int32, (8, 128), 0) == 3, 1.0, 0.0
+        )
     for b, c in SHIFTS:
         amount = 12 * b + c
         moved = [turn(cells_even, amount), turn(cells_odd, amount)]
@@ -168,22 +238,21 @@
     hw = hw_ref[...]
     hb = hb_ref[...]
     own = even_ref[128:192]
-    cot = (cot_ref[...].astype(f32) * (active / 512.0)).astype(bf16)
-    d_pred, dz2, h2_all = [], [], []
+    dz2, h2_all = [], []
+    grad_b2 = jnp.zeros((C, 128), f32)
     for x in range(8):
         stack = v_ref[x : x + 3].reshape(ACROSS, 128)
         value, slope = gelu_parts(dot(w2, stack) + b2)
         h2 = (value * active).astype(bf16)
         pred = ((dot(hw, h2) + hb) * active).astype(bf16)
         pred_ref[:, 64 * x : 64 * x + 64] = dot_t(pred, own).astype(bf16)
-        dp = dot(cot[:, 64 * x : 64 * x + 64], own)
-        d_pred.append(dp)
-        dp = dp.astype(bf16)
-        dh2 = lax.dot_general(hw, dp, (((0,), (0,)), ((), ())), preferred_element_type=f32)
-        d2 = (dh2 * slope * active).astype(bf16)
+        d2 = (dh2_ref[x] * slope).astype(bf16)
         dz2.append(d2)
         h2_all.append(h2)
-    grad_b2 = sum(d.astype(f32) for d in dz2)
+        d2 = d2.astype(f32)
+        grad_b2 = grad_b2 + d2
+        for index, (b, c) in enumerate(SHIFTS):
+            g_ref[x, 64 * index : 64 * index + 64] = turn(d2, -(12 * b + c)).astype(bf16)
     grad_b2 = jnp.sum(grad_b2, axis=1, keepdims=True)
     grad_w2 = None
     for x in range(0, 8, 2):
@@ -195,21 +264,7 @@
         grad_w2 = piece if grad_w2 is None else grad_w2 + piece
     for block in range(13):
         part_ref[block] = grad_w2[:, 128 * block : 128 * block + 128].astype(bf16)
-    d_flat = jnp.concatenate(d_pred, axis=1)
-    h2_flat = jnp.concatenate(h2_all, axis=1)
-    grad_wh = dot_t(h2_flat, d_flat.astype(bf16))
-    grad_bh = jnp.sum(d_flat, axis=1, keepdims=True)
-    w2f = w2.astype(f32)
-    for pair in range(14):
-        wide = w2f[:, 128 * pair : min(128 * pair + 128, ACROSS)].T
-        for half in range(wide.shape[0] // 64):
-            tap = 2 * pair + half
-            at = 64 * ((2 - tap // 9) * 9 + tap % 9)
-            wb_ref[:, at : at + 64] = wide[64 * half : 64 * half + 64].astype(bf16)
-    for x in range(8):
-        d2 = dz2[x].astype(f32)
-        for index, (b, c) in enumerate(SHIFTS):
-            g_ref[x, 64 * index : 64 * index + 64] = turn(d2, -(12 * b + c)).astype(bf16)
+    grad_wh = dot_t(jnp.concatenate(h2_all, axis=1), dp_ref[...])
     grad_w1 = None
     for cell in range(10):
         low, high = max(cell - 2, 0), min(cell + 1, 8)
@@ -219,12 +274,10 @@
         dz1 = dot(back, stack) * slope_ref[cell]
         head = dz1.astype(bf16)
         tail = (dz1 - head.astype(f32)).astype(bf16)
-        taps = s1_ref[cell]
-        ones = lax.broadcasted_iota(jnp.int32, (32, 128), 0) == 27
-        taps = jnp.where(ones, 1.0, taps).astype(bf16)
+        taps = s1_ref[cell].astype(bf16)
         piece = dot_t(head, taps) + dot_t(tail, taps)
         grad_w1 = piece if grad_w1 is None else grad_w1 + piece
-    column = jnp.concatenate([grad_bh, jnp.zeros((60, 1), f32)], axis=0)
+    column = jnp.concatenate([gbh_ref[:, 0:1], jnp.zeros((60, 1), f32)], axis=0)
     small = jnp.concatenate(
         [grad_w1[:, 0:28], grad_b2, grad_wh, column, jnp.zeros((64, 30), f32)], axis=1
     )
@@ -273,33 +326,37 @@
 BIG = 48 * 1024 * 1024
 
 
-def all_brick_work(near, far, position, cot, w1, b1, w2, b2, hw, hb):
+def prepare(tissue, cot, w1, b1, w2, b2, hw, hb):
     bf16, f32 = jnp.bfloat16, jnp.float32
     even, odd, spread, keep = tables()
+    shapes = [
+        ((384, 128), bf16),
+        ((384, 128), bf16),
+        ((128, 512), bf16),
+        ((3, 48, 128), f32),
+        ((C, 32), bf16),
+        ((C, ACROSS), bf16),
+        ((C, ACROSS), bf16),
+        ((OUT_CH, C), bf16),
+        ((C, 128), f32),
+        ((C, 128), f32),
+        ((OUT_CH, 128), f32),
+        ((OUT_CH, 1024), bf16),
+        ((8, C, 128), f32),
+        ((OUT_CH, 128), f32),
+    ]
     return pl.pallas_call(
-        brick_kernel,
-        out_shape=(
-            jax.ShapeDtypeStruct((OUT_CH, 512), bf16),
-            jax.ShapeDtypeStruct((BLOCKS, C, 128), bf16),
+        prep_kernel,
+        out_shape=tuple(jax.ShapeDtypeStruct(shape, kind) for shape, kind in shapes),
+        in_specs=[SMEM] + [VMEM] * 11,
+        out_specs=(VMEM,) * len(shapes),
+        compiler_params=pltpu.CompilerParams(vmem_limit_bytes=BIG),
+        cost_estimate=pl.CostEstimate(
+            flops=4_000_000_000, bytes_accessed=4_000_000, transcendentals=0
         ),
-        in_specs=[SMEM] + [VMEM] * 13,
-        out_specs=(VMEM, VMEM),
-        scratch_shapes=[
-            pltpu.VMEM((8, 384), f32),
-            pltpu.VMEM((48, 128), f32),
-            pltpu.VMEM((10, 32, 128), f32),
-            pltpu.VMEM((8, 128), f32),
-            pltpu.VMEM((10, C, 128), f32),
-            pltpu.VMEM((10, GROUP, 128), bf16),
-            pltpu.VMEM((C, ACROSS), bf16),
-            pltpu.VMEM((8, GROUP, 128), bf16),
-        ],
-        compiler_params=pltpu.CompilerParams(vmem_limit_bytes=BIG),
-        name="brick",
+        name="prep",
     )(
-        position,
-        near,
-        far,
+        tissue,
         cot,
         w1,
         b1,
@@ -312,6 +369,29 @@
         spread.astype(bf16),
         keep,
     )
+
+
+def all_brick_work(near, far, position, ready):
+    bf16, f32 = jnp.bfloat16, jnp.float32
+    return pl.pallas_call(
+        brick_kernel,
+        out_shape=(
+            jax.ShapeDtypeStruct((OUT_CH, 512), bf16),
+            jax.ShapeDtypeStruct((BLOCKS, C, 128), bf16),
+        ),
+        in_specs=[SMEM] + [VMEM] * (2 + len(ready)),
+        out_specs=(VMEM, VMEM),
+        scratch_shapes=[
+            pltpu.VMEM((8, 384), f32),
+            pltpu.VMEM((48, 128), f32),
+            pltpu.VMEM((10, 32, 128), f32),
+            pltpu.VMEM((10, C, 128), f32),
+            pltpu.VMEM((10, GROUP, 128), bf16),
+            pltpu.VMEM((8, GROUP, 128), bf16),
+        ],
+        compiler_params=pltpu.CompilerParams(vmem_limit_bytes=BIG),
+        name="brick",
+    )(position, near, far, *ready)
 
 
 def unpack(gathered):
@@ -365,10 +445,8 @@
     mine = pack(neighbours[0], tissue, micrograph[0])
     near = lax.all_to_all(mine, ("ylo", "core"), 0, 0, tiled=True)
     far = lax.ppermute(near, BRICK, PAIRS)
-    w1p = jnp.pad(w1, ((0, 0), (0, 5)))
-    prediction, parts = all_brick_work(
-        near, far, position, cot[0, 0], w1p, b1[:, None], w2, b2[:, None], hw, hb[:, None]
-    )
+    ready = prepare(tissue, cot[0, 0], w1.T, b1[None], w2, b2[None], hw, hb[None])
+    prediction, parts = all_brick_work(near, far, position, ready)
     mixed = lax.all_to_all(parts.reshape(32, 32, 128), FIRST, 0, 0, tiled=True)
     share = jnp.sum(mixed.astype(f32), axis=0).astype(bf16)
     shares = spread_out(share, SECOND, 16)

time: 90.6 us -> 89.3 us (0.986)
  blocking collectives: 72.5 us -> 70.6 us
  Pallas kernels: 9.44 us -> 10.7 us
    broadcast_in_dim x3 -> x0, local copies, waits for them, and re-layouts: 1.62 us -> none  [the longest x1 0.78 us: shards(): hb[:, None]]
    all_to_all x2, blocking collectives: 39.6 us -> 38.1 us  [spread_out(): return lax.all_to_all(copies, axes, 0, 0, tiled=True)]
    unnamed x17 -> x22, local copies, waits for them, and re-layouts: 4.19 us -> 5.15 us
  transfers between devices with their start and end apart: 1 -> 1, of which waited for: 0 -> 0; matrix products, arithmetic and copies ran while one was open for 3% -> 0% of each run, Pallas kernels for 0% -> 1%
where the time goes in v3:
time: 89.3 us; the launch traced here: 88.8 us
  blocking collectives  70.6 us (79%)
  Pallas kernels  10.7 us (12%)
  local copies, waits for them, and re-layouts  5.21 us (6%)
  between operations  1.38 us (2%)
    all_to_all x2, blocking collectives, spread_out(): return lax.all_to_all(copies, axes, 0, 0, tiled=True)  38.1 us
    all_to_all x1, blocking collectives, shards(): mixed = lax.all_to_all(parts.reshape(32, 32, 128), FIRST, 0, 0, tiled=True)  17.3 us
    all_to_all x1, blocking collectives, shards(): near = lax.all_to_all(mine, ('ylo', 'core'), 0, 0, tiled=True)  15.2 us
    pallas_call x1, Pallas kernels, all_brick_work(): pl.pallas_call(brick_kernel, out_shape=(jax.ShapeDtypeStruct((OUT_CH, 512...  6.91 us
    unnamed x22, local copies, waits for them, and re-layouts  5.15 us
  transfers between devices with their start and end apart: 1, of which 0 were waited for; matrix products, arithmetic and copies ran while one was open for 0% of the time, Pallas kernels for 1%

profile of v3, /device:TPU:1, one launch (start us, length us, event | category | flops | bytes accessed | tf_op | source)
XLA Modules:
  0.0 88.8 jit_solution(6891291690555670318)
XLA Ops:
  1.3 1.3 %pack.1 = bf16[8,5,128]{2,1,0:T(8,128)(2,1)} custom-call(s32[1,26]{1,0:T(1,128)} %bitcast.23, s32[1,1]{1,0:T(1,128)S(6)} %copy.21.tissue_ref, bf16[1,512]{1,0:T(2,128)(2,1)} %bitcast.22), custom_call_target="tpu_custom_call" | custom-call | tf_op jit(solution)/shard_map/pack/pallas_call | solution.py:416
  2.6 0.0 copy-start.2
  2.6 0.0 copy-start.4
  2.6 0.0 copy-start.5
  2.6 0.0 copy-start.6
  2.6 15.2 %all_to_all.20.near_ref = bf16[8,5,128]{2,1,0:T(8,128)(2,1)S(1)} all-to-all(bf16[8,5,128]{2,1,0:T(8,128)(2,1)} %pack.1), channel_id=1, replica_groups=mesh['z'=8,'yhi'=2,'ylo'=4,'core'=2,'x'=4] {'ylo','core'}, dimensions={0} | all-to-all | bytes 20480 | tf_op jit(solution)/shard_map/all_to_all | solution.py:446
  17.8 0.0 copy-start.1
  17.8 0.8 collective-permute-start
  18.6 0.0 copy-start.3
  18.6 0.0 copy-done.2
  18.6 0.0 copy-done.4
  18.6 0.0 copy-done.5
  18.6 0.0 copy-done.6
  18.6 0.0 copy-done.1
  18.6 0.6 copy-done.3
  19.3 0.0 copy-start
  19.3 0.9 %copy-done = bf16[64,1728]{1,0:T(8,128)(2,1)S(1)} copy-done((bf16[64,1728]{1,0:T(8,128)(2,1)S(1)}, bf16[64,1728]{1,0:T(8,128)(2,1)}, u32[]{:S(2)}) %copy-start) | copy-done | bytes 221208
  20.2 0.0 copy-start.7
  20.2 0.9 %copy-done.7 = bf16[128,512]{1,0:T(8,128)(2,1)S(1)} copy-done((bf16[128,512]{1,0:T(8,128)(2,1)S(1)}, bf16[128,512]{1,0:T(8,128)(2,1)}, u32[]{:S(2)}) %copy-start.7) | copy-done | bytes 131096
  21.1 0.0 copy-start.8
  21.1 0.9 %copy-done.8 = bf16[384,128]{1,0:T(8,128)(2,1)S(1)} copy-done((bf16[384,128]{1,0:T(8,128)(2,1)S(1)}, bf16[384,128]{1,0:T(8,128)(2,1)}, u32[]{:S(2)}) %copy-start.8) | copy-done | bytes 98328
  22.0 0.0 copy-start.9
  22.0 0.9 %copy-done.9 = bf16[384,128]{1,0:T(8,128)(2,1)S(1)} copy-done((bf16[384,128]{1,0:T(8,128)(2,1)S(1)}, bf16[384,128]{1,0:T(8,128)(2,1)}, u32[]{:S(2)}) %copy-start.9) | copy-done | bytes 98328
  22.9 0.0 copy-start.10
  22.9 0.9 copy-done.10
  23.8 0.7 prep.1
  24.5 0.0 collective-permute-done.far_ref
  24.5 6.9 %brick.1 = (bf16[4,512]{1,0:T(4,128)(2,1)}, bf16[16,64,128]{2,1,0:T(8,128)(2,1)S(1)}) custom-call(s32[1]{0:T(128)} %bitcast.place_ref, bf16[8,5,128]{2,1,0:T(8,128)(2,1)S(1)} %all_to_all.20.near_ref, bf16[8,5,128]{2,1,0:T(8,128)(2,1)S(1)} %collective-permute-done.far_ref, bf16[384,128]{1,0:T(8,128)(2,1)S(1)} %get-tuple-element.29.even_ref, ...), custom_call_target="tpu_custom_call" | custom-call | tf_op jit(solution)/shard_map/brick/pallas_call | solution.py:376
  31.4 17.3 %all_to_all.21 = bf16[32,32,128]{2,1,0:T(8,128)(2,1)S(1)} all-to-all(bf16[32,32,128]{2,1,0:T(8,128)(2,1)S(1)} %bitcast.15), channel_id=1, replica_groups=mesh['z'=8,'yhi'=2,'ylo'=4,'core'=2,'x'=4] {'yhi','ylo','x'}, dimensions={0} | all-to-all | bytes 524288 | tf_op jit(solution)/shard_map/all_to_all | solution.py:450
  48.7 0.1 reduce_sum.24
  48.8 21.7 %all_to_all.22 = bf16[16,32,128]{2,1,0:T(8,128)(2,1)S(1)} all-to-all(bf16[16,32,128]{2,1,0:T(8,128)(2,1)S(1)} %broadcast_in_dim.28), channel_id=1, replica_groups=mesh['z'=8,'yhi'=2,'ylo'=4,'core'=2,'x'=4] {'z','core'}, dimensions={0} | all-to-all | bytes 262144 | tf_op jit(solution)/shard_map/all_to_all | solution.py:427
  70.6 16.4 %all_to_all.23 = bf16[32,32,128]{2,1,0:T(8,128)(2,1)} all-to-all(bf16[32,32,128]{2,1,0:T(8,128)(2,1)S(1)} %broadcast_in_dim.29), channel_id=1, replica_groups=mesh['z'=8,'yhi'=2,'ylo'=4,'core'=2,'x'=4] {'yhi','ylo','x'}, dimensions={0} | all-to-all | bytes 524288 | tf_op jit(solution)/shard_map/all_to_all | solution.py:427
  87.0 1.8 %unpack.1 = (f32[27,64]{1,0:T(8,128)}, f32[1,64]{1,0:T(1,128)}, f32[64,1728]{1,0:T(8,128)}, f32[1,64]{1,0:T(1,128)}, f32[4,64]{1,0:T(4,128)}, /*index=5*/f32[1,4]{1,0:T(1,128)}) custom-call(bf16[16,64,128]{2,1,0:T(8,128)(2,1)} %bitcast.21), custom_call_target="tpu_custom_call" | custom-call | tf_op jit(solution)/shard_map/unpack/pallas_call | solution.py:399
  (3 shorter events, 0.1 us)
Async XLA Ops:
  2.6 16.0 %copy-start.2 = (bf16[1,1,4,512]{3,2,1,0:T(4,128)(2,1)S(1)}, bf16[1,1,4,512]{3,2,1,0:T(4,128)(2,1)}, u32[]{:S(2)}) copy-start(bf16[1,1,4,512]{3,2,1,0:T(4,128)(2,1)} %param.23) | copy-start | bytes 12292
  2.6 16.0 %copy-start.4 = (f32[64]{0:T(128)S(1)}, f32[64]{0:T(128)}, u32[]{:S(2)}) copy-start(f32[64]{0:T(128)} %param.18) | copy-start | bytes 772
  2.6 16.0 %copy-start.5 = (f32[64]{0:T(128)S(1)}, f32[64]{0:T(128)}, u32[]{:S(2)}) copy-start(f32[64]{0:T(128)} %param.20) | copy-start | bytes 772
  2.6 16.0 %copy-start.6 = (f32[4]{0:T(128)S(1)}, f32[4]{0:T(128)}, u32[]{:S(2)}) copy-start(f32[4]{0:T(128)} %param.22) | copy-start | bytes 52
  17.8 0.8 copy-start.1
  17.8 6.7 %collective-permute-start = (bf16[8,5,128]{2,1,0:T(8,128)(2,1)S(1)}, bf16[8,5,128]{2,1,0:T(8,128)(2,1)S(1)}, u32[]{:S(2)}, u32[]{:S(2)}) collective-permute-start(bf16[8,5,128]{2,1,0:T(8,128)(2,1)S(1)} %all_to_all.20.near_ref), channel_id=1, source_target_pairs={{16,32},{32,16},{20,36},{36,20},{24,40},{40,24},{28,44},{44,28},{4... | collective-permute-start | bytes 30728 | tf_op jit(solution)/shard_map/ppermute | solution.py:447
  18.6 0.7 copy-start.3
  19.3 0.9 %copy-start = (bf16[64,1728]{1,0:T(8,128)(2,1)S(1)}, bf16[64,1728]{1,0:T(8,128)(2,1)}, u32[]{:S(2)}) copy-start(bf16[64,1728]{1,0:T(8,128)(2,1)} %w2_ref.1) | copy-start | bytes 663556
  20.2 0.9 %copy-start.7 = (bf16[128,512]{1,0:T(8,128)(2,1)S(1)}, bf16[128,512]{1,0:T(8,128)(2,1)}, u32[]{:S(2)}) copy-start(bf16[128,512]{1,0:T(8,128)(2,1)} %constant.26.clone.spread_ref) | copy-start | bytes 393220
  21.1 0.9 %copy-start.8 = (bf16[384,128]{1,0:T(8,128)(2,1)S(1)}, bf16[384,128]{1,0:T(8,128)(2,1)}, u32[]{:S(2)}) copy-start(bf16[384,128]{1,0:T(8,128)(2,1)} %constant.25.clone.odd_ref) | copy-start | bytes 294916
  22.0 0.9 %copy-start.9 = (bf16[384,128]{1,0:T(8,128)(2,1)S(1)}, bf16[384,128]{1,0:T(8,128)(2,1)}, u32[]{:S(2)}) copy-start(bf16[384,128]{1,0:T(8,128)(2,1)} %constant.24.clone.even_ref) | copy-start | bytes 294916
  22.9 0.9 copy-start.10

commit v4 on v3

--- a/solution.py
+++ b/solution.py
@@ -12,7 +12,7 @@
 ROW = 12
 GROUP = 576
 ACROSS = 1728
-BLOCKS = 16
+BLOCKS = 14
 GROUP_SIZE = 8
 ROOT = 0.7978845608028654
 CUBIC = 0.044715
@@ -78,6 +78,17 @@
 
 def dot_t(a, b):
     return lax.dot_general(a, b, (((1,), (1,)), ((), ())), preferred_element_type=jnp.float32)
+
+
+def paired(ref, first, count):
+    rows = count * GROUP
+    return jnp.concatenate(
+        [
+            ref[first : first + count].reshape(rows, 128),
+            ref[first + 1 : first + 1 + count].reshape(rows, 128),
+        ],
+        axis=1,
+    )
 
 
 SHIFTS = [(b, c) for b in (-1, 0, 1) for c in (-1, 0, 1)]
@@ -139,14 +150,12 @@
     own = even_ref[128:192]
     scale = jnp.where(tissue_ref[0, 0] > 0, 1.0 / 512.0, 0.0)
     cot = (cot_ref[...].astype(f32) * scale).astype(bf16)
-    total = jnp.zeros((OUT_CH, 128), f32)
     for x in range(8):
-        dp = dot(cot[:, 64 * x : 64 * x + 64], own)
-        total = total + dp
-        dp = dp.astype(bf16)
+        dp = dot(cot[:, 64 * x : 64 * x + 64], own).astype(bf16)
         dp_out[:, 128 * x : 128 * x + 128] = dp
         dh2_out[x] = lax.dot_general(hw, dp, (((0,), (0,)), ((), ())), preferred_element_type=f32)
-    gbh_out[...] = jnp.broadcast_to(jnp.sum(total, axis=1, keepdims=True), (OUT_CH, 128))
+    sums = dot_t(jnp.ones((8, 1024), bf16), dp_out[...])
+    gbh_out[...] = jnp.concatenate([sums, jnp.zeros((8, C - OUT_CH), f32)], axis=1)
 
 
 def brick_kernel(
@@ -239,67 +248,67 @@
     hb = hb_ref[...]
     own = even_ref[128:192]
     dz2, h2_all = [], []
-    grad_b2 = jnp.zeros((C, 128), f32)
-    for x in range(8):
-        stack = v_ref[x : x + 3].reshape(ACROSS, 128)
-        value, slope = gelu_parts(dot(w2, stack) + b2)
-        h2 = (value * active).astype(bf16)
-        pred = ((dot(hw, h2) + hb) * active).astype(bf16)
-        pred_ref[:, 64 * x : 64 * x + 64] = dot_t(pred, own).astype(bf16)
-        d2 = (dh2_ref[x] * slope).astype(bf16)
-        dz2.append(d2)
-        h2_all.append(h2)
-        d2 = d2.astype(f32)
-        grad_b2 = grad_b2 + d2
-        for index, (b, c) in enumerate(SHIFTS):
-            g_ref[x, 64 * index : 64 * index + 64] = turn(d2, -(12 * b + c)).astype(bf16)
-    grad_b2 = jnp.sum(grad_b2, axis=1, keepdims=True)
+    for x in range(0, 8, 2):
+        both_z2 = dot(w2, paired(v_ref, x, 3))
+        for half in range(2):
+            value, slope = gelu_parts(both_z2[:, 128 * half : 128 * half + 128] + b2)
+            h2 = (value * active).astype(bf16)
+            pred = ((dot(hw, h2) + hb) * active).astype(bf16)
+            at = 64 * (x + half)
+            pred_ref[:, at : at + 64] = dot_t(pred, own).astype(bf16)
+            d2 = (dh2_ref[x + half] * slope).astype(bf16)
+            dz2.append(d2)
+            h2_all.append(h2)
+            d2 = d2.astype(f32)
+            for index, (b, c) in enumerate(SHIFTS):
+                g_ref[x + half + 1, 64 * index : 64 * index + 64] = turn(
+                    d2, -(12 * b + c)
+                ).astype(bf16)
     grad_w2 = None
+    grad_b2 = None
+    ones = jnp.ones((8, 256), bf16)
     for x in range(0, 8, 2):
         left = jnp.concatenate(dz2[x : x + 2], axis=1)
-        right = jnp.concatenate(
-            [v_ref[x : x + 3].reshape(ACROSS, 128), v_ref[x + 1 : x + 4].reshape(ACROSS, 128)], axis=1
-        )
-        piece = dot_t(left, right)
+        piece = dot_t(left, paired(v_ref, x, 3))
         grad_w2 = piece if grad_w2 is None else grad_w2 + piece
+        piece = dot_t(ones, left)
+        grad_b2 = piece if grad_b2 is None else grad_b2 + piece
     for block in range(13):
         part_ref[block] = grad_w2[:, 128 * block : 128 * block + 128].astype(bf16)
-    grad_wh = dot_t(jnp.concatenate(h2_all, axis=1), dp_ref[...])
+    grad_wh = dot_t(dp_ref[...], jnp.concatenate(h2_all, axis=1))
     grad_w1 = None
-    for cell in range(10):
-        low, high = max(cell - 2, 0), min(cell + 1, 8)
-        skip = low - (cell - 2)
-        stack = g_ref[low:high].reshape((high - low) * GROUP, 128)
-        back = wb_ref[:, skip * GROUP : (skip + high - low) * GROUP]
-        dz1 = dot(back, stack) * slope_ref[cell]
-        head = dz1.astype(bf16)
-        tail = (dz1 - head.astype(f32)).astype(bf16)
-        taps = s1_ref[cell].astype(bf16)
-        piece = dot_t(head, taps) + dot_t(tail, taps)
-        grad_w1 = piece if grad_w1 is None else grad_w1 + piece
-    column = jnp.concatenate([gbh_ref[:, 0:1], jnp.zeros((60, 1), f32)], axis=0)
+    g_ref[0] = jnp.zeros((GROUP, 128), bf16)
+    g_ref[9] = jnp.zeros((GROUP, 128), bf16)
+    for cell in range(0, 10, 2):
+        skip = 1 if cell == 0 else 0
+        count = 2 if cell in (0, 8) else 3
+        back = wb_ref[:, skip * GROUP : (skip + count) * GROUP]
+        both_dh1 = dot(back, paired(g_ref, cell - 1 + skip, count))
+        for half in range(2):
+            dz1 = both_dh1[:, 128 * half : 128 * half + 128] * slope_ref[cell + half]
+            head = dz1.astype(bf16)
+            tail = (dz1 - head.astype(f32)).astype(bf16)
+            taps = s1_ref[cell + half].astype(bf16)
+            piece = dot_t(taps, head) + dot_t(taps, tail)
+            grad_w1 = piece if grad_w1 is None else grad_w1 + piece
     small = jnp.concatenate(
-        [grad_w1[:, 0:28], grad_b2, grad_wh, column, jnp.zeros((64, 30), f32)], axis=1
+        [grad_w1[0:28], grad_wh, grad_b2[0:1], gbh_ref[0:1], jnp.zeros((30, C), f32)], axis=0
     )
     part_ref[13] = jnp.concatenate([grad_w2[:, 1664:1728], small], axis=1).astype(bf16)
-    part_ref[14] = jnp.concatenate([small.T, jnp.zeros((64, 64), f32)], axis=1).astype(bf16)
-    part_ref[15] = jnp.zeros((64, 128), bf16)
-
-
-LISTED = (3, 4, 5, 12, None, 13, 20, 21, 22)
 
 
 def pack_kernel(list_ref, tissue_ref, cells_ref, out_ref):
     f32 = jnp.float32
     lane = lax.broadcasted_iota(jnp.int32, (1, 128), 1)
-    slot = jnp.where(lane < 48, lane % 16, 16)
-    flags = jnp.zeros((1, 128), f32)
-    for index, entry in enumerate(LISTED):
-        if entry is None:
-            present = tissue_ref[0, 0] > 0
-        else:
-            present = list_ref[0, entry] >= 0
-        flags = jnp.where(slot == index, jnp.where(present, 1.0, 0.0), flags)
+    listed = jnp.concatenate([list_ref[...], jnp.zeros((1, 102), jnp.int32)], axis=1)
+    present = jnp.where(listed >= 0, 1.0, 0.0)
+    flags = jnp.where(lane < 3, turn(present, 3), 0.0)
+    flags = jnp.where(lane == 3, turn(present, 9), flags)
+    own = jnp.where(tissue_ref[...] > 0, 1.0, 0.0)
+    flags = jnp.where(lane == 4, own, flags)
+    flags = jnp.where(lane == 5, turn(present, 8), flags)
+    flags = jnp.where((lane > 5) & (lane < 9), turn(present, 14), flags)
+    flags = flags + turn(flags, -16) + turn(flags, -32)
     cells = cells_ref[...].astype(f32)
     rows = [cells[:, 128 * row : 128 * row + 128] for row in range(4)]
     tile = jnp.concatenate(rows + [flags], axis=0).astype(jnp.bfloat16)
@@ -313,17 +322,18 @@
         w2_ref[:, 128 * block : 128 * block + 128] = all_ref[block].astype(f32)
     mixed = all_ref[13].astype(f32)
     w2_ref[:, 1664:1728] = mixed[:, 0:64]
-    rows = all_ref[14].astype(f32)
-    w1_ref[...] = rows[0:27, 0:64]
-    b1_ref[...] = rows[27:28, 0:64]
-    b2_ref[...] = rows[28:29, 0:64]
-    hw_ref[...] = rows[29:33, 0:64]
+    rows = mixed[:, 64:128]
+    w1_ref[...] = rows[0:27]
+    b1_ref[...] = rows[27:28]
+    hw_ref[...] = rows[28:32]
+    b2_ref[...] = rows[32:33]
     hb_ref[...] = rows[33:34, 0:4]
 
 
 VMEM = pl.BlockSpec(memory_space=pltpu.VMEM)
 SMEM = pl.BlockSpec(memory_space=pltpu.SMEM)
-BIG = 48 * 1024 * 1024
+BIG = 24 * 1024 * 1024
+SMALL = 4 * 1024 * 1024
 
 
 def prepare(tissue, cot, w1, b1, w2, b2, hw, hb):
@@ -343,7 +353,7 @@
         ((OUT_CH, 128), f32),
         ((OUT_CH, 1024), bf16),
         ((8, C, 128), f32),
-        ((OUT_CH, 128), f32),
+        ((8, C), f32),
     ]
     return pl.pallas_call(
         prep_kernel,
@@ -387,7 +397,7 @@
             pltpu.VMEM((10, 32, 128), f32),
             pltpu.VMEM((10, C, 128), f32),
             pltpu.VMEM((10, GROUP, 128), bf16),
-            pltpu.VMEM((8, GROUP, 128), bf16),
+            pltpu.VMEM((10, GROUP, 128), bf16),
         ],
         compiler_params=pltpu.CompilerParams(vmem_limit_bytes=BIG),
         name="brick",
@@ -408,6 +418,7 @@
         ),
         in_specs=[VMEM],
         out_specs=(VMEM,) * 6,
+        compiler_params=pltpu.CompilerParams(vmem_limit_bytes=SMALL),
         name="unpack",
     )(gathered)
 
@@ -416,8 +427,9 @@
     return pl.pallas_call(
         pack_kernel,
         out_shape=jax.ShapeDtypeStruct((GROUP_SIZE, 5, 128), jnp.bfloat16),
-        in_specs=[SMEM, SMEM, VMEM],
+        in_specs=[VMEM] * 3,
         out_specs=VMEM,
+        compiler_params=pltpu.CompilerParams(vmem_limit_bytes=SMALL),
         name="pack",
     )(neighbours, tissue, micrograph)
 
@@ -427,9 +439,11 @@
     return lax.all_to_all(copies, axes, 0, 0, tiled=True)
 
 
-BRICK = ("z", "yhi", "ylo", "core")
-FIRST = ("yhi", "ylo", "x")
-SECOND = ("z", "core")
+BRICK = ("z", "yhi", "ymid", "ylo", "core")
+NEAR = ("ymid", "ylo", "core")
+FIRST = ("ylo", "core", "x")
+SECOND = ("z", "yhi", "ymid")
+SHARES, ROWS = 16, 56
 HALF = GROUP_SIZE // 2
 PAIRS = [
     pair
@@ -441,17 +455,17 @@
 
 def shards(micrograph, tissue, neighbours, w1, b1, w2, b2, hw, hb, cot):
     bf16, f32 = jnp.bfloat16, jnp.float32
-    position = lax.axis_index(("ylo", "core")).astype(jnp.int32).reshape(1)
+    position = lax.axis_index(NEAR).astype(jnp.int32).reshape(1)
     mine = pack(neighbours[0], tissue, micrograph[0])
-    near = lax.all_to_all(mine, ("ylo", "core"), 0, 0, tiled=True)
+    near = lax.all_to_all(mine, NEAR, 0, 0, tiled=True)
     far = lax.ppermute(near, BRICK, PAIRS)
     ready = prepare(tissue, cot[0, 0], w1.T, b1[None], w2, b2[None], hw, hb[None])
     prediction, parts = all_brick_work(near, far, position, ready)
-    mixed = lax.all_to_all(parts.reshape(32, 32, 128), FIRST, 0, 0, tiled=True)
+    mixed = lax.all_to_all(parts.reshape(SHARES, ROWS, 128), FIRST, 0, 0, tiled=True)
     share = jnp.sum(mixed.astype(f32), axis=0).astype(bf16)
-    shares = spread_out(share, SECOND, 16)
+    shares = spread_out(share, SECOND, 512 // SHARES)
     share = jnp.sum(shares.astype(f32), axis=0).astype(bf16)
-    gathered = spread_out(share, FIRST, 32).reshape(BLOCKS, C, 128)
+    gathered = spread_out(share, FIRST, SHARES).reshape(BLOCKS, C, 128)
     g_w1, g_b1, g_w2, g_b2, g_hw, g_hb = unpack(gathered)
     return (
         prediction[None, None],
@@ -465,7 +479,7 @@
 
 
 def solution(mesh):
-    fine = Mesh(mesh.devices.reshape(8, 2, 4, 2, 4), ("z", "yhi", "ylo", "core", "x"))
+    fine = Mesh(mesh.devices.reshape(8, 2, 2, 2, 2, 4), BRICK + ("x",))
     return jax.shard_map(
         shards,
         mesh=fine,

time: 89.3 us -> 84.5 us (0.946)
  Pallas kernels: 10.7 us -> 7.64 us
  blocking collectives: 70.6 us -> 68.2 us
    all_to_all x2, blocking collectives: 32.5 us -> 24.7 us  [the longest x1 14.3 us: shards(): near = lax.all_to_all(mine, NEAR, 0, 0, tiled=True)]
    all_to_all x2, blocking collectives: 38.1 us -> 43.5 us  [spread_out(): return lax.all_to_all(copies, axes, 0, 0, tiled=True)]
    pallas_call x1, Pallas kernels: 1.31 us -> 0.15 us  [pack(): pl.pallas_call(pack_kernel, out_shape=jax.ShapeDtypeStruct((GROUP_SIZE, 5...]
    pallas_call x1, Pallas kernels: 6.91 us -> 5.87 us  [all_brick_work(): pl.pallas_call(brick_kernel, out_shape=(jax.ShapeDtypeStruct((OUT_CH, 512...]
    pallas_call x1, Pallas kernels: 1.75 us -> 0.85 us  [unpack(): pl.pallas_call(unpack_kernel, out_shape=(jax.ShapeDtypeStruct((27, C), f3...]
    unnamed x22 -> x26, local copies, waits for them, and re-layouts: 5.15 us -> 5.83 us
where the time goes in v4:
time: 84.5 us; the launch traced here: 84 us
  blocking collectives  68.2 us (81%)
  Pallas kernels  7.64 us (9%)
  local copies, waits for them, and re-layouts  5.92 us (7%)
  between operations  1.4 us (2%)
    all_to_all x2, blocking collectives, spread_out(): return lax.all_to_all(copies, axes, 0, 0, tiled=True)  43.5 us
    all_to_all x1, blocking collectives, shards(): near = lax.all_to_all(mine, NEAR, 0, 0, tiled=True)  14.3 us
    all_to_all x1, blocking collectives, shards(): lax.all_to_all(parts.reshape(SHARES, ROWS, 128), FIRST, 0, 0, tiled=True)  10.4 us
    pallas_call x1, Pallas kernels, all_brick_work(): pl.pallas_call(brick_kernel, out_shape=(jax.ShapeDtypeStruct((OUT_CH, 512...  5.87 us
    unnamed x26, local copies, waits for them, and re-layouts  5.83 us
  transfers between devices with their start and end apart: 1, of which 0 were waited for; matrix products, arithmetic and copies ran while one was open for 0% of the time, Pallas kernels for 1%

profile of v4, /device:TPU:1, one launch (start us, length us, event | category | flops | bytes accessed | tf_op | source)
XLA Modules:
  0.0 84.0 jit_solution(3076590895389079478)
XLA Ops:
  1.3 0.0 copy-start
  1.3 0.0 copy-start.1
  1.3 0.7 copy-done
  2.0 0.0 copy-done.1
  2.0 0.2 pack.1
  2.1 0.0 copy-start.4
  2.1 0.0 copy-start.6
  2.1 0.0 copy-start.7
  2.1 0.0 copy-start.8
  2.1 14.3 %all_to_all.20.near_ref = bf16[8,5,128]{2,1,0:T(8,128)(2,1)S(1)} all-to-all(bf16[8,5,128]{2,1,0:T(8,128)(2,1)S(1)} %pack.1), channel_id=1, replica_groups=mesh['z'=8,'yhi'=2,'ymid'=2,'ylo'=2,'core'=2,'x'=4] {'ymid','ylo','core'}, dimensions={0} | all-to-all | bytes 20480 | tf_op jit(solution)/shard_map/all_to_all | solution.py:460
  16.4 0.0 copy-start.3
  16.4 0.8 collective-permute-start
  17.2 0.0 copy-start.5
  17.2 0.0 copy-done.4
  17.3 0.0 copy-done.6
  17.3 0.0 copy-done.7
  17.3 0.0 copy-done.8
  17.3 0.0 copy-done.3
  17.3 0.6 copy-done.5
  17.9 0.0 copy-start.2
  17.9 0.9 %copy-done.2 = bf16[64,1728]{1,0:T(8,128)(2,1)S(1)} copy-done((bf16[64,1728]{1,0:T(8,128)(2,1)S(1)}, bf16[64,1728]{1,0:T(8,128)(2,1)}, u32[]{:S(2)}) %copy-start.2) | copy-done | bytes 221208
  18.9 0.0 copy-start.9
  18.9 0.9 %copy-done.9 = bf16[128,512]{1,0:T(8,128)(2,1)S(1)} copy-done((bf16[128,512]{1,0:T(8,128)(2,1)S(1)}, bf16[128,512]{1,0:T(8,128)(2,1)}, u32[]{:S(2)}) %copy-start.9) | copy-done | bytes 131096
  19.8 0.0 copy-start.10
  19.8 0.9 %copy-done.10 = bf16[384,128]{1,0:T(8,128)(2,1)S(1)} copy-done((bf16[384,128]{1,0:T(8,128)(2,1)S(1)}, bf16[384,128]{1,0:T(8,128)(2,1)}, u32[]{:S(2)}) %copy-start.10) | copy-done | bytes 98328
  20.7 0.0 copy-start.11
  20.7 0.9 %copy-done.11 = bf16[384,128]{1,0:T(8,128)(2,1)S(1)} copy-done((bf16[384,128]{1,0:T(8,128)(2,1)S(1)}, bf16[384,128]{1,0:T(8,128)(2,1)}, u32[]{:S(2)}) %copy-start.11) | copy-done | bytes 98328
  21.5 0.0 copy-start.12
  21.5 0.9 %copy-done.12 = f32[3,48,128]{2,1,0:T(8,128)S(1)} copy-done((f32[3,48,128]{2,1,0:T(8,128)S(1)}, f32[3,48,128]{2,1,0:T(8,128)}, u32[]{:S(2)}) %copy-start.12) | copy-done | bytes 73752
  22.4 0.8 prep.1
  23.2 0.0 collective-permute-done.far_ref
  23.2 5.9 %brick.1 = (bf16[4,512]{1,0:T(4,128)(2,1)}, bf16[14,64,128]{2,1,0:T(8,128)(2,1)S(1)}) custom-call(s32[1]{0:T(128)} %bitcast.place_ref, bf16[8,5,128]{2,1,0:T(8,128)(2,1)S(1)} %all_to_all.20.near_ref, bf16[8,5,128]{2,1,0:T(8,128)(2,1)S(1)} %collective-permute-done.far_ref, bf16[384,128]{1,0:T(8,128)(2,1)S(1)} %get-tuple-element.29.even_ref, ...), custom_call_target="tpu_custom_call" | custom-call | tf_op jit(solution)/shard_map/brick/pallas_call | solution.py:386
  29.1 10.4 %all_to_all.21 = bf16[16,56,128]{2,1,0:T(8,128)(2,1)S(1)} all-to-all(bf16[16,56,128]{2,1,0:T(8,128)(2,1)S(1)} %bitcast.16), channel_id=1, replica_groups=mesh['z'=8,'yhi'=2,'ymid'=2,'ylo'=2,'core'=2,'x'=4] {'ylo','core','x'}, dimensions={0} | all-to-all | bytes 458752 | tf_op jit(solution)/shard_map/all_to_all | solution.py:464
  39.5 0.1 broadcast_in_dim.28
  39.6 30.7 %all_to_all.22 = bf16[32,56,128]{2,1,0:T(8,128)(2,1)S(1)} all-to-all(bf16[32,56,128]{2,1,0:T(8,128)(2,1)S(1)} %broadcast_in_dim.28), channel_id=1, replica_groups=mesh['z'=8,'yhi'=2,'ymid'=2,'ylo'=2,'core'=2,'x'=4] {'z','yhi','ymid'}, dimensions={0} | all-to-all | bytes 917504 | tf_op jit(solution)/shard_map/all_to_all | solution.py:439
  70.3 0.1 reduce_sum.25
  70.4 12.7 %all_to_all.23 = bf16[16,56,128]{2,1,0:T(8,128)(2,1)S(1)} all-to-all(bf16[16,56,128]{2,1,0:T(8,128)(2,1)S(1)} %broadcast_in_dim.29), channel_id=1, replica_groups=mesh['z'=8,'yhi'=2,'ymid'=2,'ylo'=2,'core'=2,'x'=4] {'ylo','core','x'}, dimensions={0} | all-to-all | bytes 458752 | tf_op jit(solution)/shard_map/all_to_all | solution.py:439
  83.2 0.9 %unpack.1 = (f32[27,64]{1,0:T(8,128)}, f32[1,64]{1,0:T(1,128)}, f32[64,1728]{1,0:T(8,128)}, f32[1,64]{1,0:T(1,128)}, f32[4,64]{1,0:T(4,128)}, /*index=5*/f32[1,4]{1,0:T(1,128)}) custom-call(bf16[14,64,128]{2,1,0:T(8,128)(2,1)S(1)} %bitcast.15), custom_call_target="tpu_custom_call" | custom-call | tf_op jit(solution)/shard_map/unpack/pallas_call | solution.py:409
  (2 shorter events, 0.1 us)
Async XLA Ops:
  1.3 0.7 copy-start
  1.3 0.7 copy-start.1
  2.1 15.1 %copy-start.4 = (bf16[1,1,4,512]{3,2,1,0:T(4,128)(2,1)S(1)}, bf16[1,1,4,512]{3,2,1,0:T(4,128)(2,1)}, u32[]{:S(2)}) copy-start(bf16[1,1,4,512]{3,2,1,0:T(4,128)(2,1)} %param.23) | copy-start | bytes 12292
  2.1 15.1 %copy-start.6 = (f32[64]{0:T(128)S(1)}, f32[64]{0:T(128)}, u32[]{:S(2)}) copy-start(f32[64]{0:T(128)} %param.18) | copy-start | bytes 772
  2.1 15.1 %copy-start.7 = (f32[64]{0:T(128)S(1)}, f32[64]{0:T(128)}, u32[]{:S(2)}) copy-start(f32[64]{0:T(128)} %param.20) | copy-start | bytes 772
  2.1 15.1 %copy-start.8 = (f32[4]{0:T(128)S(1)}, f32[4]{0:T(128)}, u32[]{:S(2)}) copy-start(f32[4]{0:T(128)} %param.22) | copy-start | bytes 52
  16.4 0.8 %copy-start.3 = (bf16[64,27]{0,1:T(8,128)(2,1)S(1)}, bf16[64,27]{0,1:T(8,128)(2,1)}, u32[]{:S(2)}) copy-start(bf16[64,27]{0,1:T(8,128)(2,1)} %param.17) | copy-start | bytes 10372
  16.4 6.8 %collective-permute-start = (bf16[8,5,128]{2,1,0:T(8,128)(2,1)S(1)}, bf16[8,5,128]{2,1,0:T(8,128)(2,1)S(1)}, u32[]{:S(2)}, u32[]{:S(2)}) collective-permute-start(bf16[8,5,128]{2,1,0:T(8,128)(2,1)S(1)} %all_to_all.20.near_ref), channel_id=1, source_target_pairs={{16,32},{32,16},{20,36},{36,20},{24,40},{40,24},{28,44},{44,28},{4... | collective-permute-start | bytes 30728 | tf_op jit(solution)/shard_map/ppermute | solution.py:461
  17.2 0.7 copy-start.5
  17.9 0.9 %copy-start.2 = (bf16[64,1728]{1,0:T(8,128)(2,1)S(1)}, bf16[64,1728]{1,0:T(8,128)(2,1)}, u32[]{:S(2)}) copy-start(bf16[64,1728]{1,0:T(8,128)(2,1)} %w2_ref.1) | copy-start | bytes 663556
  18.9 0.9 %copy-start.9 = (bf16[128,512]{1,0:T(8,128)(2,1)S(1)}, bf16[128,512]{1,0:T(8,128)(2,1)}, u32[]{:S(2)}) copy-start(bf16[128,512]{1,0:T(8,128)(2,1)} %constant.32.clone.spread_ref) | copy-start | bytes 393220
  19.8 0.9 %copy-start.10 = (bf16[384,128]{1,0:T(8,128)(2,1)S(1)}, bf16[384,128]{1,0:T(8,128)(2,1)}, u32[]{:S(2)}) copy-start(bf16[384,128]{1,0:T(8,128)(2,1)} %constant.31.clone.odd_ref) | copy-start | bytes 294916
  20.7 0.9 %copy-start.11 = (bf16[384,128]{1,0:T(8,128)(2,1)S(1)}, bf16[384,128]{1,0:T(8,128)(2,1)}, u32[]{:S(2)}) copy-start(bf16[384,128]{1,0:T(8,128)(2,1)} %constant.30.clone.even_ref) | copy-start | bytes 294916
  21.5 0.9 %copy-start.12 = (f32[3,48,128]{2,1,0:T(8,128)S(1)}, f32[3,48,128]{2,1,0:T(8,128)}, u32[]{:S(2)}) copy-start(f32[3,48,128]{2,1,0:T(8,128)} %constant.33.clone.keep_ref) | copy-start | bytes 221188

commit v5 on v4

--- a/solution.py
+++ b/solution.py
@@ -1,6 +1,5 @@
 import jax
 import jax.numpy as jnp
-import numpy as np
 from jax import lax
 from jax.experimental import pallas as pl
 from jax.experimental.pallas import tpu as pltpu
@@ -22,40 +21,44 @@
     return -1 if place < 2 else (1 if place > 9 else 0)
 
 
-def tables():
-    even = np.zeros((384, 128), np.float32)
-    odd = np.zeros((384, 128), np.float32)
-    for step in (-1, 0, 1):
-        for y in range(EDGE):
-            for z in range(EDGE):
-                place = z + 2 + 8 * step
-                if 0 <= place < ROW:
-                    lane = y * ROW + place
-                    even[(step + 1) * 128 + y * 8 + z, lane] = 1
-                    odd[(step + 1) * 128 + 64 + y * 8 + z, lane] = 1
-    spread = np.zeros((128, 512), np.float32)
-    for y in range(EDGE):
-        for place in range(1, ROW - 1):
-            lane = y * ROW + place
-            dc = region_of(place)
-            for shift in (-1, 0, 1):
-                ec = region_of(place + shift) - dc
-                for ea in (-1, 0, 1):
-                    spread[16 * (dc + 1) + 3 * (ea + 1) + ec + 1, (shift + 1) * 128 + lane] = 1
-            for da in (-1, 0, 1):
-                spread[3 * (da + 1) + dc + 1, 384 + lane] = 1
-    keep = np.zeros((3, 48, 128), np.float32)
+def wide_iota(shape, axis):
+    return lax.broadcasted_iota(jnp.int32, shape, axis)
+
+
+def region_at(place):
+    return jnp.where(place < 2, -1, jnp.where(place > 9, 1, 0))
+
+
+def cell_places():
+    shape = (384, 128)
+    row, lane = wide_iota(shape, 0), wide_iota(shape, 1)
+    cell = row & 127
+    place = (cell & 7) + 8 * (row >> 7) - 6
+    target = 12 * ((cell >> 3) & 7) + place
+    hit = (place >= 0) & (place < ROW) & (lane == target)
+    even = jnp.where(hit & (cell < 64), 1.0, 0.0).astype(jnp.bfloat16)
+    odd = jnp.where(hit & (cell >= 64), 1.0, 0.0).astype(jnp.bfloat16)
+    return even, odd
+
+
+def flag_places():
+    shape = (128, 128)
+    row, lane = wide_iota(shape, 0), wide_iota(shape, 1)
+    line = (lane * 43) >> 9
+    place = lane - 12 * line
+    inside = (line < 8) & (place > 0) & (place < ROW - 1)
+    dc = region_at(place)
+    slot = row & 15
+    third = (slot * 11) >> 5
+    ec = slot - 3 * third - 1
+    mine = inside & ((row >> 4) - 1 == dc) & (slot < 9)
+    tables = []
     for shift in (-1, 0, 1):
-        for cell in range(10):
-            da = region_of(cell + 1)
-            ea = region_of(cell + 1 + shift) - da
-            for dc in (-1, 0, 1):
-                first = 16 * (dc + 1) + 3 * (ea + 1)
-                keep[dc + 1, 10 * (shift + 1) + cell, first : first + 3] = 1
-    for cell in range(10):
-        da = region_of(cell + 1)
-        keep[0, 30 + cell, 3 * (da + 1) : 3 * (da + 1) + 3] = 1
-    return even, odd, spread, keep
+        hit = mine & (ec == region_at(place + shift) - dc)
+        tables.append(jnp.where(hit, 1.0, 0.0).astype(jnp.bfloat16))
+    hit = inside & (row < 9) & (ec == dc)
+    tables.append(jnp.where(hit, 1.0, 0.0).astype(jnp.bfloat16))
+    return tables
 
 
 def gelu_parts(v):
@@ -81,7 +84,7 @@
 
 
 def paired(ref, first, count):
-    rows = count * GROUP
+    rows = count * ref.shape[1]
     return jnp.concatenate(
         [
             ref[first : first + count].reshape(rows, 128),
@@ -103,14 +106,9 @@
     b2_ref,
     hw_ref,
     hb_ref,
-    even_ref,
-    odd_ref,
-    spread_ref,
-    keep_ref,
     even_out,
     odd_out,
     spread_out_ref,
-    keep_out,
     w1_out,
     w2_out,
     wb_out,
@@ -124,11 +122,11 @@
 ):
     bf16 = jnp.bfloat16
     f32 = jnp.float32
-    even_out[...] = even_ref[...]
-    odd_out[...] = odd_ref[...]
-    spread_out_ref[...] = spread_ref[...]
-    keep_out[...] = keep_ref[...]
-    w2_out[...] = w2_ref[...]
+    even, odd = cell_places()
+    even_out[...] = even
+    odd_out[...] = odd
+    for index, table in enumerate(flag_places()):
+        spread_out_ref[:, 128 * index : 128 * index + 128] = table
     hw = hw_ref[...]
     hw_out[...] = hw
     rows = jnp.concatenate([b1_ref[...], b2_ref[...], jnp.zeros((6, C), f32)], axis=0)
@@ -142,13 +140,16 @@
     w1_out[...] = w1.astype(bf16)
     w2f = w2_ref[...].astype(f32)
     for pair in range(14):
-        wide = w2f[:, 128 * pair : min(128 * pair + 128, ACROSS)].T
+        block = w2f[:, 128 * pair : min(128 * pair + 128, ACROSS)]
+        wide = block.T
         for half in range(wide.shape[0] // 64):
             tap = 2 * pair + half
+            row, column = 64 * (tap % 9), 64 * (tap // 9)
+            w2_out[row : row + 64, column : column + 64] = block[:, 64 * half : 64 * half + 64].astype(bf16)
             at = 64 * ((2 - tap // 9) * 9 + tap % 9)
             wb_out[:, at : at + 64] = wide[64 * half : 64 * half + 64].astype(bf16)
-    own = even_ref[128:192]
-    scale = jnp.where(tissue_ref[0, 0] > 0, 1.0 / 512.0, 0.0)
+    own = even[128:192]
+    scale = jnp.where(tissue_ref[...] > 0, 1.0 / 512.0, 0.0)
     cot = (cot_ref[...].astype(f32) * scale).astype(bf16)
     for x in range(8):
         dp = dot(cot[:, 64 * x : 64 * x + 64], own).astype(bf16)
@@ -165,7 +166,6 @@
     even_ref,
     odd_ref,
     spread_ref,
-    keep_ref,
     w1_ref,
     w2_ref,
     wb_ref,
@@ -182,7 +182,7 @@
     flag_ref,
     s1_ref,
     slope_ref,
-    v_ref,
+    h_ref,
     g_ref,
 ):
     position = place_ref[0]
@@ -203,22 +203,23 @@
     cells_even = dot(lines, even_ref[...])
     cells_odd = dot(lines, odd_ref[...])
     flags = {w: tiles[w][4:5] for w in range(-3, 4)}
-    for shift in (-1, 0, 1):
+    lane = wide_iota((1, 128), 1)
+    group, third = lane >> 4, ((lane & 15) * 11) >> 5
+    flag_ref[40:48] = jnp.zeros((8, 128), f32)
+    for da in (-1, 0, 1):
+        merged = sum(jnp.where(group == dc + 1, flags[2 * da + dc], 0.0) for dc in (-1, 0, 1))
+        listed = {ea: jnp.where(third == ea + 1, merged, 0.0) for ea in (-1, 0, 1)}
+        known = jnp.where((group == 0) & (third == da + 1), flags[0], 0.0)
         for cell in range(10):
-            da = region_of(cell + 1)
-            row = 10 * (shift + 1) + cell
-            flag_ref[row : row + 1] = sum(
-                flags[2 * da + dc] * keep_ref[dc + 1, row : row + 1] for dc in (-1, 0, 1)
-            )
-    for cell in range(10):
-        flag_ref[30 + cell : 31 + cell] = flags[0] * keep_ref[0, 30 + cell : 31 + cell]
-    flag_ref[40:48] = jnp.zeros((8, 128), f32)
+            if region_of(cell + 1) == da:
+                for shift in (-1, 0, 1):
+                    row = 10 * (shift + 1) + cell
+                    flag_ref[row : row + 1] = listed[region_of(cell + 1 + shift) - da]
+                flag_ref[30 + cell : 31 + cell] = known
     masks = dot(flag_ref[...].astype(bf16), spread_ref[...])
     valid = masks[30:40, 384:512]
     for cell in range(10):
-        s1_ref[cell, 24:32] = jnp.where(
-            lax.broadcasted_iota(jnp.int32, (8, 128), 0) == 3, 1.0, 0.0
-        )
+        s1_ref[cell, 24:32] = jnp.where(wide_iota((8, 128), 0) == 3, 1.0, 0.0)
     for b, c in SHIFTS:
         amount = 12 * b + c
         moved = [turn(cells_even, amount), turn(cells_odd, amount)]
@@ -238,9 +239,7 @@
         value, slope = gelu_parts(dot(w1, taps) + b1)
         ok = valid[cell : cell + 1]
         slope_ref[cell] = slope * ok
-        h1 = (value * ok).astype(bf16).astype(f32)
-        for index, (b, c) in enumerate(SHIFTS):
-            v_ref[cell, 64 * index : 64 * index + 64] = turn(h1, 12 * b + c).astype(bf16)
+        h_ref[cell] = (value * ok).astype(bf16)
     active = valid[2:3, 2:3]
     w2 = w2_ref[...]
     b2 = b2_ref[...]
@@ -248,10 +247,16 @@
     hb = hb_ref[...]
     own = even_ref[128:192]
     dz2, h2_all = [], []
+    g_ref[0] = jnp.zeros((GROUP, 128), bf16)
+    g_ref[9] = jnp.zeros((GROUP, 128), bf16)
     for x in range(0, 8, 2):
-        both_z2 = dot(w2, paired(v_ref, x, 3))
+        both = dot(w2, paired(h_ref, x, 3))
         for half in range(2):
-            value, slope = gelu_parts(both_z2[:, 128 * half : 128 * half + 128] + b2)
+            z2 = b2
+            for index, (b, c) in enumerate(SHIFTS):
+                part = both[64 * index : 64 * index + 64, 128 * half : 128 * half + 128]
+                z2 = z2 + turn(part, 12 * b + c)
+            value, slope = gelu_parts(z2)
             h2 = (value * active).astype(bf16)
             pred = ((dot(hw, h2) + hb) * active).astype(bf16)
             at = 64 * (x + half)
@@ -264,28 +269,25 @@
                 g_ref[x + half + 1, 64 * index : 64 * index + 64] = turn(
                     d2, -(12 * b + c)
                 ).astype(bf16)
-    grad_w2 = None
-    grad_b2 = None
-    ones = jnp.ones((8, 256), bf16)
-    for x in range(0, 8, 2):
-        left = jnp.concatenate(dz2[x : x + 2], axis=1)
-        piece = dot_t(left, paired(v_ref, x, 3))
-        grad_w2 = piece if grad_w2 is None else grad_w2 + piece
-        piece = dot_t(ones, left)
-        grad_b2 = piece if grad_b2 is None else grad_b2 + piece
-    for block in range(13):
-        part_ref[block] = grad_w2[:, 128 * block : 128 * block + 128].astype(bf16)
+    grad_w2 = dot_t(
+        jnp.concatenate([g_ref[x + 1] for x in range(8)], axis=1),
+        jnp.concatenate([h_ref[x : x + 3].reshape(3 * C, 128) for x in range(8)], axis=1),
+    )
+    for index in range(9):
+        part_ref[index] = grad_w2[64 * index : 64 * index + 64, 0:128].astype(bf16)
+    last = [grad_w2[64 * index : 64 * index + 64, 128:192] for index in range(9)]
+    for pair in range(4):
+        part_ref[9 + pair] = jnp.concatenate(last[2 * pair : 2 * pair + 2], axis=1).astype(bf16)
+    grad_b2 = dot_t(jnp.ones((8, 1024), bf16), jnp.concatenate(dz2, axis=1))
     grad_wh = dot_t(dp_ref[...], jnp.concatenate(h2_all, axis=1))
     grad_w1 = None
-    g_ref[0] = jnp.zeros((GROUP, 128), bf16)
-    g_ref[9] = jnp.zeros((GROUP, 128), bf16)
     for cell in range(0, 10, 2):
         skip = 1 if cell == 0 else 0
         count = 2 if cell in (0, 8) else 3
         back = wb_ref[:, skip * GROUP : (skip + count) * GROUP]
-        both_dh1 = dot(back, paired(g_ref, cell - 1 + skip, count))
+        both = dot(back, paired(g_ref, cell - 1 + skip, count))
         for half in range(2):
-            dz1 = both_dh1[:, 128 * half : 128 * half + 128] * slope_ref[cell + half]
+            dz1 = both[:, 128 * half : 128 * half + 128] * slope_ref[cell + half]
             head = dz1.astype(bf16)
             tail = (dz1 - head.astype(f32)).astype(bf16)
             taps = s1_ref[cell + half].astype(bf16)
@@ -294,7 +296,7 @@
     small = jnp.concatenate(
         [grad_w1[0:28], grad_wh, grad_b2[0:1], gbh_ref[0:1], jnp.zeros((30, C), f32)], axis=0
     )
-    part_ref[13] = jnp.concatenate([grad_w2[:, 1664:1728], small], axis=1).astype(bf16)
+    part_ref[13] = jnp.concatenate([last[8], small], axis=1).astype(bf16)
 
 
 def pack_kernel(list_ref, tissue_ref, cells_ref, out_ref):
@@ -318,10 +320,20 @@
 
 def unpack_kernel(all_ref, w1_ref, b1_ref, w2_ref, b2_ref, hw_ref, hb_ref):
     f32 = jnp.float32
-    for block in range(13):
-        w2_ref[:, 128 * block : 128 * block + 128] = all_ref[block].astype(f32)
-    mixed = all_ref[13].astype(f32)
-    w2_ref[:, 1664:1728] = mixed[:, 0:64]
+    blocks = [all_ref[block].astype(f32) for block in range(BLOCKS)]
+
+    def of_tap(tap):
+        offset, index = tap // 9, tap % 9
+        if offset < 2:
+            return blocks[index][:, 64 * offset : 64 * offset + 64]
+        return blocks[9 + index // 2][:, 64 * (index % 2) : 64 * (index % 2) + 64]
+
+    for pair in range(13):
+        w2_ref[:, 128 * pair : 128 * pair + 128] = jnp.concatenate(
+            [of_tap(2 * pair), of_tap(2 * pair + 1)], axis=1
+        )
+    w2_ref[:, 1664:1728] = of_tap(26)
+    mixed = blocks[13]
     rows = mixed[:, 64:128]
     w1_ref[...] = rows[0:27]
     b1_ref[...] = rows[27:28]
@@ -338,14 +350,12 @@
 
 def prepare(tissue, cot, w1, b1, w2, b2, hw, hb):
     bf16, f32 = jnp.bfloat16, jnp.float32
-    even, odd, spread, keep = tables()
     shapes = [
         ((384, 128), bf16),
         ((384, 128), bf16),
         ((128, 512), bf16),
-        ((3, 48, 128), f32),
         ((C, 32), bf16),
-        ((C, ACROSS), bf16),
+        ((GROUP, 3 * C), bf16),
         ((C, ACROSS), bf16),
         ((OUT_CH, C), bf16),
         ((C, 128), f32),
@@ -358,7 +368,7 @@
     return pl.pallas_call(
         prep_kernel,
         out_shape=tuple(jax.ShapeDtypeStruct(shape, kind) for shape, kind in shapes),
-        in_specs=[SMEM] + [VMEM] * 11,
+        in_specs=[VMEM] * 8,
         out_specs=(VMEM,) * len(shapes),
         compiler_params=pltpu.CompilerParams(vmem_limit_bytes=BIG),
         cost_estimate=pl.CostEstimate(
@@ -374,10 +384,6 @@
         b2,
         hw,
         hb,
-        even.astype(bf16),
-        odd.astype(bf16),
-        spread.astype(bf16),
-        keep,
     )
 
 
@@ -396,7 +402,7 @@
             pltpu.VMEM((48, 128), f32),
             pltpu.VMEM((10, 32, 128), f32),
             pltpu.VMEM((10, C, 128), f32),
-            pltpu.VMEM((10, GROUP, 128), bf16),
+            pltpu.VMEM((10, C, 128), bf16),
             pltpu.VMEM((10, GROUP, 128), bf16),
         ],
         compiler_params=pltpu.CompilerParams(vmem_limit_bytes=BIG),

time: 84.5 us -> 81.2 us (0.961)
  local copies, waits for them, and re-layouts: 5.92 us -> 2.35 us
  blocking collectives: 68.2 us -> 69.9 us
  Pallas kernels: 7.64 us -> 6.28 us
    unnamed x26 -> x18, local copies, waits for them, and re-layouts: 5.83 us -> 2.25 us
    all_to_all x2, blocking collectives: 43.5 us -> 45.2 us  [spread_out(): return lax.all_to_all(copies, axes, 0, 0, tiled=True)]
    pallas_call x1, Pallas kernels: 5.87 us -> 4.29 us  [all_brick_work(): pl.pallas_call(brick_kernel, out_shape=(jax.ShapeDtypeStruct((OUT_CH, 512...]
where the time goes in v5:
time: 81.2 us; the launch traced here: 80.8 us
  blocking collectives  69.9 us (86%)
  Pallas kernels  6.28 us (8%)
  local copies, waits for them, and re-layouts  2.35 us (3%)
  between operations  1.4 us (2%)
    all_to_all x2, blocking collectives, spread_out(): return lax.all_to_all(copies, axes, 0, 0, tiled=True)  45.2 us
    all_to_all x1, blocking collectives, shards(): near = lax.all_to_all(mine, NEAR, 0, 0, tiled=True)  14.3 us
    all_to_all x1, blocking collectives, shards(): lax.all_to_all(parts.reshape(SHARES, ROWS, 128), FIRST, 0, 0, tiled=True)  10.5 us
    pallas_call x1, Pallas kernels, all_brick_work(): pl.pallas_call(brick_kernel, out_shape=(jax.ShapeDtypeStruct((OUT_CH, 512...  4.29 us
    unnamed x18, local copies, waits for them, and re-layouts  2.25 us
  transfers between devices with their start and end apart: 1, of which 0 were waited for; matrix products, arithmetic and copies ran while one was open for 0% of the time, Pallas kernels for 1%

profile of v5, /device:TPU:1, one launch (start us, length us, event | category | flops | bytes accessed | tf_op | source)
XLA Modules:
  0.0 80.8 jit_solution(9019692383643511386)
XLA Ops:
  1.3 0.0 copy-start
  1.3 0.0 copy-start.1
  1.3 0.7 copy-done
  2.0 0.0 copy-done.1
  2.0 0.2 pack.1
  2.1 0.0 copy-start.4
  2.1 0.0 copy-start.6
  2.1 0.0 copy-start.7
  2.1 0.0 copy-start.8
  2.1 14.3 %all_to_all.20.near_ref = bf16[8,5,128]{2,1,0:T(8,128)(2,1)S(1)} all-to-all(bf16[8,5,128]{2,1,0:T(8,128)(2,1)S(1)} %pack.1), channel_id=1, replica_groups=mesh['z'=8,'yhi'=2,'ymid'=2,'ylo'=2,'core'=2,'x'=4] {'ymid','ylo','core'}, dimensions={0} | all-to-all | bytes 20480 | tf_op jit(solution)/shard_map/all_to_all | solution.py:466
  16.4 0.0 copy-start.3
  16.4 0.8 collective-permute-start
  17.2 0.0 copy-start.5
  17.2 0.0 copy-done.4
  17.3 0.0 copy-done.6
  17.3 0.0 copy-done.7
  17.3 0.0 copy-done.8
  17.3 0.0 copy-done.3
  17.3 0.6 copy-done.5
  17.9 0.0 copy-start.2
  17.9 0.9 %copy-done.2 = bf16[64,1728]{1,0:T(8,128)(2,1)S(1)} copy-done((bf16[64,1728]{1,0:T(8,128)(2,1)S(1)}, bf16[64,1728]{1,0:T(8,128)(2,1)}, u32[]{:S(2)}) %copy-start.2) | copy-done | bytes 221208
  18.9 1.0 %prep.1 = (bf16[384,128]{1,0:T(8,128)(2,1)S(1)}, bf16[384,128]{1,0:T(8,128)(2,1)S(1)}, bf16[128,512]{1,0:T(8,128)(2,1)S(1)}, bf16[64,32]{1,0:T(8,128)(2,1)S(1)},...) custom-call(s32[1,1]{1,0:T(1,128)S(6)} %copy.17.tissue_ref, ...), custom_call_target="tpu_custom_call" | custom-call | flops 4000000000 | bytes 4000000 | tf_op jit(solution)/shard_map/prep/pallas_call | solution.py:368
  19.8 0.0 collective-permute-done.far_ref
  19.8 4.3 %brick.1 = (bf16[4,512]{1,0:T(4,128)(2,1)}, bf16[14,64,128]{2,1,0:T(8,128)(2,1)S(1)}) custom-call(s32[1]{0:T(128)} %bitcast.place_ref, bf16[8,5,128]{2,1,0:T(8,128)(2,1)S(1)} %all_to_all.20.near_ref, bf16[8,5,128]{2,1,0:T(8,128)(2,1)S(1)} %collective-permute-done.far_ref, bf16[384,128]{1,0:T(8,128)(2,1)S(1)} %get-tuple-element.28.even_ref, ...), custom_call_target="tpu_custom_call" | custom-call | tf_op jit(solution)/shard_map/brick/pallas_call | solution.py:392
  24.1 10.5 %all_to_all.21 = bf16[16,56,128]{2,1,0:T(8,128)(2,1)S(1)} all-to-all(bf16[16,56,128]{2,1,0:T(8,128)(2,1)S(1)} %bitcast.16), channel_id=1, replica_groups=mesh['z'=8,'yhi'=2,'ymid'=2,'ylo'=2,'core'=2,'x'=4] {'ylo','core','x'}, dimensions={0} | all-to-all | bytes 458752 | tf_op jit(solution)/shard_map/all_to_all | solution.py:470
  34.6 0.1 broadcast_in_dim.28
  34.7 32.4 %all_to_all.22 = bf16[32,56,128]{2,1,0:T(8,128)(2,1)S(1)} all-to-all(bf16[32,56,128]{2,1,0:T(8,128)(2,1)S(1)} %broadcast_in_dim.28), channel_id=1, replica_groups=mesh['z'=8,'yhi'=2,'ymid'=2,'ylo'=2,'core'=2,'x'=4] {'z','yhi','ymid'}, dimensions={0} | all-to-all | bytes 917504 | tf_op jit(solution)/shard_map/all_to_all | solution.py:445
  67.1 0.1 reduce_sum.25
  67.2 12.7 %all_to_all.23 = bf16[16,56,128]{2,1,0:T(8,128)(2,1)S(1)} all-to-all(bf16[16,56,128]{2,1,0:T(8,128)(2,1)S(1)} %broadcast_in_dim.29), channel_id=1, replica_groups=mesh['z'=8,'yhi'=2,'ymid'=2,'ylo'=2,'core'=2,'x'=4] {'ylo','core','x'}, dimensions={0} | all-to-all | bytes 458752 | tf_op jit(solution)/shard_map/all_to_all | solution.py:445
  80.0 0.9 %unpack.1 = (f32[27,64]{1,0:T(8,128)}, f32[1,64]{1,0:T(1,128)}, f32[64,1728]{1,0:T(8,128)}, f32[1,64]{1,0:T(1,128)}, f32[4,64]{1,0:T(4,128)}, /*index=5*/f32[1,4]{1,0:T(1,128)}) custom-call(bf16[14,64,128]{2,1,0:T(8,128)(2,1)S(1)} %bitcast.15), custom_call_target="tpu_custom_call" | custom-call | tf_op jit(solution)/shard_map/unpack/pallas_call | solution.py:415
  (2 shorter events, 0.1 us)
Async XLA Ops:
  1.3 0.7 copy-start
  1.3 0.7 copy-start.1
  2.1 15.1 %copy-start.4 = (bf16[1,1,4,512]{3,2,1,0:T(4,128)(2,1)S(1)}, bf16[1,1,4,512]{3,2,1,0:T(4,128)(2,1)}, u32[]{:S(2)}) copy-start(bf16[1,1,4,512]{3,2,1,0:T(4,128)(2,1)} %param.19) | copy-start | bytes 12292
  2.1 15.1 %copy-start.6 = (f32[64]{0:T(128)S(1)}, f32[64]{0:T(128)}, u32[]{:S(2)}) copy-start(f32[64]{0:T(128)} %param.14) | copy-start | bytes 772
  2.1 15.1 %copy-start.7 = (f32[64]{0:T(128)S(1)}, f32[64]{0:T(128)}, u32[]{:S(2)}) copy-start(f32[64]{0:T(128)} %param.16) | copy-start | bytes 772
  2.1 15.1 %copy-start.8 = (f32[4]{0:T(128)S(1)}, f32[4]{0:T(128)}, u32[]{:S(2)}) copy-start(f32[4]{0:T(128)} %param.18) | copy-start | bytes 52
  16.4 0.8 %copy-start.3 = (bf16[64,27]{0,1:T(8,128)(2,1)S(1)}, bf16[64,27]{0,1:T(8,128)(2,1)}, u32[]{:S(2)}) copy-start(bf16[64,27]{0,1:T(8,128)(2,1)} %param.13) | copy-start | bytes 10372
  16.4 3.4 %collective-permute-start = (bf16[8,5,128]{2,1,0:T(8,128)(2,1)S(1)}, bf16[8,5,128]{2,1,0:T(8,128)(2,1)S(1)}, u32[]{:S(2)}, u32[]{:S(2)}) collective-permute-start(bf16[8,5,128]{2,1,0:T(8,128)(2,1)S(1)} %all_to_all.20.near_ref), channel_id=1, source_target_pairs={{16,32},{32,16},{20,36},{36,20},{24,40},{40,24},{28,44},{44,28},{4... | collective-permute-start | bytes 30728 | tf_op jit(solution)/shard_map/ppermute | solution.py:467
  17.2 0.7 copy-start.5
  17.9 0.9 %copy-start.2 = (bf16[64,1728]{1,0:T(8,128)(2,1)S(1)}, bf16[64,1728]{1,0:T(8,128)(2,1)}, u32[]{:S(2)}) copy-start(bf16[64,1728]{1,0:T(8,128)(2,1)} %w2_ref.1) | copy-start | bytes 663556

commit v6 on v5

--- a/solution.py
+++ b/solution.py
@@ -146,8 +146,8 @@
             tap = 2 * pair + half
             row, column = 64 * (tap % 9), 64 * (tap // 9)
             w2_out[row : row + 64, column : column + 64] = block[:, 64 * half : 64 * half + 64].astype(bf16)
-            at = 64 * ((2 - tap // 9) * 9 + tap % 9)
-            wb_out[:, at : at + 64] = wide[64 * half : 64 * half + 64].astype(bf16)
+            column = 64 * (2 - tap // 9)
+            wb_out[row : row + 64, column : column + 64] = wide[64 * half : 64 * half + 64].astype(bf16)
     own = even[128:192]
     scale = jnp.where(tissue_ref[...] > 0, 1.0 / 512.0, 0.0)
     cot = (cot_ref[...].astype(f32) * scale).astype(bf16)
@@ -183,6 +183,7 @@
     s1_ref,
     slope_ref,
     h_ref,
+    d_ref,
     g_ref,
 ):
     position = place_ref[0]
@@ -244,11 +245,11 @@
     w2 = w2_ref[...]
     b2 = b2_ref[...]
     hw = hw_ref[...]
-    hb = hb_ref[...]
+    hb = hb_ref[:, 0:1]
     own = even_ref[128:192]
     dz2, h2_all = [], []
-    g_ref[0] = jnp.zeros((GROUP, 128), bf16)
-    g_ref[9] = jnp.zeros((GROUP, 128), bf16)
+    d_ref[0] = jnp.zeros((C, 128), bf16)
+    d_ref[9] = jnp.zeros((C, 128), bf16)
     for x in range(0, 8, 2):
         both = dot(w2, paired(h_ref, x, 3))
         for half in range(2):
@@ -257,20 +258,23 @@
                 part = both[64 * index : 64 * index + 64, 128 * half : 128 * half + 128]
                 z2 = z2 + turn(part, 12 * b + c)
             value, slope = gelu_parts(z2)
-            h2 = (value * active).astype(bf16)
-            pred = ((dot(hw, h2) + hb) * active).astype(bf16)
-            at = 64 * (x + half)
-            pred_ref[:, at : at + 64] = dot_t(pred, own).astype(bf16)
+            h2_all.append((value * active).astype(bf16))
             d2 = (dh2_ref[x + half] * slope).astype(bf16)
             dz2.append(d2)
-            h2_all.append(h2)
+            d_ref[x + half + 1] = d2
             d2 = d2.astype(f32)
             for index, (b, c) in enumerate(SHIFTS):
-                g_ref[x + half + 1, 64 * index : 64 * index + 64] = turn(
+                g_ref[x + half, 64 * index : 64 * index + 64] = turn(
                     d2, -(12 * b + c)
                 ).astype(bf16)
+    h2 = jnp.concatenate(h2_all, axis=1)
+    pred = (dot(hw, h2) + hb) * active
+    pred = jnp.concatenate([pred[:, 128 * x : 128 * x + 128] for x in range(8)], axis=0)
+    pred = dot_t(pred.astype(bf16), own).astype(bf16)
+    for x in range(8):
+        pred_ref[:, 64 * x : 64 * x + 64] = pred[OUT_CH * x : OUT_CH * x + OUT_CH]
     grad_w2 = dot_t(
-        jnp.concatenate([g_ref[x + 1] for x in range(8)], axis=1),
+        jnp.concatenate([g_ref[x] for x in range(8)], axis=1),
         jnp.concatenate([h_ref[x : x + 3].reshape(3 * C, 128) for x in range(8)], axis=1),
     )
     for index in range(9):
@@ -279,20 +283,28 @@
     for pair in range(4):
         part_ref[9 + pair] = jnp.concatenate(last[2 * pair : 2 * pair + 2], axis=1).astype(bf16)
     grad_b2 = dot_t(jnp.ones((8, 1024), bf16), jnp.concatenate(dz2, axis=1))
-    grad_wh = dot_t(dp_ref[...], jnp.concatenate(h2_all, axis=1))
-    grad_w1 = None
+    grad_wh = dot_t(dp_ref[...], h2)
+    wb = wb_ref[...]
+    heads, tails = [], []
     for cell in range(0, 10, 2):
         skip = 1 if cell == 0 else 0
         count = 2 if cell in (0, 8) else 3
-        back = wb_ref[:, skip * GROUP : (skip + count) * GROUP]
-        both = dot(back, paired(g_ref, cell - 1 + skip, count))
+        back = wb[:, skip * C : (skip + count) * C]
+        both = dot(back, paired(d_ref, cell - 1 + skip, count))
         for half in range(2):
-            dz1 = both[:, 128 * half : 128 * half + 128] * slope_ref[cell + half]
+            dh1 = None
+            for index, (b, c) in enumerate(SHIFTS):
+                part = both[64 * index : 64 * index + 64, 128 * half : 128 * half + 128]
+                part = turn(part, -(12 * b + c))
+                dh1 = part if dh1 is None else dh1 + part
+            dz1 = dh1 * slope_ref[cell + half]
             head = dz1.astype(bf16)
-            tail = (dz1 - head.astype(f32)).astype(bf16)
-            taps = s1_ref[cell + half].astype(bf16)
-            piece = dot_t(taps, head) + dot_t(taps, tail)
-            grad_w1 = piece if grad_w1 is None else grad_w1 + piece
+            heads.append(head)
+            tails.append((dz1 - head.astype(f32)).astype(bf16))
+    taps = jnp.concatenate([s1_ref[cell].astype(bf16) for cell in range(10)], axis=1)
+    grad_w1 = dot_t(taps, jnp.concatenate(heads, axis=1)) + dot_t(
+        taps, jnp.concatenate(tails, axis=1)
+    )
     small = jnp.concatenate(
         [grad_w1[0:28], grad_wh, grad_b2[0:1], gbh_ref[0:1], jnp.zeros((30, C), f32)], axis=0
     )
@@ -356,7 +368,7 @@
         ((128, 512), bf16),
         ((C, 32), bf16),
         ((GROUP, 3 * C), bf16),
-        ((C, ACROSS), bf16),
+        ((GROUP, 3 * C), bf16),
         ((OUT_CH, C), bf16),
         ((C, 128), f32),
         ((C, 128), f32),
@@ -403,7 +415,8 @@
             pltpu.VMEM((10, 32, 128), f32),
             pltpu.VMEM((10, C, 128), f32),
             pltpu.VMEM((10, C, 128), bf16),
-            pltpu.VMEM((10, GROUP, 128), bf16),
+            pltpu.VMEM((10, C, 128), bf16),
+            pltpu.VMEM((8, GROUP, 128), bf16),
         ],
         compiler_params=pltpu.CompilerParams(vmem_limit_bytes=BIG),
         name="brick",
@@ -448,7 +461,7 @@
 BRICK = ("z", "yhi", "ymid", "ylo", "core")
 NEAR = ("ymid", "ylo", "core")
 FIRST = ("ylo", "core", "x")
-SECOND = ("z", "yhi", "ymid")
+SECOND = ("yhi", "ymid", "z")
 SHARES, ROWS = 16, 56
 HALF = GROUP_SIZE // 2
 PAIRS = [

time: 81.2 us -> 79.5 us (0.979)
  Pallas kernels: 6.28 us -> 5.24 us
    pallas_call x1, Pallas kernels: 4.29 us -> 3.23 us  [all_brick_work(): pl.pallas_call(brick_kernel, out_shape=(jax.ShapeDtypeStruct((OUT_CH, 512...]
where the time goes in v6:
time: 79.5 us; the launch traced here: 79 us
  blocking collectives  69.1 us (87%)
  Pallas kernels  5.24 us (7%)
  local copies, waits for them, and re-layouts  2.35 us (3%)
  between operations  1.41 us (2%)
    all_to_all x2, blocking collectives, spread_out(): return lax.all_to_all(copies, axes, 0, 0, tiled=True)  44.4 us
    all_to_all x1, blocking collectives, shards(): near = lax.all_to_all(mine, NEAR, 0, 0, tiled=True)  14.3 us
    all_to_all x1, blocking collectives, shards(): lax.all_to_all(parts.reshape(SHARES, ROWS, 128), FIRST, 0, 0, tiled=True)  10.4 us
    pallas_call x1, Pallas kernels, all_brick_work(): pl.pallas_call(brick_kernel, out_shape=(jax.ShapeDtypeStruct((OUT_CH, 512...  3.23 us
    unnamed x18, local copies, waits for them, and re-layouts  2.25 us
  transfers between devices with their start and end apart: 1, of which 0 were waited for; matrix products, arithmetic and copies ran while one was open for 0% of the time, Pallas kernels for 1%

profile of v6, /device:TPU:1, one launch (start us, length us, event | category | flops | bytes accessed | tf_op | source)
XLA Modules:
  0.0 79.0 jit_solution(10393719582896043516)
XLA Ops:
  1.3 0.0 copy-start
  1.3 0.0 copy-start.1
  1.3 0.7 copy-done
  2.0 0.0 copy-done.1
  2.0 0.2 pack.1
  2.1 0.0 copy-start.4
  2.1 0.0 copy-start.6
  2.1 0.0 copy-start.7
  2.1 0.0 copy-start.8
  2.1 14.3 %all_to_all.20.near_ref = bf16[8,5,128]{2,1,0:T(8,128)(2,1)S(1)} all-to-all(bf16[8,5,128]{2,1,0:T(8,128)(2,1)S(1)} %pack.1), channel_id=1, replica_groups=mesh['z'=8,'yhi'=2,'ymid'=2,'ylo'=2,'core'=2,'x'=4] {'ymid','ylo','core'}, dimensions={0} | all-to-all | bytes 20480 | tf_op jit(solution)/shard_map/all_to_all | solution.py:479
  16.4 0.0 copy-start.3
  16.4 0.8 collective-permute-start
  17.2 0.0 copy-start.5
  17.2 0.0 copy-done.4
  17.3 0.0 copy-done.6
  17.3 0.0 copy-done.7
  17.3 0.0 copy-done.8
  17.3 0.0 copy-done.3
  17.3 0.6 copy-done.5
  17.9 0.0 copy-start.2
  17.9 0.9 %copy-done.2 = bf16[64,1728]{1,0:T(8,128)(2,1)S(1)} copy-done((bf16[64,1728]{1,0:T(8,128)(2,1)S(1)}, bf16[64,1728]{1,0:T(8,128)(2,1)}, u32[]{:S(2)}) %copy-start.2) | copy-done | bytes 221208
  18.9 1.0 %prep.1 = (bf16[384,128]{1,0:T(8,128)(2,1)S(1)}, bf16[384,128]{1,0:T(8,128)(2,1)S(1)}, bf16[128,512]{1,0:T(8,128)(2,1)S(1)}, bf16[64,32]{1,0:T(8,128)(2,1)S(1)},...) custom-call(s32[1,1]{1,0:T(1,128)S(6)} %copy.17.tissue_ref, ...), custom_call_target="tpu_custom_call" | custom-call | flops 4000000000 | bytes 4000000 | tf_op jit(solution)/shard_map/prep/pallas_call | solution.py:380
  19.9 0.0 collective-permute-done.far_ref
  19.9 3.2 %brick.1 = (bf16[4,512]{1,0:T(4,128)(2,1)}, bf16[14,64,128]{2,1,0:T(8,128)(2,1)S(1)}) custom-call(s32[1]{0:T(128)} %bitcast.place_ref, bf16[8,5,128]{2,1,0:T(8,128)(2,1)S(1)} %all_to_all.20.near_ref, bf16[8,5,128]{2,1,0:T(8,128)(2,1)S(1)} %collective-permute-done.far_ref, bf16[384,128]{1,0:T(8,128)(2,1)S(1)} %get-tuple-element.28.even_ref, ...), custom_call_target="tpu_custom_call" | custom-call | tf_op jit(solution)/shard_map/brick/pallas_call | solution.py:404
  23.1 10.4 %all_to_all.21 = bf16[16,56,128]{2,1,0:T(8,128)(2,1)S(1)} all-to-all(bf16[16,56,128]{2,1,0:T(8,128)(2,1)S(1)} %bitcast.16), channel_id=1, replica_groups=mesh['z'=8,'yhi'=2,'ymid'=2,'ylo'=2,'core'=2,'x'=4] {'ylo','core','x'}, dimensions={0} | all-to-all | bytes 458752 | tf_op jit(solution)/shard_map/all_to_all | solution.py:483
  33.6 0.1 broadcast_in_dim.28
  33.6 32.1 %all_to_all.22 = bf16[32,56,128]{2,1,0:T(8,128)(2,1)S(1)} all-to-all(bf16[32,56,128]{2,1,0:T(8,128)(2,1)S(1)} %broadcast_in_dim.28), channel_id=1, replica_groups=mesh['z'=8,'yhi'=2,'ymid'=2,'ylo'=2,'core'=2,'x'=4] {'yhi','ymid','z'}, dimensions={0} | all-to-all | bytes 917504 | tf_op jit(solution)/shard_map/all_to_all | solution.py:458
  65.7 0.1 reduce_sum.25
  65.8 12.3 %all_to_all.23 = bf16[16,56,128]{2,1,0:T(8,128)(2,1)S(1)} all-to-all(bf16[16,56,128]{2,1,0:T(8,128)(2,1)S(1)} %broadcast_in_dim.29), channel_id=1, replica_groups=mesh['z'=8,'yhi'=2,'ymid'=2,'ylo'=2,'core'=2,'x'=4] {'ylo','core','x'}, dimensions={0} | all-to-all | bytes 458752 | tf_op jit(solution)/shard_map/all_to_all | solution.py:458
  78.2 0.9 %unpack.1 = (f32[27,64]{1,0:T(8,128)}, f32[1,64]{1,0:T(1,128)}, f32[64,1728]{1,0:T(8,128)}, f32[1,64]{1,0:T(1,128)}, f32[4,64]{1,0:T(4,128)}, /*index=5*/f32[1,4]{1,0:T(1,128)}) custom-call(bf16[14,64,128]{2,1,0:T(8,128)(2,1)S(1)} %bitcast.15), custom_call_target="tpu_custom_call" | custom-call | tf_op jit(solution)/shard_map/unpack/pallas_call | solution.py:428
  (2 shorter events, 0.1 us)
Async XLA Ops:
  1.3 0.7 copy-start
  1.3 0.7 copy-start.1
  2.1 15.1 %copy-start.4 = (bf16[1,1,4,512]{3,2,1,0:T(4,128)(2,1)S(1)}, bf16[1,1,4,512]{3,2,1,0:T(4,128)(2,1)}, u32[]{:S(2)}) copy-start(bf16[1,1,4,512]{3,2,1,0:T(4,128)(2,1)} %param.19) | copy-start | bytes 12292
  2.1 15.1 %copy-start.6 = (f32[64]{0:T(128)S(1)}, f32[64]{0:T(128)}, u32[]{:S(2)}) copy-start(f32[64]{0:T(128)} %param.14) | copy-start | bytes 772
  2.1 15.1 %copy-start.7 = (f32[64]{0:T(128)S(1)}, f32[64]{0:T(128)}, u32[]{:S(2)}) copy-start(f32[64]{0:T(128)} %param.16) | copy-start | bytes 772
  2.1 15.1 %copy-start.8 = (f32[4]{0:T(128)S(1)}, f32[4]{0:T(128)}, u32[]{:S(2)}) copy-start(f32[4]{0:T(128)} %param.18) | copy-start | bytes 52
  16.4 0.8 %copy-start.3 = (bf16[64,27]{0,1:T(8,128)(2,1)S(1)}, bf16[64,27]{0,1:T(8,128)(2,1)}, u32[]{:S(2)}) copy-start(bf16[64,27]{0,1:T(8,128)(2,1)} %param.13) | copy-start | bytes 10372
  16.4 3.4 %collective-permute-start = (bf16[8,5,128]{2,1,0:T(8,128)(2,1)S(1)}, bf16[8,5,128]{2,1,0:T(8,128)(2,1)S(1)}, u32[]{:S(2)}, u32[]{:S(2)}) collective-permute-start(bf16[8,5,128]{2,1,0:T(8,128)(2,1)S(1)} %all_to_all.20.near_ref), channel_id=1, source_target_pairs={{16,32},{32,16},{20,36},{36,20},{24,40},{40,24},{28,44},{44,28},{4... | collective-permute-start | bytes 30728 | tf_op jit(solution)/shard_map/ppermute | solution.py:480
  17.2 0.7 copy-start.5
  17.9 0.9 %copy-start.2 = (bf16[64,1728]{1,0:T(8,128)(2,1)S(1)}, bf16[64,1728]{1,0:T(8,128)(2,1)}, u32[]{:S(2)}) copy-start(bf16[64,1728]{1,0:T(8,128)(2,1)} %w2_ref.1) | copy-start | bytes 663556

commit v7 on v6

--- a/solution.py
+++ b/solution.py
@@ -11,7 +11,7 @@
 ROW = 12
 GROUP = 576
 ACROSS = 1728
-BLOCKS = 14
+BLOCKS = 16
 GROUP_SIZE = 8
 ROOT = 0.7978845608028654
 CUBIC = 0.044715
@@ -308,6 +308,8 @@
     small = jnp.concatenate(
         [grad_w1[0:28], grad_wh, grad_b2[0:1], gbh_ref[0:1], jnp.zeros((30, C), f32)], axis=0
     )
+    part_ref[14] = jnp.zeros((64, 128), bf16)
+    part_ref[15] = jnp.zeros((64, 128), bf16)
     part_ref[13] = jnp.concatenate([last[8], small], axis=1).astype(bf16)
 
 
@@ -458,11 +460,11 @@
     return lax.all_to_all(copies, axes, 0, 0, tiled=True)
 
 
-BRICK = ("z", "yhi", "ymid", "ylo", "core")
+BRICK = ("zhi", "zlo", "yhi", "ymid", "ylo", "core")
 NEAR = ("ymid", "ylo", "core")
-FIRST = ("ylo", "core", "x")
-SECOND = ("yhi", "ymid", "z")
-SHARES, ROWS = 16, 56
+FIRST = ("x", "ylo", "zlo", "core")
+SECOND = ("yhi", "ymid", "zhi")
+SHARES, ROWS = 32, 32
 HALF = GROUP_SIZE // 2
 PAIRS = [
     pair
@@ -498,7 +500,7 @@
 
 
 def solution(mesh):
-    fine = Mesh(mesh.devices.reshape(8, 2, 2, 2, 2, 4), BRICK + ("x",))
+    fine = Mesh(mesh.devices.reshape(4, 2, 2, 2, 2, 2, 4), BRICK + ("x",))
     return jax.shard_map(
         shards,
         mesh=fine,

time: 79.5 us -> 77.6 us (0.976)
  blocking collectives: 69.1 us -> 67.4 us
    all_to_all x2, blocking collectives: 44.4 us -> 35.6 us  [spread_out(): return lax.all_to_all(copies, axes, 0, 0, tiled=True)]
    all_to_all x1, blocking collectives: 10.4 us -> 17.4 us  [shards(): lax.all_to_all(parts.reshape(SHARES, ROWS, 128), FIRST, 0, 0, tiled=True)]
where the time goes in v7:
time: 77.6 us; the launch traced here: 77.2 us
  blocking collectives  67.4 us (87%)
  Pallas kernels  5.24 us (7%)
  local copies, waits for them, and re-layouts  2.31 us (3%)
  between operations  1.4 us (2%)
  starting transfers between devices  0.78 us (1%)
    all_to_all x2, blocking collectives, spread_out(): return lax.all_to_all(copies, axes, 0, 0, tiled=True)  35.6 us
    all_to_all x1, blocking collectives, shards(): lax.all_to_all(parts.reshape(SHARES, ROWS, 128), FIRST, 0, 0, tiled=True)  17.4 us
    all_to_all x1, blocking collectives, shards(): near = lax.all_to_all(mine, NEAR, 0, 0, tiled=True)  14.3 us
    pallas_call x1, Pallas kernels, all_brick_work(): pl.pallas_call(brick_kernel, out_shape=(jax.ShapeDtypeStruct((OUT_CH, 512...  3.23 us
    unnamed x18, local copies, waits for them, and re-layouts  2.25 us
  transfers between devices with their start and end apart: 1, of which 0 were waited for; matrix products, arithmetic and copies ran while one was open for 0% of the time, Pallas kernels for 1%

profile of v7, /device:TPU:1, one launch (start us, length us, event | category | flops | bytes accessed | tf_op | source)
XLA Modules:
  0.0 77.2 jit_solution(15562053077513265978)
XLA Ops:
  1.3 0.0 copy-start
  1.3 0.0 copy-start.1
  1.3 0.7 copy-done
  2.0 0.0 copy-done.1
  2.0 0.2 pack.1
  2.1 0.0 copy-start.4
  2.1 0.0 copy-start.6
  2.1 0.0 copy-start.7
  2.1 0.0 copy-start.8
  2.1 14.3 %all_to_all.20.near_ref = bf16[8,5,128]{2,1,0:T(8,128)(2,1)S(1)} all-to-all(bf16[8,5,128]{2,1,0:T(8,128)(2,1)S(1)} %pack.1), channel_id=1, replica_groups=mesh['zhi'=4,'zlo'=2,'yhi'=2,'ymid'=2,'ylo'=2,'core'=2,'x'=4] {'ymid','y..., dimensions={0} | all-to-all | bytes 20480 | tf_op jit(solution)/shard_map/all_to_all | solution.py:481
  16.4 0.0 copy-start.3
  16.4 0.8 %collective-permute-start = (bf16[8,5,128]{2,1,0:T(8,128)(2,1)S(1)}, bf16[8,5,128]{2,1,0:T(8,128)(2,1)S(1)}, u32[]{:S(2)}, u32[]{:S(2)}) collective-permute-start(bf16[8,5,128]{2,1,0:T(8,128)(2,1)S(1)} %all_to_all.20.near_ref), channel_id=1, source_target_pairs={{16,32},{32,16},{20,36},{36,20},{24,40},{40,24},{28,44},{44,28},{4... | collective-permute-start | bytes 30728 | tf_op jit(solution)/shard_map/ppermute | solution.py:482
  17.2 0.0 copy-start.5
  17.2 0.0 copy-done.4
  17.3 0.0 copy-done.6
  17.3 0.0 copy-done.7
  17.3 0.0 copy-done.8
  17.3 0.0 copy-done.3
  17.3 0.6 copy-done.5
  17.9 0.0 copy-start.2
  17.9 0.9 %copy-done.2 = bf16[64,1728]{1,0:T(8,128)(2,1)S(1)} copy-done((bf16[64,1728]{1,0:T(8,128)(2,1)S(1)}, bf16[64,1728]{1,0:T(8,128)(2,1)}, u32[]{:S(2)}) %copy-start.2) | copy-done | bytes 221208
  18.9 1.0 %prep.1 = (bf16[384,128]{1,0:T(8,128)(2,1)S(1)}, bf16[384,128]{1,0:T(8,128)(2,1)S(1)}, bf16[128,512]{1,0:T(8,128)(2,1)S(1)}, bf16[64,32]{1,0:T(8,128)(2,1)S(1)},...) custom-call(s32[1,1]{1,0:T(1,128)S(6)} %copy.17.tissue_ref, ...), custom_call_target="tpu_custom_call" | custom-call | flops 4000000000 | bytes 4000000 | tf_op jit(solution)/shard_map/prep/pallas_call | solution.py:382
  19.9 0.0 collective-permute-done.far_ref
  19.9 3.2 %brick.1 = (bf16[4,512]{1,0:T(4,128)(2,1)}, bf16[16,64,128]{2,1,0:T(8,128)(2,1)S(1)}) custom-call(s32[1]{0:T(128)} %bitcast.place_ref, bf16[8,5,128]{2,1,0:T(8,128)(2,1)S(1)} %all_to_all.20.near_ref, bf16[8,5,128]{2,1,0:T(8,128)(2,1)S(1)} %collective-permute-done.far_ref, bf16[384,128]{1,0:T(8,128)(2,1)S(1)} %get-tuple-element.28.even_ref, ...), custom_call_target="tpu_custom_call" | custom-call | tf_op jit(solution)/shard_map/brick/pallas_call | solution.py:406
  23.1 17.4 %all_to_all.21 = bf16[32,32,128]{2,1,0:T(8,128)(2,1)S(1)} all-to-all(bf16[32,32,128]{2,1,0:T(8,128)(2,1)S(1)} %bitcast.16), channel_id=1, replica_groups=mesh['zhi'=4,'zlo'=2,'yhi'=2,'ymid'=2,'ylo'=2,'core'=2,'x'=4] {'x','ylo'..., dimensions={0} | all-to-all | bytes 524288 | tf_op jit(solution)/shard_map/all_to_all | solution.py:485
  40.5 0.1 reduce_sum.24
  40.6 22.5 %all_to_all.22 = bf16[16,32,128]{2,1,0:T(8,128)(2,1)S(1)} all-to-all(bf16[16,32,128]{2,1,0:T(8,128)(2,1)S(1)} %broadcast_in_dim.28), channel_id=1, replica_groups=mesh['zhi'=4,'zlo'=2,'yhi'=2,'ymid'=2,'ylo'=2,'core'=2,'x'=4] {'yhi','ym..., dimensions={0} | all-to-all | bytes 262144 | tf_op jit(solution)/shard_map/all_to_all | solution.py:460
  63.2 13.1 %all_to_all.23 = bf16[32,32,128]{2,1,0:T(8,128)(2,1)S(1)} all-to-all(bf16[32,32,128]{2,1,0:T(8,128)(2,1)S(1)} %broadcast_in_dim.29), channel_id=1, replica_groups=mesh['zhi'=4,'zlo'=2,'yhi'=2,'ymid'=2,'ylo'=2,'core'=2,'x'=4] {'x','ylo'..., dimensions={0} | all-to-all | bytes 524288 | tf_op jit(solution)/shard_map/all_to_all | solution.py:460
  76.3 0.9 %unpack.1 = (f32[27,64]{1,0:T(8,128)}, f32[1,64]{1,0:T(1,128)}, f32[64,1728]{1,0:T(8,128)}, f32[1,64]{1,0:T(1,128)}, f32[4,64]{1,0:T(4,128)}, /*index=5*/f32[1,4]{1,0:T(1,128)}) custom-call(bf16[16,64,128]{2,1,0:T(8,128)(2,1)S(1)} %bitcast.15), custom_call_target="tpu_custom_call" | custom-call | tf_op jit(solution)/shard_map/unpack/pallas_call | solution.py:430
  (3 shorter events, 0.1 us)
Async XLA Ops:
  1.3 0.7 copy-start
  1.3 0.7 copy-start.1
  2.1 15.1 %copy-start.4 = (bf16[1,1,4,512]{3,2,1,0:T(4,128)(2,1)S(1)}, bf16[1,1,4,512]{3,2,1,0:T(4,128)(2,1)}, u32[]{:S(2)}) copy-start(bf16[1,1,4,512]{3,2,1,0:T(4,128)(2,1)} %param.19) | copy-start | bytes 12292
  2.1 15.1 %copy-start.6 = (f32[64]{0:T(128)S(1)}, f32[64]{0:T(128)}, u32[]{:S(2)}) copy-start(f32[64]{0:T(128)} %param.14) | copy-start | bytes 772
  2.1 15.1 %copy-start.7 = (f32[64]{0:T(128)S(1)}, f32[64]{0:T(128)}, u32[]{:S(2)}) copy-start(f32[64]{0:T(128)} %param.16) | copy-start | bytes 772
  2.1 15.1 %copy-start.8 = (f32[4]{0:T(128)S(1)}, f32[4]{0:T(128)}, u32[]{:S(2)}) copy-start(f32[4]{0:T(128)} %param.18) | copy-start | bytes 52
  16.4 0.8 %copy-start.3 = (bf16[64,27]{0,1:T(8,128)(2,1)S(1)}, bf16[64,27]{0,1:T(8,128)(2,1)}, u32[]{:S(2)}) copy-start(bf16[64,27]{0,1:T(8,128)(2,1)} %param.13) | copy-start | bytes 10372
  16.4 3.4 %collective-permute-start = (bf16[8,5,128]{2,1,0:T(8,128)(2,1)S(1)}, bf16[8,5,128]{2,1,0:T(8,128)(2,1)S(1)}, u32[]{:S(2)}, u32[]{:S(2)}) collective-permute-start(bf16[8,5,128]{2,1,0:T(8,128)(2,1)S(1)} %all_to_all.20.near_ref), channel_id=1, source_target_pairs={{16,32},{32,16},{20,36},{36,20},{24,40},{40,24},{28,44},{44,28},{4... | collective-permute-start | bytes 30728 | tf_op jit(solution)/shard_map/ppermute | solution.py:482
  17.2 0.7 copy-start.5
  17.9 0.9 %copy-start.2 = (bf16[64,1728]{1,0:T(8,128)(2,1)S(1)}, bf16[64,1728]{1,0:T(8,128)(2,1)}, u32[]{:S(2)}) copy-start(bf16[64,1728]{1,0:T(8,128)(2,1)} %w2_ref.1) | copy-start | bytes 663556

commit v8 on v7

--- a/solution.py
+++ b/solution.py
@@ -13,6 +13,7 @@
 ACROSS = 1728
 BLOCKS = 16
 GROUP_SIZE = 8
+HALF = GROUP_SIZE // 2
 ROOT = 0.7978845608028654
 CUBIC = 0.044715
 
@@ -119,6 +120,7 @@
     dp_out,
     dh2_out,
     gbh_out,
+    own_out,
 ):
     bf16 = jnp.bfloat16
     f32 = jnp.float32
@@ -149,7 +151,9 @@
             column = 64 * (2 - tap // 9)
             wb_out[row : row + 64, column : column + 64] = wide[64 * half : 64 * half + 64].astype(bf16)
     own = even[128:192]
-    scale = jnp.where(tissue_ref[...] > 0, 1.0 / 512.0, 0.0)
+    tissue = jnp.where(tissue_ref[...] > 0, 1.0, 0.0)
+    own_out[...] = jnp.broadcast_to(tissue, (1, 128))
+    scale = tissue / 512.0
     cot = (cot_ref[...].astype(f32) * scale).astype(bf16)
     for x in range(8):
         dp = dot(cot[:, 64 * x : 64 * x + 64], own).astype(bf16)
@@ -162,7 +166,6 @@
 def brick_kernel(
     place_ref,
     near_ref,
-    far_ref,
     even_ref,
     odd_ref,
     spread_ref,
@@ -192,8 +195,10 @@
     tiles = {}
     for w in range(-3, 4):
         at = lax.rem(position + w + GROUP_SIZE, GROUP_SIZE)
+        partner = lax.rem(at + HALF, GROUP_SIZE)
         inside = at == position + w
-        tiles[w] = jnp.where(inside, near_ref[at].astype(f32), far_ref[at].astype(f32))
+        own_tile, partner_tile = near_ref[at].astype(f32), near_ref[partner].astype(f32)
+        tiles[w] = jnp.where(inside, own_tile[0:8], partner_tile[8:16])
     rows_ref[...] = jnp.zeros_like(rows_ref)
     for rc in (-1, 0, 1):
         lanes = slice(128 * (rc + 1), 128 * (rc + 2))
@@ -313,23 +318,31 @@
     part_ref[13] = jnp.concatenate([last[8], small], axis=1).astype(bf16)
 
 
-def pack_kernel(list_ref, tissue_ref, cells_ref, out_ref):
+def pack_kernel(list_ref, cells_ref, out_ref):
     f32 = jnp.float32
     lane = lax.broadcasted_iota(jnp.int32, (1, 128), 1)
     listed = jnp.concatenate([list_ref[...], jnp.zeros((1, 102), jnp.int32)], axis=1)
     present = jnp.where(listed >= 0, 1.0, 0.0)
     flags = jnp.where(lane < 3, turn(present, 3), 0.0)
     flags = jnp.where(lane == 3, turn(present, 9), flags)
-    own = jnp.where(tissue_ref[...] > 0, 1.0, 0.0)
-    flags = jnp.where(lane == 4, own, flags)
+    flags = jnp.where(lane == 4, 1.0, flags)
     flags = jnp.where(lane == 5, turn(present, 8), flags)
     flags = jnp.where((lane > 5) & (lane < 9), turn(present, 14), flags)
     flags = flags + turn(flags, -16) + turn(flags, -32)
     cells = cells_ref[...].astype(f32)
     rows = [cells[:, 128 * row : 128 * row + 128] for row in range(4)]
-    tile = jnp.concatenate(rows + [flags], axis=0).astype(jnp.bfloat16)
+    out_ref[...] = jnp.concatenate(rows + [flags], axis=0).astype(jnp.bfloat16)
+
+
+def pair_kernel(place_ref, own_ref, mine_ref, far_ref, out_ref):
+    f32 = jnp.float32
+    place = wide_iota((5, 128), 0) * 128 + wide_iota((5, 128), 1)
+    mine = jnp.where(place == 4 * 128 + 4, own_ref[...], mine_ref[...].astype(f32))
+    blank = jnp.zeros((3, 128), f32)
+    both = jnp.concatenate([mine, blank, far_ref[...].astype(f32), blank], axis=0)
+    both = both.astype(jnp.bfloat16)
     for copy in range(GROUP_SIZE):
-        out_ref[copy] = tile
+        out_ref[copy] = both
 
 
 def unpack_kernel(all_ref, w1_ref, b1_ref, w2_ref, b2_ref, hw_ref, hb_ref):
@@ -378,6 +391,7 @@
         ((OUT_CH, 1024), bf16),
         ((8, C, 128), f32),
         ((8, C), f32),
+        ((1, 128), f32),
     ]
     return pl.pallas_call(
         prep_kernel,
@@ -401,7 +415,7 @@
     )
 
 
-def all_brick_work(near, far, position, ready):
+def all_brick_work(near, position, ready):
     bf16, f32 = jnp.bfloat16, jnp.float32
     return pl.pallas_call(
         brick_kernel,
@@ -409,7 +423,7 @@
             jax.ShapeDtypeStruct((OUT_CH, 512), bf16),
             jax.ShapeDtypeStruct((BLOCKS, C, 128), bf16),
         ),
-        in_specs=[SMEM] + [VMEM] * (2 + len(ready)),
+        in_specs=[SMEM] + [VMEM] * (1 + len(ready)),
         out_specs=(VMEM, VMEM),
         scratch_shapes=[
             pltpu.VMEM((8, 384), f32),
@@ -422,7 +436,7 @@
         ],
         compiler_params=pltpu.CompilerParams(vmem_limit_bytes=BIG),
         name="brick",
-    )(position, near, far, *ready)
+    )(position, near, *ready)
 
 
 def unpack(gathered):
@@ -444,15 +458,26 @@
     )(gathered)
 
 
-def pack(neighbours, tissue, micrograph):
+def pack(neighbours, micrograph):
     return pl.pallas_call(
         pack_kernel,
-        out_shape=jax.ShapeDtypeStruct((GROUP_SIZE, 5, 128), jnp.bfloat16),
-        in_specs=[VMEM] * 3,
+        out_shape=jax.ShapeDtypeStruct((5, 128), jnp.bfloat16),
+        in_specs=[VMEM] * 2,
         out_specs=VMEM,
         compiler_params=pltpu.CompilerParams(vmem_limit_bytes=SMALL),
         name="pack",
-    )(neighbours, tissue, micrograph)
+    )(neighbours, micrograph)
+
+
+def pair(position, own, mine, far):
+    return pl.pallas_call(
+        pair_kernel,
+        out_shape=jax.ShapeDtypeStruct((GROUP_SIZE, 16, 128), jnp.bfloat16),
+        in_specs=[SMEM] + [VMEM] * 3,
+        out_specs=VMEM,
+        compiler_params=pltpu.CompilerParams(vmem_limit_bytes=SMALL),
+        name="pair",
+    )(position, own, mine, far)
 
 
 def spread_out(block, axes, number):
@@ -465,23 +490,24 @@
 FIRST = ("x", "ylo", "zlo", "core")
 SECOND = ("yhi", "ymid", "zhi")
 SHARES, ROWS = 32, 32
-HALF = GROUP_SIZE // 2
 PAIRS = [
-    pair
+    link
     for lower in range(HALF, 128 - HALF)
     if lower % GROUP_SIZE >= HALF
-    for pair in ((lower, lower + HALF), (lower + HALF, lower))
+    for link in ((lower, lower + HALF), (lower + HALF, lower))
 ]
 
 
 def shards(micrograph, tissue, neighbours, w1, b1, w2, b2, hw, hb, cot):
     bf16, f32 = jnp.bfloat16, jnp.float32
     position = lax.axis_index(NEAR).astype(jnp.int32).reshape(1)
-    mine = pack(neighbours[0], tissue, micrograph[0])
-    near = lax.all_to_all(mine, NEAR, 0, 0, tiled=True)
-    far = lax.ppermute(near, BRICK, PAIRS)
+    mine = pack(neighbours[0], micrograph[0])
+    far = lax.ppermute(mine, BRICK, PAIRS)
     ready = prepare(tissue, cot[0, 0], w1.T, b1[None], w2, b2[None], hw, hb[None])
-    prediction, parts = all_brick_work(near, far, position, ready)
+    *ready, own = ready
+    both = pair(position, own, mine, far)
+    near = lax.all_to_all(both, NEAR, 0, 0, tiled=True)
+    prediction, parts = all_brick_work(near, position, ready)
     mixed = lax.all_to_all(parts.reshape(SHARES, ROWS, 128), FIRST, 0, 0, tiled=True)
     share = jnp.sum(mixed.astype(f32), axis=0).astype(bf16)
     shares = spread_out(share, SECOND, 512 // SHARES)

time: 77.6 us -> 77.1 us (level)
    all_to_all x1, blocking collectives: 17.4 us -> 15.2 us  [shards(): lax.all_to_all(parts.reshape(SHARES, ROWS, 128), FIRST, 0, 0, tiled=True)]
    all_to_all x1, blocking collectives: 14.3 us -> 15.3 us  [shards(): near = lax.all_to_all(both, NEAR, 0, 0, tiled=True)]
    all_to_all x2, blocking collectives: 35.6 us -> 36.5 us  [spread_out(): return lax.all_to_all(copies, axes, 0, 0, tiled=True)]
where the time goes in v8:
time: 77.1 us; the launch traced here: 76.7 us
  blocking collectives  67 us (87%)
  Pallas kernels  5.25 us (7%)
  local copies, waits for them, and re-layouts  2.35 us (3%)
  between operations  1.39 us (2%)
    all_to_all x2, blocking collectives, spread_out(): return lax.all_to_all(copies, axes, 0, 0, tiled=True)  36.5 us
    all_to_all x1, blocking collectives, shards(): near = lax.all_to_all(both, NEAR, 0, 0, tiled=True)  15.3 us
    all_to_all x1, blocking collectives, shards(): lax.all_to_all(parts.reshape(SHARES, ROWS, 128), FIRST, 0, 0, tiled=True)  15.2 us
    pallas_call x1, Pallas kernels, all_brick_work(): pl.pallas_call(brick_kernel, out_shape=(jax.ShapeDtypeStruct((OUT_CH, 512...  3.23 us
    unnamed x18, local copies, waits for them, and re-layouts  2.29 us
  transfers between devices with their start and end apart: 1, of which 0 were waited for; matrix products, arithmetic and copies ran while one was open for 0% of the time, Pallas kernels for 1%

profile of v8, /device:TPU:1, one launch (start us, length us, event | category | flops | bytes accessed | tf_op | source)
XLA Modules:
  0.0 76.7 jit_solution(14381701306138889980)
XLA Ops:
  0.6 0.0 copy-start
  0.6 0.0 copy-start.1
  0.7 0.7 copy-done
  1.3 0.0 copy-done.1
  1.3 0.0 copy-start.3
  1.3 0.1 pack.1.mine_ref
  1.5 0.7 collective-permute-start
  2.8 0.0 copy-start.4
  2.8 0.0 copy-start.7
  2.8 0.0 copy-start.8
  2.8 0.0 copy-start.5
  2.8 0.0 copy-start.6
  2.8 0.0 copy-done.3
  2.8 0.6 copy-done.4
  3.5 0.0 copy-done.7
  3.5 0.0 copy-done.8
  3.5 0.0 copy-done.5
  3.5 0.0 copy-done.6
  3.5 0.0 copy-start.2
  3.5 0.9 %copy-done.2 = bf16[64,1728]{1,0:T(8,128)(2,1)S(1)} copy-done((bf16[64,1728]{1,0:T(8,128)(2,1)S(1)}, bf16[64,1728]{1,0:T(8,128)(2,1)}, u32[]{:S(2)}) %copy-start.2) | copy-done | bytes 221208
  4.4 1.0 %prep.1 = (bf16[384,128]{1,0:T(8,128)(2,1)S(1)}, bf16[384,128]{1,0:T(8,128)(2,1)S(1)}, bf16[128,512]{1,0:T(8,128)(2,1)S(1)}, bf16[64,32]{1,0:T(8,128)(2,1)S(1)},...) custom-call(s32[1,1]{1,0:T(1,128)S(6)} %copy.17.tissue_ref, ...), custom_call_target="tpu_custom_call" | custom-call | flops 4000000000 | bytes 4000000 | tf_op jit(solution)/shard_map/prep/pallas_call | solution.py:396
  5.4 0.0 collective-permute-done.far_ref
  5.5 15.3 %all_to_all.20.near_ref = bf16[8,16,128]{2,1,0:T(8,128)(2,1)S(1)} all-to-all(bf16[8,16,128]{2,1,0:T(8,128)(2,1)S(1)} %pair.1), channel_id=1, replica_groups=mesh['zhi'=4,'zlo'=2,'yhi'=2,'ymid'=2,'ylo'=2,'core'=2,'x'=4] {'ymid','y..., dimensions={0} | all-to-all | bytes 65536 | tf_op jit(solution)/shard_map/all_to_all | solution.py:509
  20.8 3.2 %brick.1 = (bf16[4,512]{1,0:T(4,128)(2,1)}, bf16[16,64,128]{2,1,0:T(8,128)(2,1)S(1)}) custom-call(s32[1]{0:T(128)} %bitcast.place_ref, bf16[8,16,128]{2,1,0:T(8,128)(2,1)S(1)} %all_to_all.20.near_ref, bf16[384,128]{1,0:T(8,128)(2,1)S(1)} %get-tuple-element.30.even_ref, bf16[384,128]{1,0:T(8,128)(2,1)S(1)} %get-tuple-element.31.odd_ref, ...), custom_call_target="tpu_custom_call" | custom-call | tf_op jit(solution)/shard_map/brick/pallas_call | solution.py:420
  24.0 15.2 %all_to_all.21 = bf16[32,32,128]{2,1,0:T(8,128)(2,1)S(1)} all-to-all(bf16[32,32,128]{2,1,0:T(8,128)(2,1)S(1)} %bitcast.16), channel_id=1, replica_groups=mesh['zhi'=4,'zlo'=2,'yhi'=2,'ymid'=2,'ylo'=2,'core'=2,'x'=4] {'x','ylo'..., dimensions={0} | all-to-all | bytes 524288 | tf_op jit(solution)/shard_map/all_to_all | solution.py:511
  39.2 0.1 reduce_sum.24
  39.3 23.3 %all_to_all.22 = bf16[16,32,128]{2,1,0:T(8,128)(2,1)S(1)} all-to-all(bf16[16,32,128]{2,1,0:T(8,128)(2,1)S(1)} %broadcast_in_dim.28), channel_id=1, replica_groups=mesh['zhi'=4,'zlo'=2,'yhi'=2,'ymid'=2,'ylo'=2,'core'=2,'x'=4] {'yhi','ym..., dimensions={0} | all-to-all | bytes 262144 | tf_op jit(solution)/shard_map/all_to_all | solution.py:485
  62.7 13.1 %all_to_all.23 = bf16[32,32,128]{2,1,0:T(8,128)(2,1)S(1)} all-to-all(bf16[32,32,128]{2,1,0:T(8,128)(2,1)S(1)} %broadcast_in_dim.29), channel_id=1, replica_groups=mesh['zhi'=4,'zlo'=2,'yhi'=2,'ymid'=2,'ylo'=2,'core'=2,'x'=4] {'x','ylo'..., dimensions={0} | all-to-all | bytes 524288 | tf_op jit(solution)/shard_map/all_to_all | solution.py:485
  75.9 0.9 %unpack.1 = (f32[27,64]{1,0:T(8,128)}, f32[1,64]{1,0:T(1,128)}, f32[64,1728]{1,0:T(8,128)}, f32[1,64]{1,0:T(1,128)}, f32[4,64]{1,0:T(4,128)}, /*index=5*/f32[1,4]{1,0:T(1,128)}) custom-call(bf16[16,64,128]{2,1,0:T(8,128)(2,1)S(1)} %bitcast.15), custom_call_target="tpu_custom_call" | custom-call | tf_op jit(solution)/shard_map/unpack/pallas_call | solution.py:444
  (4 shorter events, 0.1 us)
Async XLA Ops:
  0.6 0.7 copy-start
  0.6 0.7 copy-start.1
  1.3 1.5 %copy-start.3 = (bf16[64,27]{0,1:T(8,128)(2,1)S(1)}, bf16[64,27]{0,1:T(8,128)(2,1)}, u32[]{:S(2)}) copy-start(bf16[64,27]{0,1:T(8,128)(2,1)} %param.13) | copy-start | bytes 10372
  1.5 4.0 %collective-permute-start = (bf16[5,128]{1,0:T(8,128)(2,1)S(1)}, bf16[5,128]{1,0:T(8,128)(2,1)S(1)}, u32[]{:S(2)}, u32[]{:S(2)}) collective-permute-start(bf16[5,128]{1,0:T(8,128)(2,1)S(1)} %pack.1.mine_ref), channel_id=1, source_target_pairs={{16,32},{32,16},{20,36},{36,20},{24,40},{40,24},{28,44},{44,28},{4... | collective-permute-start | bytes 3848 | tf_op jit(solution)/shard_map/ppermute | solution.py:505
  2.8 0.7 copy-start.4
  2.8 0.7 copy-start.7
  2.8 0.7 copy-start.8
  2.8 0.7 copy-start.5
  2.8 0.7 copy-start.6
  3.5 0.9 %copy-start.2 = (bf16[64,1728]{1,0:T(8,128)(2,1)S(1)}, bf16[64,1728]{1,0:T(8,128)(2,1)}, u32[]{:S(2)}) copy-start(bf16[64,1728]{1,0:T(8,128)(2,1)} %w2_ref.1) | copy-start | bytes 663556

commit v9 on v8

--- a/solution.py
+++ b/solution.py
@@ -487,8 +487,8 @@
 
 BRICK = ("zhi", "zlo", "yhi", "ymid", "ylo", "core")
 NEAR = ("ymid", "ylo", "core")
-FIRST = ("x", "ylo", "zlo", "core")
-SECOND = ("yhi", "ymid", "zhi")
+FIRST = ("x", "core", "ylo", "zlo")
+SECOND = ("zhi", "yhi", "ymid")
 SHARES, ROWS = 32, 32
 PAIRS = [
     link

time: 77.1 us -> 76.6 us (level)
  no operation moved by 1% of the time
where the time goes in v9:
time: 76.6 us; the launch traced here: 76.2 us
  blocking collectives  66.5 us (87%)
  Pallas kernels  5.25 us (7%)
  local copies, waits for them, and re-layouts  2.35 us (3%)
  between operations  1.39 us (2%)
    all_to_all x2, blocking collectives, spread_out(): return lax.all_to_all(copies, axes, 0, 0, tiled=True)  36.6 us
    all_to_all x1, blocking collectives, shards(): near = lax.all_to_all(both, NEAR, 0, 0, tiled=True)  15.3 us
    all_to_all x1, blocking collectives, shards(): lax.all_to_all(parts.reshape(SHARES, ROWS, 128), FIRST, 0, 0, tiled=True)  14.7 us
    pallas_call x1, Pallas kernels, all_brick_work(): pl.pallas_call(brick_kernel, out_shape=(jax.ShapeDtypeStruct((OUT_CH, 512...  3.23 us
    unnamed x18, local copies, waits for them, and re-layouts  2.29 us
  transfers between devices with their start and end apart: 1, of which 0 were waited for; matrix products, arithmetic and copies ran while one was open for 0% of the time, Pallas kernels for 1%

profile of v9, /device:TPU:1, one launch (start us, length us, event | category | flops | bytes accessed | tf_op | source)
XLA Modules:
  0.0 76.2 jit_solution(14343809804194518333)
XLA Ops:
  0.6 0.0 copy-start
  0.6 0.0 copy-start.1
  0.7 0.7 copy-done
  1.3 0.0 copy-done.1
  1.3 0.0 copy-start.3
  1.3 0.1 pack.1.mine_ref
  1.5 0.7 collective-permute-start
  2.8 0.0 copy-start.4
  2.8 0.0 copy-start.7
  2.8 0.0 copy-start.8
  2.8 0.0 copy-start.5
  2.8 0.0 copy-start.6
  2.8 0.0 copy-done.3
  2.8 0.6 copy-done.4
  3.5 0.0 copy-done.7
  3.5 0.0 copy-done.8
  3.5 0.0 copy-done.5
  3.5 0.0 copy-done.6
  3.5 0.0 copy-start.2
  3.5 0.9 %copy-done.2 = bf16[64,1728]{1,0:T(8,128)(2,1)S(1)} copy-done((bf16[64,1728]{1,0:T(8,128)(2,1)S(1)}, bf16[64,1728]{1,0:T(8,128)(2,1)}, u32[]{:S(2)}) %copy-start.2) | copy-done | bytes 221208
  4.4 1.0 %prep.1 = (bf16[384,128]{1,0:T(8,128)(2,1)S(1)}, bf16[384,128]{1,0:T(8,128)(2,1)S(1)}, bf16[128,512]{1,0:T(8,128)(2,1)S(1)}, bf16[64,32]{1,0:T(8,128)(2,1)S(1)},...) custom-call(s32[1,1]{1,0:T(1,128)S(6)} %copy.17.tissue_ref, ...), custom_call_target="tpu_custom_call" | custom-call | flops 4000000000 | bytes 4000000 | tf_op jit(solution)/shard_map/prep/pallas_call | solution.py:396
  5.4 0.0 collective-permute-done.far_ref
  5.5 15.3 %all_to_all.20.near_ref = bf16[8,16,128]{2,1,0:T(8,128)(2,1)S(1)} all-to-all(bf16[8,16,128]{2,1,0:T(8,128)(2,1)S(1)} %pair.1), channel_id=1, replica_groups=mesh['zhi'=4,'zlo'=2,'yhi'=2,'ymid'=2,'ylo'=2,'core'=2,'x'=4] {'ymid','y..., dimensions={0} | all-to-all | bytes 65536 | tf_op jit(solution)/shard_map/all_to_all | solution.py:509
  20.8 3.2 %brick.1 = (bf16[4,512]{1,0:T(4,128)(2,1)}, bf16[16,64,128]{2,1,0:T(8,128)(2,1)S(1)}) custom-call(s32[1]{0:T(128)} %bitcast.place_ref, bf16[8,16,128]{2,1,0:T(8,128)(2,1)S(1)} %all_to_all.20.near_ref, bf16[384,128]{1,0:T(8,128)(2,1)S(1)} %get-tuple-element.30.even_ref, bf16[384,128]{1,0:T(8,128)(2,1)S(1)} %get-tuple-element.31.odd_ref, ...), custom_call_target="tpu_custom_call" | custom-call | tf_op jit(solution)/shard_map/brick/pallas_call | solution.py:420
  24.0 14.7 %all_to_all.21 = bf16[32,32,128]{2,1,0:T(8,128)(2,1)S(1)} all-to-all(bf16[32,32,128]{2,1,0:T(8,128)(2,1)S(1)} %bitcast.16), channel_id=1, replica_groups=mesh['zhi'=4,'zlo'=2,'yhi'=2,'ymid'=2,'ylo'=2,'core'=2,'x'=4] {'x','core..., dimensions={0} | all-to-all | bytes 524288 | tf_op jit(solution)/shard_map/all_to_all | solution.py:511
  38.6 0.1 reduce_sum.24
  38.7 23.4 %all_to_all.22 = bf16[16,32,128]{2,1,0:T(8,128)(2,1)S(1)} all-to-all(bf16[16,32,128]{2,1,0:T(8,128)(2,1)S(1)} %broadcast_in_dim.28), channel_id=1, replica_groups=mesh['zhi'=4,'zlo'=2,'yhi'=2,'ymid'=2,'ylo'=2,'core'=2,'x'=4] {'zhi','yh..., dimensions={0} | all-to-all | bytes 262144 | tf_op jit(solution)/shard_map/all_to_all | solution.py:485
  62.2 13.2 %all_to_all.23 = bf16[32,32,128]{2,1,0:T(8,128)(2,1)S(1)} all-to-all(bf16[32,32,128]{2,1,0:T(8,128)(2,1)S(1)} %broadcast_in_dim.29), channel_id=1, replica_groups=mesh['zhi'=4,'zlo'=2,'yhi'=2,'ymid'=2,'ylo'=2,'core'=2,'x'=4] {'x','core..., dimensions={0} | all-to-all | bytes 524288 | tf_op jit(solution)/shard_map/all_to_all | solution.py:485
  75.4 0.9 %unpack.1 = (f32[27,64]{1,0:T(8,128)}, f32[1,64]{1,0:T(1,128)}, f32[64,1728]{1,0:T(8,128)}, f32[1,64]{1,0:T(1,128)}, f32[4,64]{1,0:T(4,128)}, /*index=5*/f32[1,4]{1,0:T(1,128)}) custom-call(bf16[16,64,128]{2,1,0:T(8,128)(2,1)S(1)} %bitcast.15), custom_call_target="tpu_custom_call" | custom-call | tf_op jit(solution)/shard_map/unpack/pallas_call | solution.py:444
  (4 shorter events, 0.1 us)
Async XLA Ops:
  0.6 0.7 copy-start
  0.6 0.7 copy-start.1
  1.3 1.5 %copy-start.3 = (bf16[64,27]{0,1:T(8,128)(2,1)S(1)}, bf16[64,27]{0,1:T(8,128)(2,1)}, u32[]{:S(2)}) copy-start(bf16[64,27]{0,1:T(8,128)(2,1)} %param.13) | copy-start | bytes 10372
  1.5 4.0 %collective-permute-start = (bf16[5,128]{1,0:T(8,128)(2,1)S(1)}, bf16[5,128]{1,0:T(8,128)(2,1)S(1)}, u32[]{:S(2)}, u32[]{:S(2)}) collective-permute-start(bf16[5,128]{1,0:T(8,128)(2,1)S(1)} %pack.1.mine_ref), channel_id=1, source_target_pairs={{16,32},{32,16},{20,36},{36,20},{24,40},{40,24},{28,44},{44,28},{4... | collective-permute-start | bytes 3848 | tf_op jit(solution)/shard_map/ppermute | solution.py:505
  2.8 0.7 copy-start.4
  2.8 0.7 copy-start.7
  2.8 0.7 copy-start.8
  2.8 0.7 copy-start.5
  2.8 0.7 copy-start.6
  3.5 0.9 %copy-start.2 = (bf16[64,1728]{1,0:T(8,128)(2,1)S(1)}, bf16[64,1728]{1,0:T(8,128)(2,1)}, u32[]{:S(2)}) copy-start(bf16[64,1728]{1,0:T(8,128)(2,1)} %w2_ref.1) | copy-start | bytes 663556
